TPU v7x, 32 devices: a whole 2x2x4 slice. The times are simulated.
32 devices in a mesh: rep: 2 (over y), shard: 16 (over z, x, core).
Axes of the slice: x: 2, y: 2, z: 4, core: 2. Of those that a mesh axis runs over, the one named last changes fastest.
Arguments:
- tokens: bfloat16 [12, 2048, 768], P('rep', 'shard'), may hold values from -4 to 4
- query_proj: bfloat16 [768, 768], P('shard')
- key_proj: bfloat16 [768, 768], P('shard')
- value_proj: bfloat16 [768, 768], P('shard')
- pooled_query: bfloat16 [768, 768], P('shard')
- output_proj: bfloat16 [768, 768], P('shard'), may hold values from -1.75 to 1.75
- conv_taps: bfloat16 [5, 2, 768], P(None, None, 'shard'), may hold values from -1.125 to 1.125
- output_bias: bfloat16 [768], P('shard'), may hold values from -2 to 2
- first_gain: bfloat16 [768], P('shard'), may hold values from 0.099609375 to 1.8984375
- first_shift: bfloat16 [768], P('shard'), may hold values from -2 to 2
- inner_proj: bfloat16 [768, 3072], P('shard'), may hold values from -0.21875 to 0.21875
- inner_bias: bfloat16 [3072], P('shard'), may hold values from -3 to 3
- outer_proj: bfloat16 [3072, 768], P('shard'), may hold values from -0.109375 to 0.109375
- outer_bias: bfloat16 [768], P('shard'), may hold values from -2 to 2
- second_gain: bfloat16 [768], P('shard'), may hold values from 0.099609375 to 1.8984375
- second_shift: bfloat16 [768], P('shard'), may hold values from -2 to 2
- block_ids: int32 [12, 2048], P('rep'), may hold values from 0 to 15, never falling along the last dimension, each value on 1 to 256 neighbouring positions
- cotangent: bfloat16 [12, 2048, 768], P('rep', 'shard'), may hold values from -6 to 6
Outputs:
- layer_out: bfloat16 [12, 2048, 768], P('rep', 'shard')
- tokens_grad: float32 [12, 2048, 768], P('rep', 'shard')
- grad_query: float32 [768, 768], P('shard')
- grad_keys: float32 [768, 768], P('shard')
- grad_values: float32 [768, 768], P('shard')
- grad_pooled: float32 [768, 768], P('shard')
- grad_output: float32 [768, 768], P('shard')
- grad_taps: float32 [5, 2, 768], P(None, None, 'shard')
- grad_attnbias: float32 [768], P('shard')
- grad_firstgain: float32 [768], P('shard')
- grad_firstshift: float32 [768], P('shard')
- grad_inner: float32 [768, 3072], P('shard')
- grad_innerbias: float32 [3072], P('shard')
- grad_outer: float32 [3072, 768], P('shard')
- grad_outerbias: float32 [768], P('shard')
- grad_secondgain: float32 [768], P('shard')
- grad_secondshift: float32 [768], P('shard')
Inputs may be any that keep to these rules, and one draw needn't show every extreme that they name: `block_ids`: block numbers never fall along a sequence; each block holds 1 to 256 tokens and one holds 256.
All inputs are finite; a program needn't handle non-finite values.
Results may differ from a plain program's by a relative error of at most 0.022.
Values may be sent and summed in bfloat16 or wider, within the bound.
No kernel may reach another device: no remote copies, remote signals or barrier semaphores. Data moves between devices by JAX's collectives and lax.ppermute only.
A program may use at most 256 MiB of HBM per device.

v0:
```python
import jax
import jax.numpy as jnp
from jax import lax
from jax.sharding import PartitionSpec as P

HEAD_DIM = 64
WINDOW = 128
POOL_SPAN = 512
STRIDE = 4
KERNEL = 5


neg_fill = -1e30
norm_eps = 1e-05


def padded(block, sides, width):
    for axis, dim in sides:
        count = lax.axis_size(axis)
        forward = [(i, i + 1) for i in range(count - 1)]
        backward = [(target, source) for source, target in forward]
        low = lax.ppermute(
            lax.slice_in_dim(block, block.shape[dim] - width, None, axis=dim), axis, forward
        )
        high = lax.ppermute(lax.slice_in_dim(block, 0, width, axis=dim), axis, backward)
        block = jnp.concatenate([low, block, high], axis=dim)
    return block


def from_behind(block, axis, distance):
    devices = range(lax.axis_size(axis))
    route = [(i - distance, i) for i in devices if i - distance in devices]
    return lax.ppermute(block, axis, route)


def product(former, latter):
    return jnp.dot(former, latter, preferred_element_type=jnp.float32)


def product_back(former, latter):
    return lax.dot_general(
        former, latter, (((1,), (1,)), ((), ())), preferred_element_type=jnp.float32
    )


def outer_sum(former, latter):
    return lax.dot_general(
        former, latter, (((0,), (0,)), ((), ())), preferred_element_type=jnp.float32
    )


def layer_norm(signal, norm_gain, norm_shift):
    row_mean = jnp.mean(signal, axis=-1, keepdims=True)
    centred = signal - row_mean
    variance = jnp.mean(centred * centred, axis=-1, keepdims=True)
    return centred * lax.rsqrt(variance + norm_eps) * norm_gain + norm_shift


def gelu_exact(signal):
    return jax.nn.gelu(signal, approximate=False)


def attend(queries, key_block, values, allowed, score_scale):
    scores = (
        jnp.einsum("sqhe,skhe->shqk", queries, key_block, preferred_element_type=jnp.float32)
        * score_scale
    )
    masked = jnp.where(allowed[:, None], scores, neg_fill)
    row_max = jnp.max(masked, axis=-1, keepdims=True)
    weights = jnp.exp(masked - row_max)
    row_sum = jnp.sum(weights, axis=-1, keepdims=True)
    attn_probs = (weights / row_sum).astype(jnp.bfloat16)
    attended = jnp.einsum("shqk,skhe->sqhe", attn_probs, values, preferred_element_type=jnp.float32)
    return (attended, row_max + jnp.log(row_sum))


def attend_back(queries, key_block, values, allowed, log_total, grad_out, score_scale):
    scores = (
        jnp.einsum("sqhe,skhe->shqk", queries, key_block, preferred_element_type=jnp.float32)
        * score_scale
    )
    masked = jnp.where(allowed[:, None], scores, neg_fill)
    probs_full = jnp.exp(masked - log_total)
    grad_probs = jnp.einsum("sqhe,skhe->shqk", grad_out, values, preferred_element_type=jnp.float32)
    grad_values = jnp.einsum(
        "shqk,sqhe->skhe",
        probs_full.astype(jnp.bfloat16),
        grad_out,
        preferred_element_type=jnp.float32,
    )
    centre = jnp.sum(probs_full * grad_probs, axis=-1, keepdims=True)
    grad_scores = (probs_full * (grad_probs - centre)).astype(jnp.bfloat16)
    grad_queries = (
        jnp.einsum("shqk,skhe->sqhe", grad_scores, key_block, preferred_element_type=jnp.float32)
        * score_scale
    )
    grad_keys = (
        jnp.einsum("shqk,sqhe->skhe", grad_scores, queries, preferred_element_type=jnp.float32)
        * score_scale
    )
    return (grad_queries, grad_keys, grad_values)


def conv_forward(region, conv_weights, pool_count):
    running = jnp.zeros(region[:, :pool_count, 0].shape, jnp.float32)
    for offset in range(KERNEL):
        lead_block = offset // STRIDE
        running = running + conv_weights[offset] * region[
            :, lead_block : lead_block + pool_count, offset % STRIDE
        ].astype(jnp.float32)
    return running


def conv_backward(region, conv_weights, grad_pooled, pool_count):
    spread = jnp.zeros(region.shape, jnp.float32)
    tap_grads = []
    for offset in range(KERNEL):
        lead_block = offset // STRIDE
        lane_index = offset % STRIDE
        window_rows = region[:, lead_block : lead_block + pool_count, lane_index].astype(
            jnp.float32
        )
        tap_grads.append(jnp.sum(grad_pooled * window_rows, axis=(0, 1)))
        spread = spread.at[:, lead_block : lead_block + pool_count, lane_index].add(
            conv_weights[offset] * grad_pooled
        )
    return (jnp.stack(tap_grads), spread)


def shards(
    tokens,
    query_proj,
    key_proj,
    value_proj,
    pooled_query,
    output_proj,
    conv_taps,
    output_bias,
    first_gain,
    first_shift,
    inner_proj,
    inner_bias,
    outer_proj,
    outer_bias,
    second_gain,
    second_shift,
    block_ids,
    cotangent,
):
    seq_count, tok_span, model_width = tokens.shape
    head_count = model_width // HEAD_DIM
    row_count = seq_count * tok_span
    device_count = lax.axis_size("shard")
    device_index = lax.axis_index("shard")
    seq_length = tok_span * device_count
    half_window = WINDOW // 2
    pool_reach = POOL_SPAN // (2 * STRIDE)
    pool_count = tok_span // STRIDE
    rim_base = half_window - KERNEL // 2
    region_rows = STRIDE * (pool_count + 1)
    ext_rows = tok_span + 2 * half_window
    score_scale = HEAD_DIM ** (-0.5)
    full = (
        lax.all_gather(query_proj, "shard", axis=0, tiled=True),
        lax.all_gather(key_proj, "shard", axis=0, tiled=True),
        lax.all_gather(value_proj, "shard", axis=0, tiled=True),
        lax.all_gather(pooled_query, "shard", axis=0, tiled=True),
        lax.all_gather(output_proj, "shard", axis=0, tiled=True),
        lax.all_gather(conv_taps, "shard", axis=2, tiled=True),
        lax.all_gather(output_bias, "shard", axis=0, tiled=True),
        lax.all_gather(first_gain, "shard", axis=0, tiled=True),
        lax.all_gather(first_shift, "shard", axis=0, tiled=True),
        lax.all_gather(inner_proj, "shard", axis=0, tiled=True),
        lax.all_gather(inner_bias, "shard", axis=0, tiled=True),
        lax.all_gather(outer_proj, "shard", axis=0, tiled=True),
        lax.all_gather(outer_bias, "shard", axis=0, tiled=True),
        lax.all_gather(second_gain, "shard", axis=0, tiled=True),
        lax.all_gather(second_shift, "shard", axis=0, tiled=True),
    )
    taps_full = full[5].astype(jnp.float32)
    pair_proj = jnp.concatenate([full[1], full[2]], axis=1)
    flat = tokens.reshape(row_count, model_width)
    queries = product(flat, full[0]).astype(jnp.bfloat16)
    paired = (
        product(flat, pair_proj).astype(jnp.bfloat16).reshape(seq_count, tok_span, 2, model_width)
    )
    extended = padded(paired, (("shard", 1),), half_window)
    region = extended[:, rim_base : rim_base + region_rows].reshape(
        seq_count, pool_count + 1, STRIDE, 2, model_width
    )
    pooled = conv_forward(region, taps_full, pool_count).astype(jnp.bfloat16)
    arrived = []
    for offset in (2, 1, -1, -2):
        arrived.append(from_behind(pooled, "shard", offset))
    pool_ext = jnp.concatenate([arrived[0], arrived[1], pooled, arrived[2], arrived[3]], axis=1)
    query_pos = device_index * tok_span + jnp.arange(tok_span, dtype=jnp.int32)
    key_pos = device_index * tok_span - half_window + jnp.arange(ext_rows, dtype=jnp.int32)
    query_ids = lax.dynamic_slice_in_dim(block_ids, device_index * tok_span, tok_span, 1)
    key_ids = lax.dynamic_slice_in_dim(
        jnp.pad(block_ids, ((0, 0), (half_window, half_window))),
        device_index * tok_span,
        ext_rows,
        1,
    )
    near = (
        (key_pos[None, :] >= query_pos[:, None] - half_window)
        & (key_pos[None, :] < query_pos[:, None] + half_window)
        & (key_pos[None, :] >= 0)
        & (key_pos[None, :] < seq_length)
    )
    first_mask = near[None] & (key_ids[:, None, :] <= query_ids[:, :, None])
    pool_pos = (device_index - 2) * pool_count + jnp.arange(5 * pool_count, dtype=jnp.int32)
    centre = query_pos // STRIDE
    pool_ids = lax.dynamic_slice_in_dim(
        jnp.pad(block_ids[:, ::STRIDE], ((0, 0), (2 * pool_count, 2 * pool_count))),
        device_index * pool_count,
        5 * pool_count,
        1,
    )
    pool_near = (
        (pool_pos[None, :] >= centre[:, None] - pool_reach)
        & (pool_pos[None, :] < centre[:, None] + pool_reach)
        & (pool_pos[None, :] >= 0)
        & (pool_pos[None, :] < seq_length // STRIDE)
    )
    second_mask = pool_near[None] & (pool_ids[:, None, :] <= query_ids[:, :, None])
    head_shape = (seq_count, tok_span, head_count, HEAD_DIM)
    ext_shape = (seq_count, ext_rows, head_count, HEAD_DIM)
    pool_shape = (seq_count, 5 * pool_count, head_count, HEAD_DIM)
    query_heads = queries.reshape(head_shape)
    key_heads = extended[:, :, 0].reshape(ext_shape)
    value_heads = extended[:, :, 1].reshape(ext_shape)
    first_out, first_log = attend(query_heads, key_heads, value_heads, first_mask, score_scale)
    first = first_out.astype(jnp.bfloat16).reshape(row_count, model_width)
    second_query = product(first, full[3]).astype(jnp.bfloat16)
    pool_keys = pool_ext[:, :, 0].reshape(pool_shape)
    pool_values = pool_ext[:, :, 1].reshape(pool_shape)
    second_heads = second_query.reshape(head_shape)
    second_out, second_log = attend(second_heads, pool_keys, pool_values, second_mask, score_scale)
    second = second_out.astype(jnp.bfloat16).reshape(row_count, model_width)
    mixed = (first.astype(jnp.float32) + second.astype(jnp.float32)).astype(jnp.bfloat16)
    resid = flat.astype(jnp.float32) + product(mixed, full[4]) + full[6].astype(jnp.float32)
    normed, first_pull = jax.vjp(
        layer_norm, resid, full[7].astype(jnp.float32), full[8].astype(jnp.float32)
    )
    normed_low = normed.astype(jnp.bfloat16)
    inner = product(normed_low, full[9]) + full[10].astype(jnp.float32)
    active_full, gelu_pull = jax.vjp(gelu_exact, inner)
    active = active_full.astype(jnp.bfloat16)
    summed = normed + product(active, full[11]) + full[12].astype(jnp.float32)
    result, second_pull = jax.vjp(
        layer_norm, summed, full[13].astype(jnp.float32), full[14].astype(jnp.float32)
    )
    layer_out = result.astype(jnp.bfloat16).reshape(tokens.shape)
    full = (
        lax.all_gather(query_proj, "shard", axis=0, tiled=True),
        lax.all_gather(key_proj, "shard", axis=0, tiled=True),
        lax.all_gather(value_proj, "shard", axis=0, tiled=True),
        lax.all_gather(pooled_query, "shard", axis=0, tiled=True),
        lax.all_gather(output_proj, "shard", axis=0, tiled=True),
        lax.all_gather(conv_taps, "shard", axis=2, tiled=True),
        lax.all_gather(output_bias, "shard", axis=0, tiled=True),
        lax.all_gather(first_gain, "shard", axis=0, tiled=True),
        lax.all_gather(first_shift, "shard", axis=0, tiled=True),
        lax.all_gather(inner_proj, "shard", axis=0, tiled=True),
        lax.all_gather(inner_bias, "shard", axis=0, tiled=True),
        lax.all_gather(outer_proj, "shard", axis=0, tiled=True),
        lax.all_gather(outer_bias, "shard", axis=0, tiled=True),
        lax.all_gather(second_gain, "shard", axis=0, tiled=True),
        lax.all_gather(second_shift, "shard", axis=0, tiled=True),
    )
    pair_proj = jnp.concatenate([full[1], full[2]], axis=1)
    grad_result = cotangent.reshape(row_count, model_width).astype(jnp.float32)
    grad_summed, grad_gain_two, grad_shift_two = second_pull(grad_result)
    grad_outer_low = grad_summed.astype(jnp.bfloat16)
    grad_outer_bias = jnp.sum(grad_outer_low.astype(jnp.float32), axis=0)
    grad_outer_full = outer_sum(active, grad_outer_low)
    grad_active = product_back(grad_outer_low, full[11]).astype(jnp.bfloat16)
    grad_inner_low = gelu_pull(grad_active.astype(jnp.float32))[0].astype(jnp.bfloat16)
    grad_inner_bias = jnp.sum(grad_inner_low.astype(jnp.float32), axis=0)
    grad_inner_full = outer_sum(normed_low, grad_inner_low)
    grad_normed = product_back(grad_inner_low, full[9]) + grad_summed
    grad_resid, grad_gain_one, grad_shift_one = first_pull(grad_normed)
    grad_attn_low = grad_resid.astype(jnp.bfloat16)
    grad_attn_bias = jnp.sum(grad_attn_low.astype(jnp.float32), axis=0)
    grad_output_full = outer_sum(mixed, grad_attn_low)
    grad_mixed = product_back(grad_attn_low, full[4])
    grad_second = grad_mixed.astype(jnp.bfloat16).reshape(head_shape)
    grad_squery, grad_pkeys, grad_pvalues = attend_back(
        second_heads, pool_keys, pool_values, second_mask, second_log, grad_second, score_scale
    )
    grad_squery_low = grad_squery.astype(jnp.bfloat16).reshape(row_count, model_width)
    grad_pooled_full = outer_sum(first, grad_squery_low)
    grad_first = (
        (grad_mixed + product_back(grad_squery_low, full[3]))
        .astype(jnp.bfloat16)
        .reshape(head_shape)
    )
    grad_fquery, grad_fkeys, grad_fvalues = attend_back(
        query_heads, key_heads, value_heads, first_mask, first_log, grad_first, score_scale
    )
    pool_grads = jnp.stack(
        [
            grad_pkeys.reshape(seq_count, 5 * pool_count, model_width),
            grad_pvalues.reshape(seq_count, 5 * pool_count, model_width),
        ],
        axis=2,
    )
    pool_total = pool_grads[:, 2 * pool_count : 3 * pool_count]
    for slot_index, offset in ((0, -2), (1, -1), (3, 1), (4, 2)):
        rim_piece = pool_grads[:, slot_index * pool_count : (slot_index + 1) * pool_count]
        pool_total = pool_total + from_behind(
            rim_piece.astype(jnp.bfloat16), "shard", offset
        ).astype(rim_piece.dtype)
    grad_pool_low = pool_total.astype(jnp.bfloat16).astype(jnp.float32)
    tap_grads, spread = conv_backward(region, taps_full, grad_pool_low, pool_count)
    ext_grads = jnp.stack(
        [
            grad_fkeys.reshape(seq_count, ext_rows, model_width),
            grad_fvalues.reshape(seq_count, ext_rows, model_width),
        ],
        axis=2,
    )
    ext_grads = ext_grads + jnp.pad(
        spread.reshape(seq_count, region_rows, 2, model_width),
        ((0, 0), (rim_base, ext_rows - rim_base - region_rows), (0, 0), (0, 0)),
    )
    own_grads = ext_grads[:, half_window : half_window + tok_span]
    for offset in (1, -1):
        rim_piece = (
            ext_grads[:, half_window + tok_span :] if offset == 1 else ext_grads[:, :half_window]
        )
        arrived_rim = from_behind(rim_piece.astype(jnp.bfloat16), "shard", offset).astype(
            rim_piece.dtype
        )
        lead_rows = 0 if offset == 1 else tok_span - half_window
        own_grads = own_grads + jnp.pad(
            arrived_rim, ((0, 0), (lead_rows, tok_span - half_window - lead_rows), (0, 0), (0, 0))
        )
    grad_pair_low = own_grads.astype(jnp.bfloat16).reshape(row_count, 2 * model_width)
    grad_query_low = grad_fquery.astype(jnp.bfloat16).reshape(row_count, model_width)
    grad_query_full = outer_sum(flat, grad_query_low)
    grad_pair_full = outer_sum(flat, grad_pair_low)
    tokens_grad = (
        grad_resid + product_back(grad_query_low, full[0]) + product_back(grad_pair_low, pair_proj)
    )
    local_grads = (
        grad_query_full,
        grad_pair_full[:, :model_width],
        grad_pair_full[:, model_width:],
        grad_pooled_full,
        grad_output_full,
        tap_grads,
        grad_attn_bias,
        grad_gain_one,
        grad_shift_one,
        grad_inner_full,
        grad_inner_bias,
        grad_outer_full,
        grad_outer_bias,
        grad_gain_two,
        grad_shift_two,
    )
    owned = (
        lax.psum_scatter(local_grads[0], "shard", scatter_dimension=0, tiled=True),
        lax.psum_scatter(local_grads[1], "shard", scatter_dimension=0, tiled=True),
        lax.psum_scatter(local_grads[2], "shard", scatter_dimension=0, tiled=True),
        lax.psum_scatter(local_grads[3], "shard", scatter_dimension=0, tiled=True),
        lax.psum_scatter(local_grads[4], "shard", scatter_dimension=0, tiled=True),
        lax.psum_scatter(local_grads[5], "shard", scatter_dimension=2, tiled=True),
        lax.psum_scatter(local_grads[6], "shard", scatter_dimension=0, tiled=True),
        lax.psum_scatter(local_grads[7], "shard", scatter_dimension=0, tiled=True),
        lax.psum_scatter(local_grads[8], "shard", scatter_dimension=0, tiled=True),
        lax.psum_scatter(local_grads[9], "shard", scatter_dimension=0, tiled=True),
        lax.psum_scatter(local_grads[10], "shard", scatter_dimension=0, tiled=True),
        lax.psum_scatter(local_grads[11], "shard", scatter_dimension=0, tiled=True),
        lax.psum_scatter(local_grads[12], "shard", scatter_dimension=0, tiled=True),
        lax.psum_scatter(local_grads[13], "shard", scatter_dimension=0, tiled=True),
        lax.psum_scatter(local_grads[14], "shard", scatter_dimension=0, tiled=True),
    )
    shared = (
        lax.psum(owned[0].astype(jnp.bfloat16), "rep").astype(jnp.float32),
        lax.psum(owned[1].astype(jnp.bfloat16), "rep").astype(jnp.float32),
        lax.psum(owned[2].astype(jnp.bfloat16), "rep").astype(jnp.float32),
        lax.psum(owned[3].astype(jnp.bfloat16), "rep").astype(jnp.float32),
        lax.psum(owned[4].astype(jnp.bfloat16), "rep").astype(jnp.float32),
        lax.psum(owned[5].astype(jnp.bfloat16), "rep").astype(jnp.float32),
        lax.psum(owned[6].astype(jnp.bfloat16), "rep").astype(jnp.float32),
        lax.psum(owned[7].astype(jnp.bfloat16), "rep").astype(jnp.float32),
        lax.psum(owned[8].astype(jnp.bfloat16), "rep").astype(jnp.float32),
        lax.psum(owned[9].astype(jnp.bfloat16), "rep").astype(jnp.float32),
        lax.psum(owned[10].astype(jnp.bfloat16), "rep").astype(jnp.float32),
        lax.psum(owned[11].astype(jnp.bfloat16), "rep").astype(jnp.float32),
        lax.psum(owned[12].astype(jnp.bfloat16), "rep").astype(jnp.float32),
        lax.psum(owned[13].astype(jnp.bfloat16), "rep").astype(jnp.float32),
        lax.psum(owned[14].astype(jnp.bfloat16), "rep").astype(jnp.float32),
    )
    return (
        layer_out,
        tokens_grad.reshape(tokens.shape),
        shared[0],
        shared[1],
        shared[2],
        shared[3],
        shared[4],
        shared[5],
        shared[6],
        shared[7],
        shared[8],
        shared[9],
        shared[10],
        shared[11],
        shared[12],
        shared[13],
        shared[14],
    )


def solution(mesh):
    in_specs = (
        P("rep", "shard", None),
        P("shard", None),
        P("shard", None),
        P("shard", None),
        P("shard", None),
        P("shard", None),
        P(None, None, "shard"),
        P("shard"),
        P("shard"),
        P("shard"),
        P("shard", None),
        P("shard"),
        P("shard", None),
        P("shard"),
        P("shard"),
        P("shard"),
        P("rep", None),
        P("rep", "shard", None),
    )
    out_specs = (
        P("rep", "shard", None),
        P("rep", "shard", None),
        P("shard", None),
        P("shard", None),
        P("shard", None),
        P("shard", None),
        P("shard", None),
        P(None, None, "shard"),
        P("shard"),
        P("shard"),
        P("shard"),
        P("shard", None),
        P("shard"),
        P("shard", None),
        P("shard"),
        P("shard"),
        P("shard"),
    )
    return jax.shard_map(shards, mesh=mesh, in_specs=in_specs, out_specs=out_specs, check_vma=False)
```

profile of v0, /device:TPU:0, one launch (start us, length us, event | category | flops | bytes accessed | tf_op | source)
XLA Modules:
  0.0 1093.2 jit_solution(16055047314128547115)
XLA Ops:
  27.6 63.3 %all-reduce.21 = (bf16[768]{0:T(1024)(128)(2,1)S(1)}, bf16[768]{0:T(1024)(128)(2,1)S(1)}, bf16[768]{0:T(1024)(128)(2,1)S(1)}, bf16[3072]{0:T(1024)(128)(2,1)S(1)...) all-reduce(bf16[768]{0:T(1024)(128)(2,1)S(1)} %dynamic-update-slice, ...), channel_id=1, replica_groups=mesh['rep'=2,'shard'=16] {'shard'}, use_global_device_ids=true, to_apply=%add.6 | all-reduce | flops 7680 | bytes 30720
  96.1 18.6 %all_gather.55 = bf16[5,2,768]{0,1,2:T(2,128)(2,1)S(1)} all-gather(bf16[5,2,48]{0,1,2:T(2,128)(2,1)S(1)} %copy.131), channel_id=1, replica_groups=mesh['rep'=2,'shard'=16] {'shard'}, dimensions={2}, use_global_device_ids=true | all-gather | bytes 16320 | tf_op jit(solution)/shard_map/all_gather | solution.py:169
  135.0 5.0 reshape.661
  153.4 4.7 reshape.742
  158.1 4.5 copy.129
  175.1 17.5 %collective-permute-start.3 = (bf16[6,32,2,768]{3,2,1,0:T(2,128)(2,1)}, bf16[6,32,2,768]{3,2,1,0:T(2,128)(2,1)}, u32[]{:S(2)}, u32[]{:S(2)}) collective-permute-start(bf16[6,32,2,768]{3,2,1,0:T(2,128)(2,1)} %fusion.70), channel_id=1, source_target_pairs={{0,1},{1,2},{2,3},{3,4},{4,5},{5,6},{6,7},{7,8},{8,9},{9,10},{10,1... | collective-permute-start | bytes 1769480 | tf_op jit(solution)/shard_map/ppermute | solution.py:33
  192.6 5.6 collective-permute-start.2
  198.3 7.8 fusion.95
  206.1 11.6 %copy.128 = bf16[6,256,1,768]{1,3,0,2:T(8,128)(2,1)} copy(bf16[6,256,1,768]{3,2,1,0:T(2,128)(2,1)} %get-tuple-element.203) | data formatting | bytes 4718592 | tf_op jit(solution)/shard_map/slice | solution.py:231
  217.7 11.6 %copy.126 = bf16[6,256,1,768]{1,3,0,2:T(8,128)(2,1)} copy(bf16[6,256,1,768]{3,2,1,0:T(2,128)(2,1)} %get-tuple-element.204) | data formatting | bytes 4718592 | tf_op jit(solution)/shard_map/slice | solution.py:232
  229.3 4.7 fusion.104
  238.1 4.7 fusion.37
  248.8 4.7 reshape.743
  253.6 4.5 copy.144
  266.6 5.9 fusion.97
  272.5 5.8 copy.143
  284.9 4.9 copy.141
  289.7 4.8 convert_bitcast_fusion
  301.7 28.2 %multiply_convert_fusion.1 = (bf16[768,3072]{1,0:T(8,128)(2,1)}, f32[768,3072]{1,0:T(8,128)}, f32[768,3072]{1,0:T(8,128)}) fusion(f32[3072]{0:T(1024)} %convert_element_type.336, bf16[768,3072]{1,0:T(8,128)(2,1)} %all-gather.18.cloned.1.call-done, f32[768,768]{1,0:T(8,128)S(1)} %get-tuple-element.232, f32[768]{0:T(1024)S(1)} %convert_element_type.334, ...), kind=kOutput, calls=%fused_computation.16 | convolution fusion | flops 3782541312 | bytes 30695424 | tf_op jit(solution)/shard_map/dot_general | solution.py:37
  329.9 9.2 all-gather.20.cloned.1.call-done
  339.1 7.3 fusion.107
  352.2 12.9 %convert_reduce_fusion = (f32[3072]{0:T(1024)}, bf16[768,3072]{1,0:T(8,128)(2,1)S(1)}) fusion(f32[768,3072]{1,0:T(8,128)} %get-tuple-element.198, bf16[768,768]{1,0:T(8,128)(2,1)S(1)} %get-tuple-element.187, bf16[3072,768]{1,0:T(8,128)(2,1)} %all-gather.20.cloned.1.call-done, f32[768,3072]{1,0:T(8,128)} %get-tuple-element.233, f32[3072]{0:T(1024)S(1)} %copy-done.62), kind=kOutput, calls=%fused_computation.12 | convolution fusion | flops 3668702208 | bytes 29515776 | tf_op jit(solution)/shard_map/dot_general | solution.py:41
  365.2 5.1 multiply_reduce_fusion.2
  386.4 7.4 fusion.25
  393.9 7.8 copy.159
  401.6 5.6 multiply_reduce_fusion.1
  412.0 4.2 broadcast_multiply_fusion
  416.2 7.8 copy.158
  430.2 5.1 copy.150
  435.3 7.2 fusion.15
  446.3 5.4 collective-permute-start.9
  459.2 6.2 fusion.17
  465.4 12.4 %copy.155 = f32[6,256,1,768]{3,2,1,0:T(1,128)} copy(f32[6,256,1,768]{1,3,0,2:T(8,128)} %bitcast.253) | data formatting | bytes 9437184 | tf_op jit(solution)/shard_map/stack;reshape | solution.py:317
  477.8 7.6 multiply_reduce_fusion
  492.2 12.4 %copy.154 = f32[6,256,1,768]{3,2,1,0:T(1,128)} copy(f32[6,256,1,768]{1,3,0,2:T(8,128)} %bitcast.249) | data formatting | bytes 9437184 | tf_op jit(solution)/shard_map/stack;reshape | solution.py:317
  516.7 6.8 fusion.61
  535.4 12.5 %fusion.89 = (bf16[6,256,2,768]{3,2,1,0:T(2,128)(2,1)S(1)}, f32[6,256,2,768]{3,2,1,0:T(2,128)S(1)}) fusion(f32[6,132,2,768]{3,2,1,0:T(2,128)S(1)} %bitcast.252, f32[6,256,1,768]{3,2,1,0:T(1,128)S(1)} %bitcast.257, f32[6,256,1,768]{3,2,1,0:T(1,128)} %copy.154), kind=kLoop, calls=%fused_computation.228 | loop fusion | flops 7077888 | bytes 28459008 | tf_op jit(solution)/shard_map/convert.13
  574.0 9.0 fusion.85
  584.3 8.8 fusion.110
  598.7 85.9 %all-reduce.20 = (bf16[768]{0:T(1024)(128)(2,1)S(1)}, bf16[768]{0:T(1024)(128)(2,1)S(1)}, bf16[768]{0:T(1024)(128)(2,1)S(1)}, bf16[3072]{0:T(1024)(128)(2,1)S(1)...) all-reduce(f32[768]{0:T(1024)S(1)} %copy-done.57, ...), channel_id=8, replica_groups=mesh['rep'=2,'shard'=16] {'shard'}, use_global_device_ids=true, to_apply=%region_34.35.clone | all-reduce | flops 7680 | bytes 46080
  691.7 43.9 %reduce-scatter.27.cloned.1.call-done = f32[48,768]{1,0:T(8,128)} async-done(((f32[768,768]{1,0:T(8,128)}), f32[48,768]{1,0:T(8,128)}) %reduce-scatter.27.cloned.1.call-update) | async-done | bytes 147472
  737.3 113.3 %reduce-scatter.21.cloned.1.call-done = f32[48,3072]{1,0:T(8,128)} async-done(((f32[768,3072]{1,0:T(8,128)}), f32[48,3072]{1,0:T(8,128)}) %reduce-scatter.21.cloned.1.call-update) | async-done | bytes 589840 | tf_op jit(solution)/shard_map/reduce_scatter | solution.py:374
  852.4 113.3 %reduce-scatter.23.cloned.1.call-done = f32[192,768]{1,0:T(8,128)} async-done(((f32[3072,768]{1,0:T(8,128)}), f32[192,768]{1,0:T(8,128)}) %reduce-scatter.23.cloned.1.call-update) | async-done | bytes 589840 | tf_op jit(solution)/shard_map/reduce_scatter | solution.py:376
  967.6 4.4 fusion.63
  972.0 53.4 %reduce-scatter.31.cloned.1.call-done = f32[48,10]{1,0:T(8,128)} async-done(((f32[768,10]{1,0:T(8,128)}), f32[48,10]{1,0:T(8,128)}) %reduce-scatter.31.cloned.1.call-update) | async-done | bytes 1936
  1026.4 5.0 all-reduce.22
  1035.6 6.5 add_add_fusion.2
  1042.1 33.2 %all-reduce.26.cloned.1.call-done = (bf16[48,768]{0,1:T(8,128)(2,1)}, bf16[48,768]{0,1:T(8,128)(2,1)}, bf16[48,768]{0,1:T(8,128)(2,1)}, bf16[48,768]{1,0:T(8,128...) async-done(((bf16[48,768]{0,1:T(8,128)(2,1)}, bf16[48,768]{0,1:T(8,128)(2,1)}, bf16[48,768]{0,1:T(8,128)(2,1)}, ...) | async-done | bytes 958480 | tf_op jit(solution)/shard_map/psum | solution.py:382
  (407 shorter events, 236.6 us)
Async XLA Ops:
  7.2 117.3 %all-gather.8.cloned.1.call-start = ((), (), s32[]{:S(2)}) async-start(), calls=%async_computation.8 | async-start | bytes 1253376 | tf_op jit(solution)/shard_map/all_gather | solution.py:165
  7.9 118.1 %all-gather.10.cloned.1.call-start = ((), (), s32[]{:S(2)}) async-start(), calls=%async_computation.9 | async-start | bytes 1253376 | tf_op jit(solution)/shard_map/all_gather | solution.py:166
  8.7 140.9 %all-gather.12.cloned.1.call-start = ((), (), s32[]{:S(2)}) async-start(), calls=%async_computation.10 | async-start | bytes 1253376 | tf_op jit(solution)/shard_map/all_gather | solution.py:164
  9.4 235.5 %all-gather.14.cloned.1.call-start = ((), (), s32[]{:S(2)}) async-start(), calls=%async_computation.11 | async-start | bytes 1253376 | tf_op jit(solution)/shard_map/all_gather | solution.py:167
  10.0 286.8 %all-gather.16.cloned.1.call-start = ((), (), s32[]{:S(2)}) async-start(), calls=%async_computation.12 | async-start | bytes 1253376 | tf_op jit(solution)/shard_map/all_gather | solution.py:168
  10.6 291.1 %all-gather.18.cloned.1.call-start = ((), (), s32[]{:S(2)}) async-start(), calls=%async_computation.13 | async-start | bytes 5013504 | tf_op jit(solution)/shard_map/all_gather | solution.py:173
  11.1 328.0 %all-gather.20.cloned.1.call-start = ((), (), s32[]{:S(2)}) async-start(), calls=%async_computation.14 | async-start | bytes 5013504 | tf_op jit(solution)/shard_map/all_gather | solution.py:175
  11.9 673.2 %reduce-scatter.19.cloned.1.call-start = ((), (), s32[]{:S(2)}) async-start(), calls=%async_computation.16 | async-start | bytes 2506752 | tf_op jit(solution)/shard_map/reduce_scatter | solution.py:369
  140.0 8.5 copy-start.67
  140.0 8.5 copy-start.69
  140.0 8.5 copy-start.70
  140.1 8.5 copy-start.71
  140.1 8.5 copy-start.72
  140.1 8.6 copy-start.55
  143.7 18.9 %collective-permute-start = (bf16[6,64,2,768]{3,2,1,0:T(2,128)(2,1)}, bf16[6,64,2,768]{3,2,1,0:T(2,128)(2,1)S(1)}, u32[]{:S(2)}, u32[]{:S(2)}) collective-permute-start(bf16[6,64,2,768]{3,2,1,0:T(2,128)(2,1)} %get-tuple-element.213), channel_id=1, source_target_pairs={{0,1},{1,2},{2,3},{3,4},{4,5},{5,6},{6,7},{7,8},{8,9},{9,10},{10,1... | collective-permute-start | bytes 3538952 | tf_op jit(solution)/shard_map/ppermute | solution.py:22
  147.1 18.3 %collective-permute-start.1 = (bf16[6,64,2,768]{3,2,1,0:T(2,128)(2,1)}, bf16[6,64,2,768]{3,2,1,0:T(2,128)(2,1)}, u32[]{:S(2)}, u32[]{:S(2)}) collective-permute-start(bf16[6,64,2,768]{3,2,1,0:T(2,128)(2,1)} %get-tuple-element.212), channel_id=1, source_target_pairs={{1,0},{2,1},{3,2},{4,3},{5,4},{6,5},{7,6},{8,7},{9,8},{10,9},{11,1... | collective-permute-start | bytes 3538952 | tf_op jit(solution)/shard_map/ppermute | solution.py:25
  169.3 92.5 %copy-start.3 = (bf16[6,132,2,768]{3,2,1,0:T(2,128)(2,1)}, bf16[6,132,2,768]{3,2,1,0:T(2,128)(2,1)S(1)}, u32[]{:S(2)}) copy-start(bf16[6,132,2,768]{3,2,1,0:T(2,128)(2,1)S(1)} %slice.329) | copy-start | bytes 7299076
  172.5 93.6 %collective-permute-start.5 = (bf16[6,32,2,768]{3,2,1,0:T(2,128)(2,1)}, bf16[6,32,2,768]{3,2,1,0:T(2,128)(2,1)S(1)}, u32[]{:S(2)}, u32[]{:S(2)}) collective-permute-start(bf16[6,32,2,768]{3,2,1,0:T(2,128)(2,1)} %fusion.70), channel_id=1, source_target_pairs={{2,0},{3,1},{4,2},{5,3},{6,4},{7,5},{8,6},{9,7},{10,8},{11,9},{12,... | collective-permute-start | bytes 1769480 | tf_op jit(solution)/shard_map/ppermute | solution.py:33
  173.8 90.7 %collective-permute-start.4 = (bf16[6,32,2,768]{3,2,1,0:T(2,128)(2,1)}, bf16[6,32,2,768]{3,2,1,0:T(2,128)(2,1)}, u32[]{:S(2)}, u32[]{:S(2)}) collective-permute-start(bf16[6,32,2,768]{3,2,1,0:T(2,128)(2,1)} %fusion.70), channel_id=1, source_target_pairs={{1,0},{2,1},{3,2},{4,3},{5,4},{6,5},{7,6},{8,7},{9,8},{10,9},{11,1... | collective-permute-start | bytes 1769480 | tf_op jit(solution)/shard_map/ppermute | solution.py:33
  175.1 85.1 %collective-permute-start.3 = (bf16[6,32,2,768]{3,2,1,0:T(2,128)(2,1)}, bf16[6,32,2,768]{3,2,1,0:T(2,128)(2,1)}, u32[]{:S(2)}, u32[]{:S(2)}) collective-permute-start(bf16[6,32,2,768]{3,2,1,0:T(2,128)(2,1)} %fusion.70), channel_id=1, source_target_pairs={{0,1},{1,2},{2,3},{3,4},{4,5},{5,6},{6,7},{7,8},{8,9},{9,10},{10,1... | collective-permute-start | bytes 1769480 | tf_op jit(solution)/shard_map/ppermute | solution.py:33
  192.6 66.1 %collective-permute-start.2 = (bf16[6,32,2,768]{3,2,1,0:T(2,128)(2,1)}, bf16[6,32,2,768]{3,2,1,0:T(2,128)(2,1)}, u32[]{:S(2)}, u32[]{:S(2)}) collective-permute-start(bf16[6,32,2,768]{3,2,1,0:T(2,128)(2,1)} %fusion.70), channel_id=1, source_target_pairs={{0,2},{1,3},{2,4},{3,5},{4,6},{5,7},{6,8},{7,9},{8,10},{9,11},{10,... | collective-permute-start | bytes 1769480 | tf_op jit(solution)/shard_map/ppermute | solution.py:33
  217.7 11.6 %copy-start.31 = (pred[6,128,256]{2,1,0:T(8,128)(4,1)S(1)}, pred[6,128,256]{2,1,0:T(8,128)(4,1)}, u32[]{:S(2)}) copy-start(pred[6,128,256]{2,1,0:T(8,128)(4,1)} %compare_and_fusion) | copy-start | bytes 589828
  299.7 70.6 %copy-start.9 = (f32[768,768]{1,0:T(8,128)}, f32[768,768]{1,0:T(8,128)S(1)}, u32[]{:S(2)}) copy-start(f32[768,768]{1,0:T(8,128)S(1)} %get-tuple-element.232) | copy-start | bytes 7077892
  349.2 15.9 %slice-start.7 = ((s8[4718592]{0:T(1024)(128)(4,1)}), s8[4194304]{0:T(1024)(128)(4,1)S(1)}, s32[]{:S(2)}) async-start(s8[4718592]{0:T(1024)(128)(4,1)} %bitcast.291), calls=%async_computation.31 | async-start | bytes 8388608
  352.2 13.0 %copy-start.28 = (bf16[768,768]{1,0:T(8,128)(2,1)}, bf16[768,768]{1,0:T(8,128)(2,1)S(1)}, u32[]{:S(2)}) copy-start(bf16[768,768]{1,0:T(8,128)(2,1)S(1)} %get-tuple-element.187) | copy-start | bytes 3538948
  352.2 13.0 %slice-start.8 = ((s8[4718592]{0:T(1024)(128)(4,1)}), s8[524288]{0:T(1024)(128)(4,1)S(1)}, s32[]{:S(2)}) async-start(s8[4718592]{0:T(1024)(128)(4,1)} %bitcast.291), calls=%async_computation.32 | async-start | bytes 1048576
  376.0 310.7 %reduce-scatter.17.cloned.1.call-start = ((), (), s32[]{:S(2)}) async-start(), calls=%async_computation.15 | async-start | bytes 2506752 | tf_op jit(solution)/shard_map/reduce_scatter | solution.py:368
  393.9 13.3 %slice-start.3 = ((s8[5898240]{0:T(1024)(128)(4,1)}), s8[1703936]{0:T(1024)(128)(4,1)S(1)}, s32[]{:S(2)}) async-start(s8[5898240]{0:T(1024)(128)(4,1)} %bitcast.242), calls=%async_computation.27 | async-start | bytes 3407872
  442.5 12.9 %copy-start.22 = (bf16[6,128,12,64]{1,0,3,2:T(8,128)(2,1)S(1)}, bf16[6,128,12,64]{1,0,3,2:T(8,128)(2,1)}, u32[]{:S(2)}) copy-start(bf16[6,128,12,64]{1,0,3,2:T(8,128)(2,1)} %copy.130) | copy-start | bytes 3538948
  442.5 12.9 %copy-start.27 = (bf16[6,128,12,64]{1,0,3,2:T(8,128)(2,1)S(1)}, bf16[6,128,12,64]{1,0,3,2:T(8,128)(2,1)}, u32[]{:S(2)}) copy-start(bf16[6,128,12,64]{1,0,3,2:T(8,128)(2,1)} %copy.148) | copy-start | bytes 3538948
  445.0 71.6 %collective-permute-start.6 = (bf16[6,32,2,768]{3,2,1,0:T(2,128)(2,1)}, bf16[6,32,2,768]{3,2,1,0:T(2,128)(2,1)}, u32[]{:S(2)}, u32[]{:S(2)}) collective-permute-start(bf16[6,32,2,768]{3,2,1,0:T(2,128)(2,1)} %get-tuple-element.205), channel_id=1, source_target_pairs={{2,0},{3,1},{4,2},{5,3},{6,4},{7,5},{8,6},{9,7},{10,8},{11,9},{12,... | collective-permute-start | bytes 1769480 | tf_op jit(solution)/shard_map/ppermute | solution.py:33
  446.3 70.3 %collective-permute-start.9 = (bf16[6,32,2,768]{3,2,1,0:T(2,128)(2,1)}, bf16[6,32,2,768]{3,2,1,0:T(2,128)(2,1)}, u32[]{:S(2)}, u32[]{:S(2)}) collective-permute-start(bf16[6,32,2,768]{3,2,1,0:T(2,128)(2,1)} %get-tuple-element.206), channel_id=1, source_target_pairs={{0,2},{1,3},{2,4},{3,5},{4,6},{5,7},{6,8},{7,9},{8,10},{9,11},{10,... | collective-permute-start | bytes 1769480 | tf_op jit(solution)/shard_map/ppermute | solution.py:33
  451.7 64.9 %collective-permute-start.8 = (bf16[6,32,2,768]{3,2,1,0:T(2,128)(2,1)}, bf16[6,32,2,768]{3,2,1,0:T(2,128)(2,1)}, u32[]{:S(2)}, u32[]{:S(2)}) collective-permute-start(bf16[6,32,2,768]{3,2,1,0:T(2,128)(2,1)} %get-tuple-element.207), channel_id=1, source_target_pairs={{0,1},{1,2},{2,3},{3,4},{4,5},{5,6},{6,7},{7,8},{8,9},{9,10},{10,1... | collective-permute-start | bytes 1769480 | tf_op jit(solution)/shard_map/ppermute | solution.py:33
  454.1 62.5 %collective-permute-start.7 = (bf16[6,32,2,768]{3,2,1,0:T(2,128)(2,1)S(1)}, bf16[6,32,2,768]{3,2,1,0:T(2,128)(2,1)}, u32[]{:S(2)}, u32[]{:S(2)}) collective-permute-start(bf16[6,32,2,768]{3,2,1,0:T(2,128)(2,1)S(1)} %get-tuple-element.208), channel_id=1, source_target_pairs={{1,0},{2,1},{3,2},{4,3},{5,4},{6,5},{7,6},{8,7},{9,8},{10,9},{11,1... | collective-permute-start | bytes 1769480 | tf_op jit(solution)/shard_map/ppermute | solution.py:33
  458.0 230.2 %reduce-scatter.25.cloned.1.call-start = ((), (), s32[]{:S(2)}) async-start(), calls=%async_computation.19 | async-start | bytes 2506752
  465.4 20.1 %slice-start = ((s8[9437184]{0:T(1024)(128)(4,1)}), s8[1048576]{0:T(1024)(128)(4,1)S(1)}, s32[]{:S(2)}) async-start(s8[9437184]{0:T(1024)(128)(4,1)} %bitcast.240), calls=%async_computation.24 | async-start | bytes 2097152
  492.2 12.4 %copy-start.8 = (bf16[6,256,1,768]{1,3,0,2:T(8,128)(2,1)S(1)}, bf16[6,256,1,768]{1,3,0,2:T(8,128)(2,1)}, u32[]{:S(2)}) copy-start(bf16[6,256,1,768]{1,3,0,2:T(8,128)(2,1)} %copy.128) | copy-start | bytes 7077892
  516.6 173.4 %reduce-scatter.29.cloned.1.call-start = ((), (), s32[]{:S(2)}) async-start(), calls=%async_computation.21 | async-start | bytes 2506752
  549.8 5.5 collective-permute-start.10
  552.9 5.5 collective-permute-start.11
  570.4 165.2 %reduce-scatter.27.cloned.1.call-start = ((), (), s32[]{:S(2)}) async-start(), calls=%async_computation.20 | async-start | bytes 2506752
  572.4 278.2 %reduce-scatter.21.cloned.1.call-start = ((), (), s32[]{:S(2)}) async-start(), calls=%async_computation.17 | async-start | bytes 10027008 | tf_op jit(solution)/shard_map/reduce_scatter | solution.py:374
  583.0 382.7 %reduce-scatter.23.cloned.1.call-start = ((), (), s32[]{:S(2)}) async-start(), calls=%async_computation.18 | async-start | bytes 10027008 | tf_op jit(solution)/shard_map/reduce_scatter | solution.py:376
  593.1 432.3 %reduce-scatter.31.cloned.1.call-start = ((), (), s32[]{:S(2)}) async-start(), calls=%async_computation.22 | async-start | bytes 417792
  595.8 479.5 %all-reduce.26.cloned.1.call-start = ((), (), s32[]{:S(2)}) async-start(), calls=%async_computation.23 | async-start | bytes 2654208 | tf_op jit(solution)/shard_map/psum | solution.py:382
  967.6 68.0 %copy-start.19 = (f32[768,768]{1,0:T(8,128)S(1)}, f32[768,768]{1,0:T(8,128)}, u32[]{:S(2)}) copy-start(f32[768,768]{1,0:T(8,128)} %copy-done.18) | copy-start | bytes 7077892
  967.6 68.0 %copy-start.59 = (f32[768]{0:T(1024)S(1)}, f32[768]{0:T(1024)}, u32[]{:S(2)}) copy-start(f32[768]{0:T(1024)} %copy-done.58) | copy-start | bytes 9220
  1075.3 10.1 copy-start.38
  (70 other events, 241.0 us)
Sparse Core Ops, SparseCore 0:
  10.3 41.2 all-gather.7
  53.9 37.2 all-gather.9
  93.4 37.7 all-gather.11
  133.4 39.8 all-gather.13
  175.4 54.4 all-gather.15
  232.0 52.8 all-gather.17
  287.1 51.9 all-gather.19
  376.1 61.4 reduce-scatter.18
  458.1 64.0 reduce-scatter.16
  525.8 77.0 reduce-scatter.24
  607.1 62.1 reduce-scatter.28
  673.5 62.0 reduce-scatter.26
  740.2 110.3 reduce-scatter.20
  854.6 111.0 reduce-scatter.22
  970.0 55.3 reduce-scatter.30
  1029.1 46.1 all-reduce.25
where the time goes:
time: 1110 us; the launch traced here: 1090 us
  waiting for transfers between devices  375 us (34%)
  local copies, waits for them, and re-layouts  224 us (20%)
  blocking collectives  173 us (16%)
  matrix products  168 us (15%)
  other arithmetic  89.4 us (8%)
  starting transfers between devices  44.9 us (4%)
  between operations  18.6 us (2%)
    unnamed x2, blocking collectives  149 us
    reduce_scatter x1, waiting for transfers between devices, shards(): lax.psum_scatter(local_grads[9], 'shard', scatter_dimension=0, tiled=True)  113 us
    reduce_scatter x1, waiting for transfers between devices, shards(): lax.psum_scatter(local_grads[11], 'shard', scatter_dimension=0, tiled=True)  113 us
    unnamed x20, waiting for transfers between devices  102 us
    unnamed x227, local copies, waits for them, and re-layouts  56.5 us
    dot_general x6, matrix products, product(): return jnp.dot(former, latter, preferred_element_type=jnp.float32)  49.8 us
    ppermute x10, starting transfers between devices, from_behind(): return lax.ppermute(block, axis, route)  40.5 us
    dot_general x6, matrix products, product_back(): lax.dot_general(former, latter, (((1,), (1,)), ((), ())), preferred_eleme...  34.8 us
  transfers between devices with their start and end apart: 28, of which 8 were waited for; matrix products, arithmetic and copies ran while one was open for 38% of the time, Pallas kernels for 0%

commit v1 on v0

v1 whole, which is shorter than its diff:
```python
import functools

import jax
import jax.numpy as jnp
from jax import lax
from jax.experimental import pallas as pl
from jax.experimental.pallas import tpu as pltpu
from jax.sharding import PartitionSpec as P

HEAD_DIM = 64
WINDOW = 128
POOL_SPAN = 512
STRIDE = 4
KERNEL = 5

neg_fill = -1e30
norm_eps = 1e-05
F32 = jnp.float32
BF16 = jnp.bfloat16
ROOT_HALF = 0.7071067811865476
ROOT_TWO_PI = 0.3989422804014327

HALF = WINDOW // 2
WIDE = 2 * WINDOW
PAIR = 2 * HEAD_DIM
TILE = 256
SLOTS = 16
VMEM_LIMIT = 60 * 1024 * 1024


def product(former, latter):
    return jnp.dot(former, latter, preferred_element_type=F32)


def product_back(former, latter):
    return lax.dot_general(former, latter, (((1,), (1,)), ((), ())), preferred_element_type=F32)


def outer_sum(former, latter):
    return lax.dot_general(former, latter, (((0,), (0,)), ((), ())), preferred_element_type=F32)


def span(index, size):
    return pl.ds(pl.multiple_of(index * size, size), size)


def any_spec():
    return pl.BlockSpec(memory_space=pl.ANY)


def vmem_spec():
    return pl.BlockSpec(memory_space=pltpu.VMEM)


def smem_spec():
    return pl.BlockSpec(memory_space=pltpu.SMEM)


def params(**more):
    return pltpu.CompilerParams(vmem_limit_bytes=VMEM_LIMIT, **more)


def fetch(order, stacks, columns, target, rows, sem):
    copies = []
    slot = 0
    for stack in stacks:
        for part in range(stack.shape[0]):
            copies.append(
                pltpu.make_async_copy(
                    stack.at[part, :, columns], target.at[span(order[slot], rows), :], sem
                )
            )
            slot += 1
    for copy in copies:
        copy.start()
    return copies


def settle(copies):
    for copy in copies:
        copy.wait()


def tap_matrix(pools):
    rows = lax.broadcasted_iota(jnp.int32, (KERNEL * pools, WIDE), 0)
    cols = lax.broadcasted_iota(jnp.int32, (KERNEL * pools, WIDE), 1)
    tap = rows // pools
    wanted = HALF - KERNEL // 2 + STRIDE * (rows - tap * pools) + tap
    return jnp.where(cols == wanted, 1.0, 0.0).astype(BF16)


def tap_matrix_back(pools):
    rows = lax.broadcasted_iota(jnp.int32, (WIDE, KERNEL * pools), 0)
    cols = lax.broadcasted_iota(jnp.int32, (WIDE, KERNEL * pools), 1)
    tap = cols // pools
    wanted = HALF - KERNEL // 2 + STRIDE * (cols - tap * pools) + tap
    return jnp.where(rows == wanted, 1.0, 0.0).astype(BF16)


def project_kernel(nbuf, order, tok, low, high, taps, *refs):
    stacks = refs[:nbuf]
    xext, queries, pairs, pooled, weights, sem = refs[nbuf:]
    width = tok.shape[1]
    copies = fetch(order, stacks, pl.ds(0, 3 * width), weights, stacks[0].shape[1], sem)
    seqs = low.shape[0] // HALF
    for s in range(seqs):
        xext[s * WIDE : s * WIDE + HALF, :] = low[s * HALF : (s + 1) * HALF, :]
        xext[s * WIDE + HALF : s * WIDE + HALF + WINDOW, :] = tok[s * WINDOW : (s + 1) * WINDOW, :]
        xext[s * WIDE + HALF + WINDOW : (s + 1) * WIDE, :] = high[s * HALF : (s + 1) * HALF, :]
    settle(copies)

    @pl.loop(0, 2 * width // TILE)
    def _(n):
        cols = span(n + width // TILE, TILE)
        pairs[:, span(n, TILE)] = product(xext[...], weights[:, cols]).astype(BF16)

    pools = WINDOW // STRIDE
    matrix = tap_matrix(pools)

    @pl.loop(0, seqs)
    def _(s):
        for n in range(2 * width // TILE):
            cols = slice(n * TILE, (n + 1) * TILE)
            slab = product(matrix, pairs[span(s, WIDE), cols])
            total = taps[0:1, cols] * slab[:pools]
            for t in range(1, KERNEL):
                total = total + taps[t : t + 1, cols] * slab[t * pools : (t + 1) * pools]
            pooled[span(s, pools), cols] = total.astype(BF16)

    @pl.loop(0, width // TILE)
    def _(n):
        cols = span(n, TILE)
        queries[:, cols] = product(tok[...], weights[:, cols]).astype(BF16) * HEAD_DIM**-0.5


def lane_masks():
    lane = lax.broadcasted_iota(jnp.int32, (WINDOW, PAIR), 1)
    first = lane < HEAD_DIM
    return first, jnp.where(first, 1.0, 0.0).astype(BF16), jnp.where(first, 0.0, 1.0).astype(BF16)


def side_masks(step):
    row = lax.broadcasted_iota(jnp.int32, (2 * WINDOW, WINDOW), 0)
    lane = lax.broadcasted_iota(jnp.int32, (2 * WINDOW, WINDOW), 1)
    near = lane >= lax.bitwise_and(row, WINDOW - 1) // step
    return near, jnp.where(near, 1.0, 0.0).astype(BF16), jnp.where(near, 0.0, 1.0).astype(BF16)


def stack_heads(block, lanes):
    return jnp.concatenate([block * lanes[1], block * lanes[2]], axis=0)


def merge_heads(block, lanes):
    return jnp.where(lanes[0], block[:WINDOW], block[WINDOW:])


def spread_sides(block, sides):
    return jnp.concatenate([block * sides[1], block * sides[2]], axis=1)


def attend(queries, keys, values, bias, lanes, sides):
    scores = product_back(stack_heads(queries, lanes), keys)
    scores = jnp.where(sides[0], scores[:, :WINDOW], scores[:, WINDOW:]) + bias
    weights = jnp.exp(scores - jnp.max(scores, axis=-1, keepdims=True))
    probs = (weights * (1.0 / jnp.sum(weights, axis=-1, keepdims=True))).astype(BF16)
    mixed = product(spread_sides(probs, sides), values)
    return probs, merge_heads(mixed, lanes)


def attend_back(queries, keys, values, probs, grad_out, lanes, sides):
    grad_stack = stack_heads(grad_out, lanes)
    grad_probs = product_back(grad_stack, values)
    grad_probs = jnp.where(sides[0], grad_probs[:, :WINDOW], grad_probs[:, WINDOW:])
    probs_full = probs.astype(F32)
    centre = jnp.sum(probs_full * grad_probs, axis=-1, keepdims=True)
    grad_scores = spread_sides((probs_full * (grad_probs - centre)).astype(BF16), sides)
    grad_values = outer_sum(spread_sides(probs, sides), grad_stack)
    grad_keys = outer_sum(grad_scores, stack_heads(queries, lanes))
    grad_queries = merge_heads(product(grad_scores, keys), lanes) * HEAD_DIM**-0.5
    return grad_queries, grad_keys, grad_values


def window_kernel(queries, pairs, bias, attended, probs):
    width = queries.shape[1]
    lanes = lane_masks()
    sides = side_masks(1)
    both = jnp.concatenate([bias[0], bias[0]], axis=0)
    for n in range(width // PAIR):
        cols = slice(n * PAIR, (n + 1) * PAIR)
        held, out = attend(
            queries[:, cols],
            pairs[:, cols],
            pairs[:, width + n * PAIR : width + (n + 1) * PAIR],
            both,
            lanes,
            sides,
        )
        probs[0, n] = held
        attended[:, cols] = out.astype(BF16)


def lay_pooled(places, blocks, field):
    pools = blocks[0].shape[0]
    for k, block in enumerate(blocks):
        field[span(places[k], pools), :] = block[...]


def pooled_kernel(nbuf, order, places, attended, bias, *refs):
    blocks = refs[:5]
    stacks = refs[5 : 5 + nbuf]
    queries, mixed, probs, field, weights, sem = refs[5 + nbuf :]
    width = attended.shape[1]
    s = pl.program_id(0)

    @pl.when(s == 0)
    def _():
        copies = fetch(order, stacks, pl.ds(0, width), weights, stacks[0].shape[1], sem)
        field[...] = jnp.zeros_like(field)
        settle(copies)

        @pl.loop(0, width // TILE)
        def _(n):
            cols = span(n, TILE)
            queries[:, cols] = product(attended[...], weights[:, cols]).astype(BF16) * HEAD_DIM**-0.5

    lay_pooled(places, blocks, field)
    lanes = lane_masks()
    sides = side_masks(STRIDE)
    both = jnp.concatenate([bias[0], bias[0]], axis=0)
    rows = span(s, WINDOW)
    for n in range(width // PAIR):
        cols = slice(n * PAIR, (n + 1) * PAIR)
        held, out = attend(
            queries[rows, cols],
            field[:, cols],
            field[:, width + n * PAIR : width + (n + 1) * PAIR],
            both,
            lanes,
            sides,
        )
        probs[0, n] = held
        first = attended[rows, cols].astype(F32)
        mixed[:, cols] = (first + out.astype(BF16).astype(F32)).astype(BF16)


def feed_kernel(counts, order, tok, mixed, cot, vecs, bias_in, *refs):
    at = sum(counts)
    out_stacks = refs[: counts[0]]
    in_stacks = refs[counts[0] : counts[0] + counts[1]]
    down_stacks = refs[counts[0] + counts[1] : at]
    (
        result,
        grad_resid,
        grad_attn,
        grad_in,
        grad_down,
        vec_grads,
        bias_grad,
        w_out,
        w_in,
        w_down,
        centred,
        rstd,
        normed,
        normed_t,
        active,
        slope,
        field,
        grad_outer,
        sems,
    ) = refs[at:]
    rows, width = tok.shape
    hidden = w_in.shape[1]
    first = fetch(order, out_stacks, pl.ds(width, width), w_out, out_stacks[0].shape[1], sems.at[0])
    second = fetch(order, in_stacks, pl.ds(0, hidden), w_in, in_stacks[0].shape[1], sems.at[1])
    third = fetch(order, down_stacks, pl.ds(0, width), w_down, down_stacks[0].shape[1], sems.at[2])
    settle(first)

    @pl.loop(0, width // TILE)
    def _(n):
        cols = span(n, TILE)
        field[:, cols] = tok[:, cols].astype(F32) + product(mixed[...], w_out[:, cols]) + vecs[0:1, cols]

    blocks = rows // WINDOW

    @pl.loop(0, blocks)
    def _(b):
        part = span(b, WINDOW)
        resid = field[part, :]
        middle = resid - jnp.mean(resid, axis=-1, keepdims=True)
        scale = lax.rsqrt(jnp.mean(middle * middle, axis=-1, keepdims=True) + norm_eps)
        unit = middle * scale
        centred[part, :] = unit
        rstd[part, :] = jnp.broadcast_to(scale, (WINDOW, 128))
        low = (unit * vecs[1:2, :] + vecs[2:3, :]).astype(BF16)
        normed[part, :] = low
        normed_t[:, part] = low.T

    settle(second)

    @pl.loop(0, hidden // TILE)
    def _(n):
        cols = span(n, TILE)
        inner = product(normed[...], w_in[:, cols]) + bias_in[0:1, cols]
        cdf = 0.5 + 0.5 * lax.erf(inner * ROOT_HALF)
        active[:, cols] = (inner * cdf).astype(BF16)
        slope[:, cols] = (cdf + inner * (jnp.exp(-0.5 * inner * inner) * ROOT_TWO_PI)).astype(BF16)

    settle(third)

    @pl.loop(0, width // TILE)
    def _(n):
        cols = span(n, TILE)
        unit = centred[:, cols] * vecs[1:2, cols] + vecs[2:3, cols]
        field[:, cols] = unit + product(active[...], w_down[:, cols]) + vecs[3:4, cols]

    vec_grads[...] = jnp.zeros_like(vec_grads)

    def add_row(k, value):
        vec_grads[k : k + 1, :] += jnp.sum(value, axis=0, keepdims=True)

    @pl.loop(0, blocks)
    def _(b):
        part = span(b, WINDOW)
        summed = field[part, :]
        middle = summed - jnp.mean(summed, axis=-1, keepdims=True)
        scale = lax.rsqrt(jnp.mean(middle * middle, axis=-1, keepdims=True) + norm_eps)
        unit = middle * scale
        result[part, :] = (unit * vecs[4:5, :] + vecs[5:6, :]).astype(BF16)
        grad = cot[part, :].astype(F32)
        add_row(4, grad * unit)
        add_row(5, grad)
        u = grad * vecs[4:5, :]
        lean = jnp.mean(u * unit, axis=-1, keepdims=True)
        grad = scale * (u - jnp.mean(u, axis=-1, keepdims=True) - unit * lean)
        field[part, :] = grad
        low = grad.astype(BF16)
        grad_outer[part, :] = low
        add_row(3, low.astype(F32))

    @pl.loop(0, hidden // TILE)
    def _(n):
        cols = span(n, TILE)
        grad = product_back(grad_outer[...], w_down[cols, :]).astype(BF16).astype(F32)
        low = (grad * slope[:, cols].astype(F32)).astype(BF16)
        slope[:, cols] = low
        bias_grad[:, cols] = jnp.sum(low.astype(F32), axis=0, keepdims=True)
        grad_down[cols, :] = outer_sum(active[:, cols], grad_outer[...]).astype(BF16)
        grad_in[:, cols] = product(normed_t[...], low).astype(BF16)

    @pl.loop(0, width // TILE)
    def _(n):
        cols = span(n, TILE)
        field[:, cols] += product_back(slope[...], w_in[cols, :])

    @pl.loop(0, blocks)
    def _(b):
        part = span(b, WINDOW)
        grad = field[part, :]
        unit = centred[part, :]
        add_row(1, grad * unit)
        add_row(2, grad)
        u = grad * vecs[1:2, :]
        lean = jnp.mean(u * unit, axis=-1, keepdims=True)
        grad = rstd[part, 0:1] * (u - jnp.mean(u, axis=-1, keepdims=True) - unit * lean)
        grad_resid[part, :] = grad
        low = grad.astype(BF16)
        grad_attn[part, :] = low
        add_row(0, low.astype(F32))


def pooled_back_kernel(nbuf, order, places, grad_attn, mixed, queries, probs, *refs):
    blocks = refs[:5]
    stacks = refs[5 : 5 + nbuf]
    grad_mixed, grad_queries, grad_out, grad_own, grad_away, grad_near, grad_far = refs[5 + nbuf : 12 + nbuf]
    field, total, grad_low, weights, sem = refs[12 + nbuf :]
    width = grad_attn.shape[1]
    pools = blocks[0].shape[0]
    s = pl.program_id(0)

    @pl.when(s == 0)
    def _():
        copies = fetch(order, stacks, pl.ds(width, width), weights, stacks[0].shape[1], sem)
        field[...] = jnp.zeros_like(field)
        settle(copies)

        @pl.loop(0, width // TILE)
        def _(n):
            cols = span(n, TILE)
            grad = product_back(grad_attn[...], weights[cols, :])
            grad_mixed[:, cols] = grad
            grad_low[:, cols] = grad.astype(BF16)
            grad_out[cols, :] = outer_sum(mixed[:, cols], grad_attn[...]).astype(BF16)

    lay_pooled(places, blocks, field)
    lanes = lane_masks()
    sides = side_masks(STRIDE)
    rows = span(s, WINDOW)
    for n in range(width // PAIR):
        cols = slice(n * PAIR, (n + 1) * PAIR)
        others = slice(width + n * PAIR, width + (n + 1) * PAIR)
        grad_q, grad_k, grad_v = attend_back(
            queries[:, cols], field[:, cols], field[:, others], probs[0, n], grad_low[rows, cols], lanes, sides
        )
        grad_queries[:, cols] = grad_q.astype(BF16)
        total[:, cols] = grad_k
        total[:, others] = grad_v
    for k, target in enumerate((grad_own, grad_away.at[0], grad_away.at[1], grad_near, grad_far)):
        target[...] = total[span(places[k], pools), :].astype(BF16)


def window_back_kernel(nbuf, order, grad_mixed, grad_second, first, queries, pairs, probs, *refs):
    stacks = refs[:nbuf]
    grad_queries, grad_pairs, grad_pooled, grad_low, weights, sem = refs[nbuf:]
    width = first.shape[1]
    s = pl.program_id(0)

    @pl.when(s == 0)
    def _():
        settle(fetch(order, stacks, pl.ds(0, width), weights, stacks[0].shape[1], sem))

        @pl.loop(0, width // TILE)
        def _(n):
            cols = span(n, TILE)
            grad = grad_mixed[:, cols] + product_back(grad_second[...], weights[cols, :])
            grad_low[:, cols] = grad.astype(BF16)
            grad_pooled[cols, :] = outer_sum(first[:, cols], grad_second[...]).astype(BF16)

    lanes = lane_masks()
    sides = side_masks(1)
    rows = span(s, WINDOW)
    for n in range(width // PAIR):
        cols = slice(n * PAIR, (n + 1) * PAIR)
        others = slice(width + n * PAIR, width + (n + 1) * PAIR)
        grad_q, grad_k, grad_v = attend_back(
            queries[:, cols], pairs[:, cols], pairs[:, others], probs[0, n], grad_low[rows, cols], lanes, sides
        )
        grad_queries[:, cols] = grad_q.astype(BF16)
        grad_pairs[:, cols] = grad_k.astype(BF16)
        grad_pairs[:, others] = grad_v.astype(BF16)


def conv_back_kernel(nbuf, order, own, away, near, far, taps, pairs, grad_pairs, *refs):
    stacks = refs[:nbuf]
    total, tap_grads, edges, weights, rim, sem = refs[nbuf:]
    width = pairs.shape[1] // 2
    seqs = pairs.shape[0] // WIDE
    pools = WINDOW // STRIDE
    copies = fetch(order, stacks, pl.ds(width, 2 * width), weights, stacks[0].shape[1], sem)
    matrix = tap_matrix(pools)
    back = tap_matrix_back(pools)
    tap_grads[...] = jnp.zeros_like(tap_grads)

    @pl.loop(0, seqs)
    def _(s):
        for n in range(2 * width // TILE):
            cols = slice(n * TILE, (n + 1) * TILE)
            part = span(s, pools)
            grad = own[part, cols].astype(F32) + away[part, cols].astype(F32)
            grad = grad + near[part, cols].astype(F32) + far[part, cols].astype(F32)
            grad = grad.astype(BF16).astype(F32)
            spread = [(taps[t : t + 1, cols] * grad).astype(BF16) for t in range(KERNEL)]
            whole = grad_pairs[span(s, WIDE), cols].astype(F32) + product(back, jnp.concatenate(spread, axis=0))
            total[span(s, WIDE), cols] = whole.astype(BF16)
            slab = product(matrix, pairs[span(s, WIDE), cols])
            for t in range(KERNEL):
                tap_grads[t : t + 1, cols] += jnp.sum(
                    grad * slab[t * pools : (t + 1) * pools], axis=0, keepdims=True
                )

    for s in range(seqs):
        rim[s * HALF : (s + 1) * HALF, :] = total[s * WIDE : s * WIDE + HALF, :]
        rim[(seqs + s) * HALF : (seqs + s + 1) * HALF, :] = total[s * WIDE + HALF + WINDOW : (s + 1) * WIDE, :]
    settle(copies)

    @pl.loop(0, width // TILE)
    def _(n):
        cols = span(n, TILE)
        edges[:, cols] = product_back(rim[...], weights[cols, :]).astype(BF16)


def weight_grad_kernel(tok, xext, grad_queries, grad_pairs, out, tok_t, xext_t):
    width = tok.shape[1]
    tok_t[...] = tok[...].T
    xext_t[...] = xext[...].T

    @pl.loop(0, width // TILE)
    def _(n):
        cols = span(n, TILE)
        out[:, cols] = product(tok_t[...], grad_queries[:, cols]).astype(BF16)

    @pl.loop(0, 2 * width // TILE)
    def _(n):
        out[:, span(n + width // TILE, TILE)] = product(xext_t[...], grad_pairs[:, span(n, TILE)]).astype(BF16)


def token_grad_kernel(nbuf, order, grad_resid, grad_queries, grad_pairs, low, high, *refs):
    stacks = refs[:nbuf]
    out, weights, own, sem = refs[nbuf:]
    width = grad_resid.shape[1]
    seqs = grad_resid.shape[0] // WINDOW
    copies = fetch(order, stacks, pl.ds(0, 3 * width), weights, stacks[0].shape[1], sem)
    for s in range(seqs):
        own[s * WINDOW : (s + 1) * WINDOW, :width] = grad_queries[s * WINDOW : (s + 1) * WINDOW, :]
        own[s * WINDOW : (s + 1) * WINDOW, width:] = grad_pairs[s * WIDE + HALF : s * WIDE + HALF + WINDOW, :]
    settle(copies)

    @pl.loop(0, width // TILE)
    def _(n):
        cols = span(n, TILE)
        out[:, cols] = grad_resid[:, cols] + product_back(own[...], weights[cols, :])
        for s in range(seqs):
            part = slice(s * HALF, (s + 1) * HALF)
            out[s * WINDOW : s * WINDOW + HALF, cols] += low[part, cols].astype(F32)
            out[s * WINDOW + HALF : (s + 1) * WINDOW, cols] += high[part, cols].astype(F32)


def shape_of(*dims, dtype=BF16):
    return jax.ShapeDtypeStruct(dims, dtype)


def gathered(block):
    rows = block.shape[0] * lax.axis_size("shard") // SLOTS
    full = lax.all_gather(block, "shard", axis=0, tiled=True)
    return [full.reshape(SLOTS, rows, block.shape[1])]


def scattered(whole):
    return lax.psum_scatter(whole, "shard", scatter_dimension=0, tiled=True)


def rep_total(piece):
    count = lax.axis_size("rep")
    total = piece.astype(F32)
    for step in range(1, count):
        route = [(i, (i + step) % count) for i in range(count)]
        total = total + lax.ppermute(piece, "rep", route).astype(F32)
    return total


def shift(block, distance):
    count = lax.axis_size("shard")
    return lax.ppermute(
        block, "shard", [(i, i + distance) for i in range(count) if 0 <= i + distance < count]
    )


def swap(block):
    return lax.ppermute(block, "shard", [(i, i ^ 1) for i in range(lax.axis_size("shard"))])


def hop(block, outer):
    count = lax.axis_size("shard")
    route = [(i, i + (2 if (i % 2 == 0) == outer else -2)) for i in range(count)]
    return lax.ppermute(block, "shard", [(i, j) for i, j in route if 0 <= j < count])


def shards(
    tokens,
    query_proj,
    key_proj,
    value_proj,
    pooled_query,
    output_proj,
    conv_taps,
    output_bias,
    first_gain,
    first_shift,
    inner_proj,
    inner_bias,
    outer_proj,
    outer_bias,
    second_gain,
    second_shift,
    block_ids,
    cotangent,
):
    seqs, tok_span, width = tokens.shape
    rows = seqs * tok_span
    hidden = inner_proj.shape[1]
    device_count = lax.axis_size("shard")
    device_index = lax.axis_index("shard")
    seq_length = tok_span * device_count
    pools = tok_span // STRIDE
    pool_reach = POOL_SPAN // (2 * STRIDE)
    n_pair = width // PAIR
    core = lax.rem(device_index, 2)

    tok = tokens.reshape(rows, width)
    cot = cotangent.reshape(rows, width)
    tok_low = shift(tokens[:, tok_span - HALF :], 1).reshape(seqs * HALF, width)
    tok_high = shift(tokens[:, :HALF], -1).reshape(seqs * HALF, width)

    vectors = [output_bias, first_gain, first_shift, outer_bias, second_gain, second_shift]
    part = width // device_count
    small = jnp.concatenate(vectors + [inner_bias, conv_taps.reshape(-1)])
    lanes = 128 * -(-small.shape[0] // (part * 128))
    small = jnp.pad(small, (0, part * lanes - small.shape[0])).reshape(part, lanes)
    lead = gathered(jnp.concatenate([query_proj, key_proj, value_proj, small], axis=1))
    mid = gathered(jnp.concatenate([pooled_query, output_proj], axis=1))
    up = gathered(inner_proj)
    down = gathered(outer_proj)
    order = jnp.arange(SLOTS, dtype=jnp.int32)

    small_full = jnp.concatenate([stack[:, :, 3 * width :] for stack in lead], axis=0)
    small_full = small_full.reshape(device_count, part * lanes).astype(F32)
    vecs = jnp.stack([small_full[:, k * part : (k + 1) * part].reshape(width) for k in range(6)])
    vecs = jnp.pad(vecs, ((0, 2), (0, 0)))
    at = 6 * part
    bias_in = small_full[:, at : at + hidden // device_count].reshape(1, hidden)
    at = at + hidden // device_count
    taps = small_full[:, at : at + 2 * KERNEL * part].reshape(device_count, KERNEL, 2, part)
    taps = taps.transpose(1, 2, 0, 3).reshape(KERNEL, 2 * width)
    taps = jnp.pad(taps, ((0, 8 - KERNEL), (0, 0)))

    row = jnp.arange(tok_span, dtype=jnp.int32)[:, None]
    lane = jnp.arange(WINDOW, dtype=jnp.int32)[None, :]
    query_ids = lax.dynamic_slice_in_dim(block_ids, device_index * tok_span, tok_span, 1)[:, :, None]

    def bias_for(ids, start, length, step, reach):
        ids = lax.dynamic_slice_in_dim(jnp.pad(ids, ((0, 0), (reach, reach + WINDOW))), start, WIDE, 1)
        near = lane >= row // step
        place = start - reach + jnp.where(near, lane, lane + WINDOW)
        key_ids = jnp.where(near[None], ids[:, None, :WINDOW], ids[:, None, WINDOW:])
        allowed = ((place >= 0) & (place < length))[None] & (key_ids <= query_ids)
        return jnp.where(allowed, 0.0, neg_fill)

    bias_one = bias_for(block_ids, device_index * tok_span, seq_length, 1, HALF)
    bias_two = bias_for(
        block_ids[:, ::STRIDE], device_index * pools, seq_length // STRIDE, STRIDE, pool_reach
    )

    n_lead = len(lead)
    xext, queries, pairs, pooled = pl.pallas_call(
        functools.partial(project_kernel, n_lead),
        out_shape=(
            shape_of(seqs * WIDE, width),
            shape_of(rows, width),
            shape_of(seqs * WIDE, 2 * width),
            shape_of(seqs * pools, 2 * width),
        ),
        in_specs=[smem_spec()] + [vmem_spec()] * 4 + [any_spec()] * n_lead,
        out_specs=(vmem_spec(),) * 4,
        scratch_shapes=[pltpu.VMEM((width, 3 * width), BF16), pltpu.SemaphoreType.DMA],
        compiler_params=params(),
        name="project",
    )(order, tok, tok_low, tok_high, taps, *lead)

    pool_away = swap(pooled)
    pool_far = hop(pooled, True)
    pool_near = hop(pooled, False)
    pool_cross = swap(pool_near)
    pool_blocks = (pooled, pool_away, pool_cross, pool_near, pool_far)
    places = jnp.where(
        core == 0, jnp.array([2, 3, 1, 4, 0], jnp.int32), jnp.array([2, 1, 3, 0, 4], jnp.int32)
    )

    seq_block = lambda r, c: pl.BlockSpec((r, c), lambda s: (s, 0))
    whole_block = lambda r, c: pl.BlockSpec((r, c), lambda s: (0, 0))
    bias_block = pl.BlockSpec((1, tok_span, WINDOW), lambda s: (s, 0, 0))
    prob_block = pl.BlockSpec((1, n_pair, 2 * tok_span, WINDOW), lambda s: (s, 0, 0, 0))
    prob_shape = shape_of(seqs, n_pair, 2 * tok_span, WINDOW)

    attended, probs_one = pl.pallas_call(
        window_kernel,
        grid=(seqs,),
        out_shape=(shape_of(rows, width), prob_shape),
        in_specs=[seq_block(tok_span, width), seq_block(WIDE, 2 * width), bias_block],
        out_specs=(seq_block(tok_span, width), prob_block),
        compiler_params=params(),
        name="window",
    )(queries, pairs, bias_one)

    n_mid = len(mid)
    pool_specs = [seq_block(pools, 2 * width)] * 5
    second, mixed, probs_two = pl.pallas_call(
        functools.partial(pooled_kernel, n_mid),
        grid=(seqs,),
        out_shape=(shape_of(rows, width), shape_of(rows, width), prob_shape),
        in_specs=[smem_spec(), smem_spec(), whole_block(rows, width), bias_block]
        + pool_specs
        + [any_spec()] * n_mid,
        out_specs=(whole_block(rows, width), seq_block(tok_span, width), prob_block),
        scratch_shapes=[
            pltpu.VMEM((WIDE, 2 * width), BF16),
            pltpu.VMEM((width, width), BF16),
            pltpu.SemaphoreType.DMA,
        ],
        compiler_params=params(),
        name="pooled",
    )(order, places, attended, bias_two, *pool_blocks, *mid)

    counts = (len(mid), len(up), len(down))
    result, grad_resid, grad_attn, grad_in, grad_down, vec_grads, bias_grad = pl.pallas_call(
        functools.partial(feed_kernel, counts),
        out_shape=(
            shape_of(rows, width),
            shape_of(rows, width, dtype=F32),
            shape_of(rows, width),
            shape_of(width, hidden),
            shape_of(hidden, width),
            shape_of(8, width, dtype=F32),
            shape_of(1, hidden, dtype=F32),
        ),
        in_specs=[smem_spec()] + [vmem_spec()] * 5 + [any_spec()] * sum(counts),
        out_specs=(vmem_spec(),) * 7,
        scratch_shapes=[
            pltpu.VMEM((width, width), BF16),
            pltpu.VMEM((width, hidden), BF16),
            pltpu.VMEM((hidden, width), BF16),
            pltpu.VMEM((rows, width), F32),
            pltpu.VMEM((rows, 128), F32),
            pltpu.VMEM((rows, width), BF16),
            pltpu.VMEM((width, rows), BF16),
            pltpu.VMEM((rows, hidden), BF16),
            pltpu.VMEM((rows, hidden), BF16),
            pltpu.VMEM((rows, width), F32),
            pltpu.VMEM((rows, width), BF16),
            pltpu.SemaphoreType.DMA((3,)),
        ],
        compiler_params=params(),
        name="feed",
    )(order, tok, mixed, cot, vecs, bias_in, *mid, *up, *down)
    own_down = scattered(grad_down)
    own_in = scattered(grad_in)

    back_shape = shape_of(seqs * pools, 2 * width)
    grad_mixed, grad_second, grad_out, pg_own, pg_away, pg_near, pg_far = pl.pallas_call(
        functools.partial(pooled_back_kernel, n_mid),
        grid=(seqs,),
        out_shape=(
            shape_of(rows, width, dtype=F32),
            shape_of(rows, width),
            shape_of(width, width),
            back_shape,
            shape_of(2, seqs * pools, 2 * width),
            back_shape,
            back_shape,
        ),
        in_specs=[
            smem_spec(),
            smem_spec(),
            whole_block(rows, width),
            whole_block(rows, width),
            seq_block(tok_span, width),
            prob_block,
        ]
        + pool_specs
        + [any_spec()] * n_mid,
        out_specs=(
            whole_block(rows, width),
            seq_block(tok_span, width),
            whole_block(width, width),
            seq_block(pools, 2 * width),
            pl.BlockSpec((2, pools, 2 * width), lambda s: (0, s, 0)),
            seq_block(pools, 2 * width),
            seq_block(pools, 2 * width),
        ),
        scratch_shapes=[
            pltpu.VMEM((WIDE, 2 * width), BF16),
            pltpu.VMEM((WIDE, 2 * width), F32),
            pltpu.VMEM((rows, width), BF16),
            pltpu.VMEM((width, width), BF16),
            pltpu.SemaphoreType.DMA,
        ],
        compiler_params=params(),
        name="pooled_back",
    )(order, places, grad_attn, mixed, second, probs_two, *pool_blocks, *mid)

    pg_cross = swap(pg_away)
    back_far = lax.ppermute(pg_far, "shard", back_route(device_count, True))
    pg_near = (pg_near.astype(F32) + pg_cross[1].astype(F32)).astype(BF16)
    back_near = lax.ppermute(pg_near, "shard", back_route(device_count, False))

    grad_queries, grad_pairs, grad_pooled = pl.pallas_call(
        functools.partial(window_back_kernel, n_mid),
        grid=(seqs,),
        out_shape=(shape_of(rows, width), shape_of(seqs * WIDE, 2 * width), shape_of(width, width)),
        in_specs=[
            smem_spec(),
            whole_block(rows, width),
            whole_block(rows, width),
            whole_block(rows, width),
            seq_block(tok_span, width),
            seq_block(WIDE, 2 * width),
            prob_block,
        ]
        + [any_spec()] * n_mid,
        out_specs=(seq_block(tok_span, width), seq_block(WIDE, 2 * width), whole_block(width, width)),
        scratch_shapes=[
            pltpu.VMEM((rows, width), BF16),
            pltpu.VMEM((width, width), BF16),
            pltpu.SemaphoreType.DMA,
        ],
        compiler_params=params(),
        name="window_back",
    )(order, grad_mixed, grad_second, attended, queries, pairs, probs_one, *mid)

    pair_total, tap_grads, edges = pl.pallas_call(
        functools.partial(conv_back_kernel, n_lead),
        out_shape=(
            shape_of(seqs * WIDE, 2 * width),
            shape_of(8, 2 * width, dtype=F32),
            shape_of(2 * seqs * HALF, width),
        ),
        in_specs=[smem_spec()] + [vmem_spec()] * 7 + [any_spec()] * n_lead,
        out_specs=(vmem_spec(),) * 3,
        scratch_shapes=[
            pltpu.VMEM((width, 2 * width), BF16),
            pltpu.VMEM((2 * seqs * HALF, 2 * width), BF16),
            pltpu.SemaphoreType.DMA,
        ],
        compiler_params=params(),
        name="conv_back",
    )(order, pg_own, pg_cross[0], back_near, back_far, taps, pairs, grad_pairs, *lead)

    edge_high = shift(edges[: seqs * HALF], -1)
    edge_low = shift(edges[seqs * HALF :], 1)

    grad_lead = pl.pallas_call(
        weight_grad_kernel,
        out_shape=shape_of(width, 3 * width),
        in_specs=[vmem_spec()] * 4,
        out_specs=vmem_spec(),
        scratch_shapes=[pltpu.VMEM((width, rows), BF16), pltpu.VMEM((width, seqs * WIDE), BF16)],
        compiler_params=params(),
        name="weight_grad",
    )(tok, xext, grad_queries, pair_total)

    small_grads = jnp.concatenate(
        [vec_grads[k].reshape(device_count, part) for k in range(6)]
        + [
            bias_grad.reshape(device_count, hidden // device_count),
            tap_grads[:KERNEL]
            .reshape(KERNEL, 2, device_count, part)
            .transpose(2, 0, 1, 3)
            .reshape(device_count, 2 * KERNEL * part),
        ],
        axis=1,
    )
    small_grads = jnp.pad(small_grads, ((0, 0), (0, part * lanes - small_grads.shape[1])))
    small_grads = small_grads.reshape(width, lanes).astype(BF16)
    own_mid = scattered(jnp.concatenate([grad_pooled, grad_out], axis=1))
    own_lead = scattered(jnp.concatenate([grad_lead, small_grads], axis=1))

    tokens_grad = pl.pallas_call(
        functools.partial(token_grad_kernel, n_lead),
        out_shape=shape_of(rows, width, dtype=F32),
        in_specs=[smem_spec()] + [vmem_spec()] * 5 + [any_spec()] * n_lead,
        out_specs=vmem_spec(),
        scratch_shapes=[
            pltpu.VMEM((width, 3 * width), BF16),
            pltpu.VMEM((rows, 3 * width), BF16),
            pltpu.SemaphoreType.DMA,
        ],
        compiler_params=params(),
        name="token_grad",
    )(order, grad_resid, grad_queries, pair_total, edge_low, edge_high, *lead)

    own_down = rep_total(own_down)
    own_in = rep_total(own_in)
    own_mid = rep_total(own_mid)
    own_lead = rep_total(own_lead)
    small_own = own_lead[:, 3 * width :].reshape(-1)
    vec_own = [small_own[k * part : (k + 1) * part] for k in range(6)]
    at = 6 * part
    bias_own = small_own[at : at + hidden // device_count]
    at = at + hidden // device_count
    taps_own = small_own[at : at + 2 * KERNEL * part].reshape(KERNEL, 2, part)
    return (
        result.reshape(tokens.shape),
        tokens_grad.reshape(tokens.shape),
        own_lead[:, :width],
        own_lead[:, width : 2 * width],
        own_lead[:, 2 * width : 3 * width],
        own_mid[:, :width],
        own_mid[:, width:],
        taps_own,
        vec_own[0],
        vec_own[1],
        vec_own[2],
        own_in,
        bias_own,
        own_down,
        vec_own[3],
        vec_own[4],
        vec_own[5],
    )


def back_route(count, outer):
    route = [(i, i + (2 if (i % 2 == 0) == outer else -2)) for i in range(count)]
    return [(j, i) for i, j in route if 0 <= j < count]


def solution(mesh):
    in_specs = (
        P("rep", "shard", None),
        P("shard", None),
        P("shard", None),
        P("shard", None),
        P("shard", None),
        P("shard", None),
        P(None, None, "shard"),
        P("shard"),
        P("shard"),
        P("shard"),
        P("shard", None),
        P("shard"),
        P("shard", None),
        P("shard"),
        P("shard"),
        P("shard"),
        P("rep", None),
        P("rep", "shard", None),
    )
    out_specs = (
        P("rep", "shard", None),
        P("rep", "shard", None),
        P("shard", None),
        P("shard", None),
        P("shard", None),
        P("shard", None),
        P("shard", None),
        P(None, None, "shard"),
        P("shard"),
        P("shard"),
        P("shard"),
        P("shard", None),
        P("shard"),
        P("shard", None),
        P("shard"),
        P("shard"),
        P("shard"),
    )
    return jax.shard_map(shards, mesh=mesh, in_specs=in_specs, out_specs=out_specs, check_vma=False)
```

time: 1110 us -> 644 us (0.58); the launches traced: 1090 us -> 643 us
  local copies, waits for them, and re-layouts: 224 us -> 22.3 us
  blocking collectives: 173 us -> 0 us
  matrix products: 168 us -> 0 us
  Pallas kernels: 0 us -> 167 us
  other arithmetic: 89.4 us -> 17.9 us
    dot_general x30 -> x0, matrix products: 168 us -> none  [the longest x6 49.8 us: product(): return jnp.dot(former, latter, preferred_element_type=jnp.float32)]
    pallas_call x0 -> x9, Pallas kernels: none -> 167 us  [the longest x1 46.5 us: shards(): pl.pallas_call(functools.partial(feed_kernel, counts), out_shape=(shape_o...]
    unnamed x2 -> x0, blocking collectives: 149 us -> none
    all_gather x7 -> x4, waiting for transfers between devices: 9.27 us -> 133 us  [gathered(): full = lax.all_gather(block, 'shard', axis=0, tiled=True)]
    unnamed x20 -> x8, waiting for transfers between devices: 102 us -> 2.45 us
    slice x17 -> x14, local copies, waits for them, and re-layouts: 67.5 us -> 4.82 us  [the longest x1 0.81 us: shards(): tap_grads[:KERNEL].reshape(KERNEL, 2, device_count, part)]
    unnamed x227 -> x41, local copies, waits for them, and re-layouts: 56.5 us -> 2.98 us
    another operation x9 -> x13, local copies, waits for them, and re-layouts: 42.2 us -> 1.04 us  [the longest x6 0.52 us: shards(): vec_grads[k].reshape(device_count, part)]
  transfers between devices with their start and end apart: 28 -> 23, of which waited for: 8 -> 12; matrix products, arithmetic and copies ran while one was open for 38% -> 3% of each run, Pallas kernels for 0% -> 12%
where the time goes in v1:
time: 644 us; the launch traced here: 643 us
  waiting for transfers between devices  379 us (59%)
  Pallas kernels  167 us (26%)
  starting transfers between devices  41.8 us (6%)
  local copies, waits for them, and re-layouts  22.3 us (3%)
  other arithmetic  17.9 us (3%)
  between operations  14.6 us (2%)
    reduce_scatter x4, waiting for transfers between devices, scattered(): return lax.psum_scatter(whole, 'shard', scatter_dimension=0, tiled=True)  204 us
    all_gather x4, waiting for transfers between devices, gathered(): full = lax.all_gather(block, 'shard', axis=0, tiled=True)  133 us
    pallas_call x1, Pallas kernels, shards(): pl.pallas_call(functools.partial(feed_kernel, counts), out_shape=(shape_o...  46.5 us
    pallas_call x1, Pallas kernels, shards(): pl.pallas_call(functools.partial(window_back_kernel, n_mid), grid=(seqs,)...  23.1 us
    pallas_call x1, Pallas kernels, shards(): pl.pallas_call(functools.partial(pooled_back_kernel, n_mid), grid=(seqs,)...  22.3 us
    ppermute x1, waiting for transfers between devices, shards(): back_near = lax.ppermute(pg_near, 'shard', back_route(device_count, False))  17.7 us
    ppermute x3, starting transfers between devices, swap(): lax.ppermute(block, 'shard', [(i, i ^ 1) for i in range(lax.axis_size('sh...  16.4 us
    pallas_call x1, Pallas kernels, shards(): pl.pallas_call(functools.partial(project_kernel, n_lead), out_shape=(shap...  14.8 us
  transfers between devices with their start and end apart: 23, of which 12 were waited for; matrix products, arithmetic and copies ran while one was open for 3% of the time, Pallas kernels for 12%

profile of v1, /device:TPU:0, one launch (start us, length us, event | category | flops | bytes accessed | tf_op | source)
XLA Modules:
  0.0 642.9 jit_solution(14583003859118999211)
XLA Ops:
  7.2 0.9 reshape.285
  8.1 4.8 concatenate.19
  12.9 1.7 pad_maximum_fusion.2
  14.6 1.6 pad_maximum_fusion.3
  17.7 2.4 collective-permute-start
  20.1 1.3 collective-permute-start.1
  21.4 46.6 %all-gather.5.cloned.1.call-done = bf16[768,2432]{1,0:T(8,128)(2,1)} async-done(((bf16[48,2432]{1,0:T(8,128)(2,1)}), bf16[768,2432]{1,0:T(8,128)(2,1)}) %all-gather.5.cloned.1.call-update) | async-done | bytes 3735568 | tf_op jit(solution)/shard_map/all_gather | solution.py:524
  68.0 1.0 slice_convert_fusion
  71.1 14.8 %project.1 = (bf16[1536,768]{1,0:T(8,128)(2,1)}, bf16[768,768]{1,0:T(8,128)(2,1)}, bf16[1536,1536]{1,0:T(8,128)(2,1)}, bf16[192,1536]{1,0:T(8,128)(2,1)}) custom-call(s32[16]{0:T(128)} %iota.66.order, bf16[768,768]{1,0:T(8,128)(2,1)} %bitcast.39, bf16[384,768]{1,0:T(8,128)(2,1)} %bitcast.50, bf16[384,768]{1,0:T(8,128)(2,1)} %bitcast.51, ...), custom_call_target="tpu_custom_call" | custom-call | tf_op jit(solution)/shard_map/project/pallas_call | solution.py:634
  85.9 1.3 collective-permute-start.3
  87.9 1.2 collective-permute-start.2
  89.1 5.1 collective-permute-start.5
  94.2 9.9 %collective-permute-done.3.refs_3_ = bf16[192,1536]{1,0:T(8,128)(2,1)S(1)} collective-permute-done((bf16[192,1536]{1,0:T(8,128)(2,1)}, bf16[192,1536]{1,0:T(8,128)(2,1)S(1)}, u32[]{:S(2)}, u32[]{:S(2)}) %collective-permute-start.3) | collective-permute-done | bytes 589856 | tf_op jit(solution)/shard_map/ppermute | solution.py:555
  104.1 14.9 %collective-permute-start.4 = (bf16[192,1536]{1,0:T(8,128)(2,1)S(1)}, bf16[192,1536]{1,0:T(8,128)(2,1)S(1)}, u32[]{:S(2)}, u32[]{:S(2)}) collective-permute-start(bf16[192,1536]{1,0:T(8,128)(2,1)S(1)} %collective-permute-done.3.refs_3_), channel_id=1, source_target_pairs={{0,1},{1,0},{2,3},{3,2},{4,5},{5,4},{6,7},{7,6},{8,9},{9,8},{10,11... | collective-permute-start | bytes 1769480 | tf_op jit(solution)/shard_map/ppermute | solution.py:549
  119.5 1.1 fusion.4
  122.6 10.2 %window.1 = (bf16[768,768]{1,0:T(8,128)(2,1)}, bf16[6,6,256,128]{3,2,1,0:T(8,128)(2,1)}) custom-call(bf16[768,768]{1,0:T(8,128)(2,1)} %get-tuple-element.46.queries, bf16[1536,1536]{1,0:T(8,128)(2,1)} %get-tuple-element.47.pairs, f32[6,128,128]{2,1,0:T(8,128)} %get-tuple-element.110.bias), custom_call_target="tpu_custom_call" | custom-call | tf_op jit(solution)/shard_map/window/pallas_call | solution.py:664
  134.1 14.0 %pooled.1 = (bf16[768,768]{1,0:T(8,128)(2,1)}, bf16[768,768]{1,0:T(8,128)(2,1)}, bf16[6,6,256,128]{3,2,1,0:T(8,128)(2,1)}) custom-call(s32[16]{0:T(128)} %iota.65.order, s32[5]{0:T(128)} %broadcast_select_fusion.places, bf16[768,768]{1,0:T(8,128)(2,1)} %get-tuple-element.48.attended.first, f32[6,128,128]{2,1,0:T(8,128)} %get-tuple-element.109.bias, ...), custom_call_target="tpu_custom_call" | custom-call | tf_op jit(solution)/shard_map/pooled/pallas_call | solution.py:676
  148.1 32.5 %all-gather.9.cloned.1.call-done = bf16[768,3072]{1,0:T(8,128)(2,1)} async-done(((bf16[48,3072]{1,0:T(8,128)(2,1)}), bf16[768,3072]{1,0:T(8,128)(2,1)}) %all-gather.9.cloned.1.call-update) | async-done | bytes 4718608 | tf_op jit(solution)/shard_map/all_gather | solution.py:524
  180.6 54.0 %all-gather.11.cloned.1.call-done = bf16[3072,768]{1,0:T(8,128)(2,1)} async-done(((bf16[192,768]{1,0:T(8,128)(2,1)}), bf16[3072,768]{1,0:T(8,128)(2,1)}) %all-gather.11.cloned.1.call-update) | async-done | bytes 4718608 | tf_op jit(solution)/shard_map/all_gather | solution.py:524
  235.1 46.5 %feed.1 = (bf16[768,768]{1,0:T(8,128)(2,1)}, f32[768,768]{1,0:T(8,128)}, bf16[768,768]{1,0:T(8,128)(2,1)}, bf16[768,3072]{1,0:T(8,128)(2,1)}, bf16[3072,768]{1,0...) custom-call(s32[16]{0:T(128)} %iota.64.order, bf16[768,768]{1,0:T(8,128)(2,1)} %bitcast.40, ...), custom_call_target="tpu_custom_call" | custom-call | tf_op jit(solution)/shard_map/feed/pallas_call | solution.py:694
  282.1 22.3 %pooled_back.1 = (f32[768,768]{1,0:T(8,128)}, bf16[768,768]{1,0:T(8,128)(2,1)}, bf16[768,768]{1,0:T(8,128)(2,1)}, bf16[192,1536]{1,0:T(8,128)(2,1)}, bf16[2,192,...) custom-call(s32[16]{0:T(128)} %iota.71.order, s32[5]{0:T(128)} %broadcast_select_fusion.places, ...), custom_call_target="tpu_custom_call" | custom-call | tf_op jit(solution)/shard_map/pooled_back/pallas_call | solution.py:728
  304.9 23.1 %window_back.1 = (bf16[768,768]{1,0:T(8,128)(2,1)}, bf16[1536,1536]{1,0:T(8,128)(2,1)}, bf16[768,768]{1,0:T(8,128)(2,1)}) custom-call(s32[16]{0:T(128)} %iota.70.order, f32[768,768]{1,0:T(8,128)} %get-tuple-element.56.grad_mixed, bf16[768,768]{1,0:T(8,128)(2,1)} %get-tuple-element.57.grad_second, bf16[768,768]{1,0:T(8,128)(2,1)} %get-tuple-element.48.attended.first, ...), custom_call_target="tpu_custom_call" | custom-call | tf_op jit(solution)/shard_map/window_back/pallas_call | solution.py:775
  328.0 2.8 pad_maximum_fusion.1
  332.5 1.3 collective-permute-start.8
  334.5 0.9 collective-permute-done.6
  335.5 3.7 collective-permute-start.7
  339.4 0.9 slice_bitcast_fusion.1.away
  340.2 7.8 %collective-permute-done.8.far = bf16[192,1536]{1,0:T(8,128)(2,1)S(1)} collective-permute-done((bf16[192,1536]{1,0:T(8,128)(2,1)}, bf16[192,1536]{1,0:T(8,128)(2,1)S(1)}, u32[]{:S(2)}, u32[]{:S(2)}) %collective-permute-start.8) | collective-permute-done | bytes 589856 | tf_op jit(solution)/shard_map/ppermute | solution.py:771
  348.0 17.7 %collective-permute-done.7.near = bf16[192,1536]{1,0:T(8,128)(2,1)S(1)} collective-permute-done((bf16[192,1536]{1,0:T(8,128)(2,1)S(1)}, bf16[192,1536]{1,0:T(8,128)(2,1)S(1)}, u32[]{:S(2)}, u32[]{:S(2)}) %collective-permute-start.7) | collective-permute-done | bytes 589856 | tf_op jit(solution)/shard_map/ppermute | solution.py:773
  366.6 12.2 %conv_back.1 = (bf16[1536,1536]{1,0:T(8,128)(2,1)}, f32[8,1536]{1,0:T(8,128)}, bf16[768,768]{1,0:T(8,128)(2,1)}) custom-call(s32[16]{0:T(128)} %iota.72.order, bf16[192,1536]{1,0:T(8,128)(2,1)} %get-tuple-element.60.own, bf16[192,1536]{1,0:T(8,128)(2,1)} %slice_bitcast_fusion.1.away, bf16[192,1536]{1,0:T(8,128)(2,1)} %copy-done.11, ...), custom_call_target="tpu_custom_call" | custom-call | tf_op jit(solution)/shard_map/conv_back/pallas_call | solution.py:799
  378.8 0.8 slice.220
  380.1 12.7 %weight_grad.1 = bf16[768,2304]{1,0:T(8,128)(2,1)} custom-call(bf16[768,768]{1,0:T(8,128)(2,1)} %bitcast.41, bf16[1536,768]{1,0:T(8,128)(2,1)} %get-tuple-element.67.xext, bf16[768,768]{1,0:T(8,128)(2,1)} %get-tuple-element.59.grad_queries, bf16[1536,1536]{1,0:T(8,128)(2,1)} %get-tuple-element.65.grad_pairs), custom_call_target="tpu_custom_call" | custom-call | tf_op jit(solution)/shard_map/weight_grad/pallas_call | solution.py:820
  392.8 4.2 pad_maximum_fusion
  397.0 1.2 copy-done.5
  398.4 1.3 collective-permute-start.10
  399.7 3.1 collective-permute-start.9
  402.8 1.3 collective-permute-start.12
  405.1 11.2 %token_grad.1 = f32[768,768]{1,0:T(8,128)} custom-call(s32[16]{0:T(128)} %iota.69.order, f32[768,768]{1,0:T(8,128)} %get-tuple-element.52.grad_resid, bf16[768,768]{1,0:T(8,128)(2,1)} %get-tuple-element.59.grad_queries, bf16[1536,1536]{1,0:T(8,128)(2,1)} %get-tuple-element.65.grad_pairs, bf16[384,768]{1,0:T(8,128)(2,1)} %copy-done.12, ...), custom_call_target="tpu_custom_call" | custom-call | tf_op jit(solution)/shard_map/token_grad/pallas_call | solution.py:846
  416.3 57.6 %reduce-scatter.9.cloned.1.call-done = bf16[48,3072]{1,0:T(8,128)(2,1)} async-done(((bf16[768,3072]{1,0:T(8,128)(2,1)}), bf16[48,3072]{1,0:T(8,128)(2,1)}) %reduce-scatter.9.cloned.1.call-update) | async-done | bytes 294928 | tf_op jit(solution)/shard_map/reduce_scatter | solution.py:529
  473.9 1.5 collective-permute-start.13
  476.1 76.3 %reduce-scatter.11.cloned.1.call-done = bf16[192,768]{1,0:T(8,128)(2,1)} async-done(((bf16[3072,768]{1,0:T(8,128)(2,1)}), bf16[192,768]{1,0:T(8,128)(2,1)}) %reduce-scatter.11.cloned.1.call-update) | async-done | bytes 294928 | tf_op jit(solution)/shard_map/reduce_scatter | solution.py:529
  552.4 1.5 collective-permute-start.14
  553.9 1.8 convert_add_fusion.2
  555.7 70.0 %reduce-scatter.5.cloned.1.call-done = bf16[48,2432]{1,0:T(8,128)(2,1)} async-done(((bf16[768,2432]{1,0:T(8,128)(2,1)}), bf16[48,2432]{1,0:T(8,128)(2,1)}) %reduce-scatter.5.cloned.1.call-update) | async-done | bytes 233488 | tf_op jit(solution)/shard_map/reduce_scatter | solution.py:529
  625.7 1.4 collective-permute-start.11
  627.2 1.8 convert_add_fusion.1
  629.0 3.3 collective-permute-done.11
  632.3 1.0 convert_add_fusion.3
  (126 shorter events, 18.0 us)
Async XLA Ops:
  7.2 10.4 %copy-start = (bf16[6,128,768]{2,1,0:T(8,128)(2,1)S(1)}, bf16[6,128,768]{2,1,0:T(8,128)(2,1)}, u32[]{:S(2)}) copy-start(bf16[6,128,768]{2,1,0:T(8,128)(2,1)} %param.20) | copy-start | bytes 3538948
  7.2 60.8 %all-gather.5.cloned.1.call-start = ((), (), s32[]{:S(2)}) async-start(), calls=%async_computation.4 | async-start | bytes 3969024 | tf_op jit(solution)/shard_map/all_gather | solution.py:524
  14.6 118.3 %all-gather.7.cloned.1.call-start = ((), (), s32[]{:S(2)}) async-start(), calls=%async_computation.5 | async-start | bytes 2506752 | tf_op jit(solution)/shard_map/all_gather | solution.py:524
  16.2 164.4 %all-gather.9.cloned.1.call-start = ((), (), s32[]{:S(2)}) async-start(), calls=%async_computation.6 | async-start | bytes 5013504 | tf_op jit(solution)/shard_map/all_gather | solution.py:524
  17.0 217.6 %all-gather.11.cloned.1.call-start = ((), (), s32[]{:S(2)}) async-start(), calls=%async_computation.7 | async-start | bytes 5013504 | tf_op jit(solution)/shard_map/all_gather | solution.py:524
  17.5 385.2 %reduce-scatter.7.cloned.1.call-start = ((), (), s32[]{:S(2)}) async-start(), calls=%async_computation.9 | async-start | bytes 2506752 | tf_op jit(solution)/shard_map/reduce_scatter | solution.py:529
  17.7 52.4 %collective-permute-start = (bf16[6,64,768]{2,1,0:T(8,128)(2,1)S(1)}, bf16[6,64,768]{2,1,0:T(8,128)(2,1)S(1)}, u32[]{:S(2)}, u32[]{:S(2)}) collective-permute-start(bf16[6,64,768]{2,1,0:T(8,128)(2,1)S(1)} %get-tuple-element.84), channel_id=1, source_target_pairs={{0,1},{1,2},{2,3},{3,4},{4,5},{5,6},{6,7},{7,8},{8,9},{9,10},{10,1... | collective-permute-start | bytes 1769480 | tf_op jit(solution)/shard_map/ppermute | solution.py:543
  20.1 50.0 %collective-permute-start.1 = (bf16[6,64,768]{2,1,0:T(8,128)(2,1)S(1)}, bf16[6,64,768]{2,1,0:T(8,128)(2,1)S(1)}, u32[]{:S(2)}, u32[]{:S(2)}) collective-permute-start(bf16[6,64,768]{2,1,0:T(8,128)(2,1)S(1)} %get-tuple-element.83), channel_id=1, source_target_pairs={{1,0},{2,1},{3,2},{4,3},{5,4},{6,5},{7,6},{8,7},{9,8},{10,9},{11,1... | collective-permute-start | bytes 1769480 | tf_op jit(solution)/shard_map/ppermute | solution.py:543
  70.1 0.8 copy-start.8
  70.1 1.0 copy-start.9
  71.1 16.2 %copy-start.18 = (s32[5]{0:T(128)S(1)}, s32[5]{0:T(128)}, u32[]{:S(2)}) copy-start(s32[5]{0:T(128)} %constant.66.clone) | copy-start | bytes 64
  71.1 16.2 %copy-start.19 = (s32[5]{0:T(128)S(1)}, s32[5]{0:T(128)}, u32[]{:S(2)}) copy-start(s32[5]{0:T(128)} %constant.67.clone) | copy-start | bytes 64
  71.1 47.9 %copy-start.15 = (s32[6,2048]{1,0:T(8,128)S(1)}, s32[6,2048]{1,0:T(8,128)}, u32[]{:S(2)}) copy-start(s32[6,2048]{1,0:T(8,128)} %param.36) | copy-start | bytes 147460
  85.9 18.1 %collective-permute-start.3 = (bf16[192,1536]{1,0:T(8,128)(2,1)}, bf16[192,1536]{1,0:T(8,128)(2,1)S(1)}, u32[]{:S(2)}, u32[]{:S(2)}) collective-permute-start(bf16[192,1536]{1,0:T(8,128)(2,1)} %get-tuple-element.49.refs_0_), channel_id=1, source_target_pairs={{1,3},{2,0},{3,5},{4,2},{5,7},{6,4},{7,9},{8,6},{9,11},{10,8},{11,... | collective-permute-start | bytes 1769480 | tf_op jit(solution)/shard_map/ppermute | solution.py:555
  87.9 45.0 %collective-permute-start.2 = (bf16[192,1536]{1,0:T(8,128)(2,1)}, bf16[192,1536]{1,0:T(8,128)(2,1)S(1)}, u32[]{:S(2)}, u32[]{:S(2)}) collective-permute-start(bf16[192,1536]{1,0:T(8,128)(2,1)} %get-tuple-element.49.refs_0_), channel_id=1, source_target_pairs={{0,1},{1,0},{2,3},{3,2},{4,5},{5,4},{6,7},{7,6},{8,9},{9,8},{10,11... | collective-permute-start | bytes 1769480 | tf_op jit(solution)/shard_map/ppermute | solution.py:549
  89.1 43.8 %collective-permute-start.5 = (bf16[192,1536]{1,0:T(8,128)(2,1)}, bf16[192,1536]{1,0:T(8,128)(2,1)S(1)}, u32[]{:S(2)}, u32[]{:S(2)}) collective-permute-start(bf16[192,1536]{1,0:T(8,128)(2,1)} %get-tuple-element.49.refs_0_), channel_id=1, source_target_pairs={{0,2},{2,4},{3,1},{4,6},{5,3},{6,8},{7,5},{8,10},{9,7},{10,12},{11... | collective-permute-start | bytes 1769480 | tf_op jit(solution)/shard_map/ppermute | solution.py:555
  104.1 28.8 %copy-start.1 = (bf16[192,1536]{1,0:T(8,128)(2,1)}, bf16[192,1536]{1,0:T(8,128)(2,1)S(1)}, u32[]{:S(2)}) copy-start(bf16[192,1536]{1,0:T(8,128)(2,1)S(1)} %collective-permute-done.3.refs_3_) | copy-start | bytes 1769476
  104.1 28.8 %collective-permute-start.4 = (bf16[192,1536]{1,0:T(8,128)(2,1)S(1)}, bf16[192,1536]{1,0:T(8,128)(2,1)S(1)}, u32[]{:S(2)}, u32[]{:S(2)}) collective-permute-start(bf16[192,1536]{1,0:T(8,128)(2,1)S(1)} %collective-permute-done.3.refs_3_), channel_id=1, source_target_pairs={{0,1},{1,0},{2,3},{3,2},{4,5},{5,4},{6,7},{7,6},{8,9},{9,8},{10,11... | collective-permute-start | bytes 1769480 | tf_op jit(solution)/shard_map/ppermute | solution.py:549
  132.9 0.8 copy-start.2
  132.9 1.0 copy-start.3
  132.9 1.2 copy-start.4
  304.9 23.1 %copy-start.6 = (bf16[768,768]{1,0:T(8,128)(2,1)S(1)}, bf16[768,768]{1,0:T(8,128)(2,1)}, u32[]{:S(2)}) copy-start(bf16[768,768]{1,0:T(8,128)(2,1)} %get-tuple-element.72) | copy-start | bytes 3538948
  330.9 143.1 %reduce-scatter.9.cloned.1.call-start = ((), (), s32[]{:S(2)}) async-start(), calls=%async_computation.10 | async-start | bytes 5013504 | tf_op jit(solution)/shard_map/reduce_scatter | solution.py:529
  331.4 221.0 %reduce-scatter.11.cloned.1.call-start = ((), (), s32[]{:S(2)}) async-start(), calls=%async_computation.11 | async-start | bytes 5013504 | tf_op jit(solution)/shard_map/reduce_scatter | solution.py:529
  331.5 2.4 copy-start.16
  331.5 3.9 copy-start.13
  331.5 7.7 %copy-start.17 = (f32[1,3072]{1,0:T(1,128)S(1)}, f32[1,3072]{1,0:T(1,128)}, u32[]{:S(2)}) copy-start(f32[1,3072]{1,0:T(1,128)} %get-tuple-element.69) | copy-start | bytes 36868
  332.2 293.5 %reduce-scatter.5.cloned.1.call-start = ((), (), s32[]{:S(2)}) async-start(), calls=%async_computation.8 | async-start | bytes 3969024 | tf_op jit(solution)/shard_map/reduce_scatter | solution.py:529
  332.2 3.1 collective-permute-start.6
  332.5 15.5 %collective-permute-start.8 = (bf16[192,1536]{1,0:T(8,128)(2,1)}, bf16[192,1536]{1,0:T(8,128)(2,1)S(1)}, u32[]{:S(2)}, u32[]{:S(2)}) collective-permute-start(bf16[192,1536]{1,0:T(8,128)(2,1)} %get-tuple-element.63), channel_id=1, source_target_pairs={{2,0},{4,2},{1,3},{6,4},{3,5},{8,6},{5,7},{10,8},{7,9},{12,10},{9,... | collective-permute-start | bytes 1769480 | tf_op jit(solution)/shard_map/ppermute | solution.py:771
  335.5 30.3 %collective-permute-start.7 = (bf16[192,1536]{1,0:T(8,128)(2,1)S(1)}, bf16[192,1536]{1,0:T(8,128)(2,1)S(1)}, u32[]{:S(2)}, u32[]{:S(2)}) collective-permute-start(bf16[192,1536]{1,0:T(8,128)(2,1)S(1)} %fusion), channel_id=1, source_target_pairs={{3,1},{0,2},{5,3},{2,4},{7,5},{4,6},{9,7},{6,8},{11,9},{8,10},{13,... | collective-permute-start | bytes 1769480 | tf_op jit(solution)/shard_map/ppermute | solution.py:773
  348.0 18.3 %copy-start.7 = (bf16[192,1536]{1,0:T(8,128)(2,1)}, bf16[192,1536]{1,0:T(8,128)(2,1)S(1)}, u32[]{:S(2)}) copy-start(bf16[192,1536]{1,0:T(8,128)(2,1)S(1)} %collective-permute-done.8.far) | copy-start | bytes 1769476
  365.8 0.8 copy-start.11
  397.0 1.3 copy-start.5
  398.4 5.7 collective-permute-start.10
  399.7 4.7 collective-permute-start.9
  402.8 72.6 %collective-permute-start.12 = (bf16[48,1536]{1,0:T(8,128)(2,1)}, bf16[48,1536]{1,0:T(8,128)(2,1)S(1)}, u32[]{:S(2)}, u32[]{:S(2)}) collective-permute-start(bf16[48,1536]{1,0:T(8,128)(2,1)} %reduce-scatter.7.cloned.1.call-done), channel_id=1, source_target_pairs={{0,16},{16,0},{1,17},{17,1},{2,18},{18,2},{3,19},{19,3},{4,20},{20... | collective-permute-start | bytes 442376 | tf_op jit(solution)/shard_map/ppermute | solution.py:537
  404.1 0.8 copy-start.10
  404.3 0.8 copy-start.12
  405.1 70.2 %copy-start.14 = (bf16[48,1536]{1,0:T(8,128)(2,1)S(1)}, bf16[48,1536]{1,0:T(8,128)(2,1)}, u32[]{:S(2)}) copy-start(bf16[48,1536]{1,0:T(8,128)(2,1)} %reduce-scatter.7.cloned.1.call-done) | copy-start | bytes 442372
  473.9 80.0 %collective-permute-start.13 = (bf16[48,3072]{1,0:T(8,128)(2,1)}, bf16[48,3072]{1,0:T(8,128)(2,1)S(1)}, u32[]{:S(2)}, u32[]{:S(2)}) collective-permute-start(bf16[48,3072]{1,0:T(8,128)(2,1)} %reduce-scatter.9.cloned.1.call-done), channel_id=1, source_target_pairs={{0,16},{16,0},{1,17},{17,1},{2,18},{18,2},{3,19},{19,3},{4,20},{20... | collective-permute-start | bytes 884744 | tf_op jit(solution)/shard_map/ppermute | solution.py:537
  552.4 74.7 %collective-permute-start.14 = (bf16[192,768]{1,0:T(8,128)(2,1)}, bf16[192,768]{1,0:T(8,128)(2,1)S(1)}, u32[]{:S(2)}, u32[]{:S(2)}) collective-permute-start(bf16[192,768]{1,0:T(8,128)(2,1)} %reduce-scatter.11.cloned.1.call-done), channel_id=1, source_target_pairs={{0,16},{16,0},{1,17},{17,1},{2,18},{18,2},{3,19},{19,3},{4,20},{20... | collective-permute-start | bytes 884744 | tf_op jit(solution)/shard_map/ppermute | solution.py:537
  625.7 6.6 %collective-permute-start.11 = (bf16[48,2432]{1,0:T(8,128)(2,1)}, bf16[48,2432]{1,0:T(8,128)(2,1)S(1)}, u32[]{:S(2)}, u32[]{:S(2)}) collective-permute-start(bf16[48,2432]{1,0:T(8,128)(2,1)} %reduce-scatter.5.cloned.1.call-done), channel_id=1, source_target_pairs={{0,16},{16,0},{1,17},{17,1},{2,18},{18,2},{3,19},{19,3},{4,20},{20... | collective-permute-start | bytes 700424 | tf_op jit(solution)/shard_map/ppermute | solution.py:537
Sparse Core Ops, SparseCore 0:
  14.7 53.3 all-gather.4
  70.9 54.8 all-gather.6
  128.0 52.4 all-gather.8
  182.7 51.7 all-gather.10
  331.0 64.0 reduce-scatter.6
  399.3 74.5 reduce-scatter.8
  477.8 74.6 reduce-scatter.10
  556.8 68.8 reduce-scatter.4

commit v2 on v1

--- a/solution.py
+++ b/solution.py
@@ -26,6 +26,7 @@
 TILE = 256
 SLOTS = 16
 VMEM_LIMIT = 60 * 1024 * 1024
+SCALE = 0.05
 
 
 def product(former, latter):
@@ -60,25 +61,84 @@
     return pltpu.CompilerParams(vmem_limit_bytes=VMEM_LIMIT, **more)
 
 
-def fetch(order, stacks, columns, target, rows, sem):
+def cost(microseconds):
+    return pl.CostEstimate(
+        flops=int(microseconds * 1.1e9 * SCALE), bytes_accessed=int(microseconds * 3.5e6 * SCALE), transcendentals=0
+    )
+
+
+def fetch(order, stacks, table, half, columns, target, sem):
+    rows = stacks[0].shape[1]
+    pairs = []
+    for k, places in enumerate(table):
+        goal = target.at[span(order[k], rows), :]
+        pairs.append(
+            [
+                pltpu.make_async_copy(
+                    stacks[stack].at[part, :, pl.ds(start + columns[0], columns[1])], goal, sem
+                )
+                for stack, part, start in places
+            ]
+        )
+
+    @pl.when(order[SLOTS] == half)
+    def _():
+        for pair in pairs:
+            pair[0].start()
+
+    @pl.when(order[SLOTS] != half)
+    def _():
+        for pair in pairs:
+            pair[1].start()
+
+    return [pair[0] for pair in pairs]
+
+
+def fetch_all(order, stacks, table, half_width, target, sem):
     copies = []
-    slot = 0
-    for stack in stacks:
-        for part in range(stack.shape[0]):
-            copies.append(
-                pltpu.make_async_copy(
-                    stack.at[part, :, columns], target.at[span(order[slot], rows), :], sem
-                )
+    for half in range(2):
+        view = target.at[:, pl.ds(half * half_width, half_width)]
+        copies = copies + fetch(order, stacks, table, half, (0, half_width), view, sem)
+    return copies
+
+
+def fetch_bulk(bulk, w_in, w_down, sems):
+    width = bulk.shape[1]
+    block = width // SLOTS
+    folds = w_in.shape[1] // width
+    first, second = [], []
+    for j in range(SLOTS):
+        start = j * 2 * folds * block
+        for m in range(folds):
+            source = bulk.at[pl.ds(start + m * block, block), :]
+            target = w_in.at[pl.ds(j * block, block), pl.ds(m * width, width)]
+            first.append(pltpu.make_async_copy(source, target, sems[0]))
+        source = bulk.at[pl.ds(start + folds * block, folds * block), :]
+        target = w_down.at[pl.ds(j * folds * block, folds * block), :]
+        second.append(pltpu.make_async_copy(source, target, sems[1]))
+    for copy in first + second:
+        copy.start()
+    return first, second
+
+
+def settle(copies):
+    for copy in copies:
+        copy.wait()
+
+
+def emit(order, source, columns, rows, targets, start, sem):
+    copies = []
+    for k in range(SLOTS):
+        copies.append(
+            pltpu.make_async_copy(
+                source.at[span(order[k], rows), columns],
+                targets[k % 2].at[k // 2 % 2, k // 4, :, pl.ds(start, columns.size)],
+                sem,
             )
-            slot += 1
+        )
     for copy in copies:
         copy.start()
     return copies
-
-
-def settle(copies):
-    for copy in copies:
-        copy.wait()
 
 
 def tap_matrix(pools):
@@ -97,11 +157,32 @@
     return jnp.where(rows == wanted, 1.0, 0.0).astype(BF16)
 
 
-def project_kernel(nbuf, order, tok, low, high, taps, *refs):
-    stacks = refs[:nbuf]
-    xext, queries, pairs, pooled, weights, sem = refs[nbuf:]
+TAP_ROW = 6
+BIAS_ROW = TAP_ROW + 2 * KERNEL
+SMALL = BIAS_ROW + 4
+SMALL_ROWS = 16
+
+
+def tap_row(tap, kind):
+    return TAP_ROW + 2 * tap + kind
+
+
+def project_kernel(table, order, tok, low, high, *refs):
+    xext, queries, pairs, pooled, vecs, weights, narrow, sem = refs[-8:]
+    stacks = refs[:-8]
     width = tok.shape[1]
-    copies = fetch(order, stacks, pl.ds(0, 3 * width), weights, stacks[0].shape[1], sem)
+    copies = fetch_all(order, stacks, table, 3 * width // 2, weights, sem)
+    rows = stacks[0].shape[1]
+    for k, places in enumerate(table):
+        stack, part, start = places[0]
+        copies.append(
+            pltpu.make_async_copy(
+                stacks[stack].at[part, :, pl.ds(start + 3 * width // 2, 128)],
+                narrow.at[span(order[k], rows), :],
+                sem,
+            )
+        )
+        copies[-1].start()
     seqs = low.shape[0] // HALF
     for s in range(seqs):
         xext[s * WIDE : s * WIDE + HALF, :] = low[s * HALF : (s + 1) * HALF, :]
@@ -114,6 +195,7 @@
         cols = span(n + width // TILE, TILE)
         pairs[:, span(n, TILE)] = product(xext[...], weights[:, cols]).astype(BF16)
 
+    vecs[...] = narrow[...].astype(F32).T[: vecs.shape[0]]
     pools = WINDOW // STRIDE
     matrix = tap_matrix(pools)
 
@@ -121,10 +203,12 @@
     def _(s):
         for n in range(2 * width // TILE):
             cols = slice(n * TILE, (n + 1) * TILE)
+            kind, own = divmod(n * TILE, width)
             slab = product(matrix, pairs[span(s, WIDE), cols])
-            total = taps[0:1, cols] * slab[:pools]
-            for t in range(1, KERNEL):
-                total = total + taps[t : t + 1, cols] * slab[t * pools : (t + 1) * pools]
+            total = 0.0
+            for t in range(KERNEL):
+                row = tap_row(t, kind)
+                total = total + vecs[row : row + 1, own : own + TILE] * slab[t * pools : (t + 1) * pools]
             pooled[span(s, pools), cols] = total.astype(BF16)
 
     @pl.loop(0, width // TILE)
@@ -205,16 +289,16 @@
         field[span(places[k], pools), :] = block[...]
 
 
-def pooled_kernel(nbuf, order, places, attended, bias, *refs):
+def pooled_kernel(table, order, places, attended, bias, *refs):
     blocks = refs[:5]
-    stacks = refs[5 : 5 + nbuf]
-    queries, mixed, probs, field, weights, sem = refs[5 + nbuf :]
+    stacks = refs[5:-6]
+    queries, mixed, probs, field, weights, sem = refs[-6:]
     width = attended.shape[1]
     s = pl.program_id(0)
 
     @pl.when(s == 0)
     def _():
-        copies = fetch(order, stacks, pl.ds(0, width), weights, stacks[0].shape[1], sem)
+        copies = fetch(order, stacks, table, 0, (0, width), weights, sem)
         field[...] = jnp.zeros_like(field)
         settle(copies)
 
@@ -243,19 +327,15 @@
         mixed[:, cols] = (first + out.astype(BF16).astype(F32)).astype(BF16)
 
 
-def feed_kernel(counts, order, tok, mixed, cot, vecs, bias_in, *refs):
-    at = sum(counts)
-    out_stacks = refs[: counts[0]]
-    in_stacks = refs[counts[0] : counts[0] + counts[1]]
-    down_stacks = refs[counts[0] + counts[1] : at]
+def feed_kernel(table, order, tok, mixed, cot, vecs, bias_in, bulk, *refs):
+    at = len(refs) - 21
+    mid_stacks = refs[:at]
     (
         result,
         grad_resid,
         grad_attn,
-        grad_in,
-        grad_down,
+        gone,
         vec_grads,
-        bias_grad,
         w_out,
         w_in,
         w_down,
@@ -267,13 +347,16 @@
         slope,
         field,
         grad_outer,
+        grad_in,
+        grad_down,
+        bias_grad,
+        narrow,
         sems,
     ) = refs[at:]
     rows, width = tok.shape
     hidden = w_in.shape[1]
-    first = fetch(order, out_stacks, pl.ds(width, width), w_out, out_stacks[0].shape[1], sems.at[0])
-    second = fetch(order, in_stacks, pl.ds(0, hidden), w_in, in_stacks[0].shape[1], sems.at[1])
-    third = fetch(order, down_stacks, pl.ds(0, width), w_down, down_stacks[0].shape[1], sems.at[2])
+    first = fetch(order, mid_stacks, table, 1, (0, width), w_out, sems.at[0])
+    second, third = fetch_bulk(bulk, w_in, w_down, (sems.at[1], sems.at[2]))
     settle(first)
 
     @pl.loop(0, width // TILE)
@@ -348,6 +431,21 @@
         grad_down[cols, :] = outer_sum(active[:, cols], grad_outer[...]).astype(BF16)
         grad_in[:, cols] = product(normed_t[...], low).astype(BF16)
 
+    block = width // SLOTS
+    folds = hidden // width
+    each = gone.shape[0] // SLOTS
+    emits = []
+    for j in range(SLOTS):
+        for m in range(folds):
+            source = grad_in.at[pl.ds(j * block, block), pl.ds(m * width, width)]
+            target = gone.at[pl.ds(j * each + m * block, block), :]
+            emits.append(pltpu.make_async_copy(source, target, sems.at[3]))
+        source = grad_down.at[pl.ds(j * folds * block, folds * block), :]
+        target = gone.at[pl.ds(j * each + folds * block, folds * block), :]
+        emits.append(pltpu.make_async_copy(source, target, sems.at[3]))
+    for copy in emits:
+        copy.start()
+
     @pl.loop(0, width // TILE)
     def _(n):
         cols = span(n, TILE)
@@ -368,19 +466,33 @@
         grad_attn[part, :] = low
         add_row(0, low.astype(F32))
 
-
-def pooled_back_kernel(nbuf, order, places, grad_attn, mixed, queries, probs, *refs):
+    narrow[...] = jnp.zeros_like(narrow)
+    small = narrow.shape[1]
+    for j in range(SLOTS):
+        narrow[j, :8, :block] = vec_grads[:, j * block : (j + 1) * block].astype(BF16)
+        part = bias_grad[:, j * folds * block : (j + 1) * folds * block]
+        narrow[j, 8:9, : folds * block] = part.astype(BF16)
+        emits.append(
+            pltpu.make_async_copy(
+                narrow.at[j], gone.at[pl.ds(j * each + each - small, small), :], sems.at[3]
+            )
+        )
+        emits[-1].start()
+    settle(emits)
+
+
+def pooled_back_kernel(table, order, places, grad_attn, mixed, queries, probs, *refs):
     blocks = refs[:5]
-    stacks = refs[5 : 5 + nbuf]
-    grad_mixed, grad_queries, grad_out, grad_own, grad_away, grad_near, grad_far = refs[5 + nbuf : 12 + nbuf]
-    field, total, grad_low, weights, sem = refs[12 + nbuf :]
+    stacks = refs[5:-12]
+    grad_mixed, grad_queries, grad_out, grad_own, grad_away, grad_near, grad_far = refs[-12:-5]
+    field, total, grad_low, weights, sem = refs[-5:]
     width = grad_attn.shape[1]
     pools = blocks[0].shape[0]
     s = pl.program_id(0)
 
     @pl.when(s == 0)
     def _():
-        copies = fetch(order, stacks, pl.ds(width, width), weights, stacks[0].shape[1], sem)
+        copies = fetch(order, stacks, table, 1, (0, width), weights, sem)
         field[...] = jnp.zeros_like(field)
         settle(copies)
 
@@ -409,15 +521,15 @@
         target[...] = total[span(places[k], pools), :].astype(BF16)
 
 
-def window_back_kernel(nbuf, order, grad_mixed, grad_second, first, queries, pairs, probs, *refs):
-    stacks = refs[:nbuf]
-    grad_queries, grad_pairs, grad_pooled, grad_low, weights, sem = refs[nbuf:]
+def window_back_kernel(table, order, grad_mixed, grad_second, first, queries, pairs, probs, *refs):
+    stacks = refs[:-6]
+    grad_queries, grad_pairs, grad_pooled, grad_low, weights, sem = refs[-6:]
     width = first.shape[1]
     s = pl.program_id(0)
 
     @pl.when(s == 0)
     def _():
-        settle(fetch(order, stacks, pl.ds(0, width), weights, stacks[0].shape[1], sem))
+        settle(fetch(order, stacks, table, 0, (0, width), weights, sem))
 
         @pl.loop(0, width // TILE)
         def _(n):
@@ -440,13 +552,13 @@
         grad_pairs[:, others] = grad_v.astype(BF16)
 
 
-def conv_back_kernel(nbuf, order, own, away, near, far, taps, pairs, grad_pairs, *refs):
-    stacks = refs[:nbuf]
-    total, tap_grads, edges, weights, rim, sem = refs[nbuf:]
+def conv_back_kernel(table, order, own, away, near, far, vecs, pairs, grad_pairs, *refs):
+    stacks = refs[:-6]
+    total, tap_grads, edges, weights, rim, sem = refs[-6:]
     width = pairs.shape[1] // 2
     seqs = pairs.shape[0] // WIDE
     pools = WINDOW // STRIDE
-    copies = fetch(order, stacks, pl.ds(width, 2 * width), weights, stacks[0].shape[1], sem)
+    copies = fetch_all(order, stacks, table, 3 * width // 2, weights, sem)
     matrix = tap_matrix(pools)
     back = tap_matrix_back(pools)
     tap_grads[...] = jnp.zeros_like(tap_grads)
@@ -455,16 +567,19 @@
     def _(s):
         for n in range(2 * width // TILE):
             cols = slice(n * TILE, (n + 1) * TILE)
+            kind, start = divmod(n * TILE, width)
+            taps = [vecs[tap_row(t, kind) : tap_row(t, kind) + 1, start : start + TILE] for t in range(KERNEL)]
             part = span(s, pools)
             grad = own[part, cols].astype(F32) + away[part, cols].astype(F32)
             grad = grad + near[part, cols].astype(F32) + far[part, cols].astype(F32)
             grad = grad.astype(BF16).astype(F32)
-            spread = [(taps[t : t + 1, cols] * grad).astype(BF16) for t in range(KERNEL)]
+            spread = [(taps[t] * grad).astype(BF16) for t in range(KERNEL)]
             whole = grad_pairs[span(s, WIDE), cols].astype(F32) + product(back, jnp.concatenate(spread, axis=0))
             total[span(s, WIDE), cols] = whole.astype(BF16)
             slab = product(matrix, pairs[span(s, WIDE), cols])
             for t in range(KERNEL):
-                tap_grads[t : t + 1, cols] += jnp.sum(
+                row = 2 * t + kind
+                tap_grads[row : row + 1, start : start + TILE] += jnp.sum(
                     grad * slab[t * pools : (t + 1) * pools], axis=0, keepdims=True
                 )
 
@@ -476,30 +591,41 @@
     @pl.loop(0, width // TILE)
     def _(n):
         cols = span(n, TILE)
-        edges[:, cols] = product_back(rim[...], weights[cols, :]).astype(BF16)
-
-
-def weight_grad_kernel(tok, xext, grad_queries, grad_pairs, out, tok_t, xext_t):
+        edges[:, cols] = product_back(rim[...], weights[cols, width:]).astype(BF16)
+
+
+def weight_grad_kernel(order, tok, xext, grad_queries, grad_pairs, tap_grads, *refs):
+    grad_pooled, grad_out, keep, give, tok_t, xext_t, total, narrow, sem = refs
     width = tok.shape[1]
+    block = width // SLOTS
+    targets = (keep, give)
+    copies = emit(order, grad_pooled, pl.ds(0, width), block, targets, 3 * width, sem)
+    copies += emit(order, grad_out, pl.ds(0, width), block, targets, 4 * width, sem)
+    taps = jnp.concatenate([tap_grads[...], jnp.zeros((112, width), F32)], axis=0).T
+    narrow[...] = taps.astype(BF16)
+    copies += emit(order, narrow, pl.ds(0, 128), block, targets, 5 * width, sem)
     tok_t[...] = tok[...].T
     xext_t[...] = xext[...].T
 
     @pl.loop(0, width // TILE)
     def _(n):
         cols = span(n, TILE)
-        out[:, cols] = product(tok_t[...], grad_queries[:, cols]).astype(BF16)
+        total[:, cols] = product(tok_t[...], grad_queries[:, cols]).astype(BF16)
 
     @pl.loop(0, 2 * width // TILE)
     def _(n):
-        out[:, span(n + width // TILE, TILE)] = product(xext_t[...], grad_pairs[:, span(n, TILE)]).astype(BF16)
-
-
-def token_grad_kernel(nbuf, order, grad_resid, grad_queries, grad_pairs, low, high, *refs):
-    stacks = refs[:nbuf]
-    out, weights, own, sem = refs[nbuf:]
+        total[:, span(n + width // TILE, TILE)] = product(xext_t[...], grad_pairs[:, span(n, TILE)]).astype(BF16)
+
+    copies += emit(order, total, pl.ds(0, 3 * width), block, targets, 0, sem)
+    settle(copies)
+
+
+def token_grad_kernel(table, order, grad_resid, grad_queries, grad_pairs, low, high, *refs):
+    stacks = refs[:-4]
+    out, weights, own, sem = refs[-4:]
     width = grad_resid.shape[1]
     seqs = grad_resid.shape[0] // WINDOW
-    copies = fetch(order, stacks, pl.ds(0, 3 * width), weights, stacks[0].shape[1], sem)
+    copies = fetch_all(order, stacks, table, 3 * width // 2, weights, sem)
     for s in range(seqs):
         own[s * WINDOW : (s + 1) * WINDOW, :width] = grad_queries[s * WINDOW : (s + 1) * WINDOW, :]
         own[s * WINDOW : (s + 1) * WINDOW, width:] = grad_pairs[s * WIDE + HALF : s * WIDE + HALF + WINDOW, :]
@@ -519,14 +645,271 @@
     return jax.ShapeDtypeStruct(dims, dtype)
 
 
-def gathered(block):
-    rows = block.shape[0] * lax.axis_size("shard") // SLOTS
-    full = lax.all_gather(block, "shard", axis=0, tiled=True)
-    return [full.reshape(SLOTS, rows, block.shape[1])]
-
-
-def scattered(whole):
-    return lax.psum_scatter(whole, "shard", scatter_dimension=0, tiled=True)
+def turn(block, step):
+    return lax.ppermute(block, "shard", [(i, (i - 4 * step) % SLOTS) for i in range(SLOTS)])
+
+
+def flip(block):
+    return lax.ppermute(block, "shard", [(i, i ^ 2) for i in range(SLOTS)])
+
+
+def other(block):
+    return lax.ppermute(block, "rep", [(0, 1), (1, 0)])
+
+
+def after(value, *others):
+    if not direct():
+        return value
+    return lax.optimization_barrier((value,) + others)[0]
+
+
+def anchor_kernel(source, out):
+    del source, out
+
+
+def anchor(value):
+    return pl.pallas_call(
+        anchor_kernel,
+        out_shape=jax.ShapeDtypeStruct(value.shape, value.dtype),
+        in_specs=[any_spec()],
+        out_specs=any_spec(),
+        input_output_aliases={0: 0},
+        compiler_params=params(),
+        cost_estimate=cost(2000),
+        name="anchor",
+    )(value)
+
+
+def direct():
+    return lax.axis_size("shard") == SLOTS and lax.axis_size("rep") == 2
+
+
+def block_order():
+    if not direct():
+        return jnp.arange(SLOTS + 1, dtype=jnp.int32) % SLOTS
+    me = lax.axis_index("shard")
+    k = jnp.arange(SLOTS, dtype=jnp.int32)
+    places = ((me // 4 + k // 4) % 4) * 4 + jnp.bitwise_xor(me % 4, k % 4)
+    return jnp.concatenate([places, lax.axis_index("rep")[None]]).astype(jnp.int32)
+
+
+class Gather:
+    def __init__(self, block, mine=None, rest=None):
+        self.block, self.mine, self.rest = block, mine, rest
+
+    def turn(self, *gate):
+        own = self.block if self.mine is None else self.mine
+        own = after(own, *gate)
+        self.along = jnp.stack([own] + [turn(own, step) for step in (1, 2, 3)])
+        return self.along
+
+    def cross(self, *gate):
+        self.across = flip(after(self.along, *gate))
+        return self.across
+
+    def rep(self, *gate):
+        self.first = jnp.concatenate([self.along, self.across], axis=0)
+        self.second = other(after(self.first, *gate))
+        return self.second
+
+    def cores(self, *gate):
+        if self.mine is None:
+            stacks = [self.along, self.across]
+            stacks = stacks + [swap(after(stack, *gate)) for stack in stacks]
+            table = [((2 * (k % 2) + k // 2 % 2, k // 4, 0),) for k in range(SLOTS)]
+        else:
+            stacks = [self.first, self.second]
+            stacks = stacks + [swap(after(stack, *gate)) for stack in stacks]
+            table = []
+            for k in range(SLOTS):
+                part = k // 2 % 2 * 4 + k // 4
+                table.append(((2 * (k % 2), part, 0), (2 * (k % 2) + 1, part, 0)))
+        return stacks, tuple(table)
+
+
+def plain_gather(block, extra=None):
+    rows, width = block.shape
+    half = width // 2
+    rows = rows * lax.axis_size("shard") // SLOTS
+    mine, rest = block[:, :half], block[:, half:]
+    both = jnp.concatenate([mine] + ([] if extra is None else [extra]) + [rest], axis=1)
+    full = lax.all_gather(both, "shard", axis=0, tiled=True)
+    table = tuple(((0, k, 0), (0, k, both.shape[1] - half)) for k in range(SLOTS))
+    return [full.reshape(SLOTS, rows, both.shape[1])], table
+
+
+def pack_kernel(order, query, key, value, pooled, out, inner, outer, tokens, taps, *refs):
+    vectors, bias = refs[:6], refs[6]
+    lead, lead_rest, mid, mid_rest, bulk, low, high, joined, small = refs[7:]
+    part, width = query.shape
+    half = 3 * width // 2
+    for k, source in enumerate((query, key, value)):
+        joined[:, k * width : (k + 1) * width] = source[...]
+    mine, rest = order[SLOTS], 1 - order[SLOTS]
+    small[...] = jnp.zeros_like(small)
+    for k, source in enumerate(vectors):
+        small[k : k + 1, :part] = source[...].astype(F32)
+    for t in range(KERNEL):
+        small[tap_row(t, 0) : tap_row(t, 0) + 2, :part] = taps[t].astype(F32)
+    small[BIAS_ROW:SMALL, :part] = bias[...].astype(F32)
+    lead[:, :half] = joined[:, span(mine, half)]
+    lead[:, half:] = small[...].T[:part].astype(BF16)
+    lead_rest[...] = joined[:, span(rest, half)]
+    first = mine == 0
+    mid[...] = jnp.where(first, pooled[...], out[...])
+    mid_rest[...] = jnp.where(first, out[...], pooled[...])
+    folds = inner.shape[1] // width
+    for m in range(folds):
+        bulk[m * part : (m + 1) * part, :] = inner[:, m * width : (m + 1) * width]
+    bulk[folds * part :, :] = outer[...]
+    high[...] = tokens[:, :HALF, :]
+    low[...] = tokens[:, tokens.shape[1] - HALF :, :]
+
+
+def split_kernel(wide, order, keep, arrived, a_keep, a_send, b_keep, b_send):
+    half = wide // 2
+    mine = span(order[SLOTS], half)
+    rest = span(1 - order[SLOTS], half)
+    for across in range(2):
+        a_keep[across, 0] = keep[across, 0, :, mine] + arrived[across, 0, :, mine]
+        a_send[across, 0] = keep[across, 0, :, rest] + arrived[across, 0, :, rest]
+        target = b_send if across else b_keep
+        target[0] = keep[across, 0, :, wide:] + arrived[across, 0, :, wide:]
+
+
+def fold_kernel(keep, arrived, x_keep, x_send):
+    x_keep[0] = keep[0, 0] + arrived[0, 0]
+    x_send[0] = keep[1, 0] + arrived[1, 0]
+
+
+def join_kernel(x_keep, x_arrived, b_keep, b_arrived, *parts):
+    half = x_keep.shape[2]
+    for k, part in enumerate(parts):
+        part[:, :half] = x_keep[k] + x_arrived[k]
+        part[:, half:] = b_keep[k] + b_arrived[k]
+
+
+def gather_sum_kernel(own, first, second, third, out):
+    total = own[...].astype(F32) + first[...].astype(F32) + second[...].astype(F32) + third[...].astype(F32)
+    out[...] = total.astype(BF16)
+
+
+def final_kernel(wide, pieces, order, own, arrived, *refs):
+    outs, total = refs[:-1], refs[-1]
+    half = wide // 2
+    total[:, span(order[SLOTS], half)] = own[:, :half].astype(F32)
+    total[:, span(1 - order[SLOTS], half)] = arrived[:, :half].astype(F32)
+    total[:, wide:] = own[:, half:].astype(F32) + arrived[:, half:].astype(F32)
+    for (start, size), out in zip(pieces, outs):
+        out[...] = total[:, start : start + size]
+
+
+class Scatter:
+    def __init__(self, keep, give, order, wide, pieces):
+        self.order, self.wide, self.pieces = order, wide, pieces
+        self.rows, self.columns = keep.shape[2:]
+        self.keep, self.give = keep, give
+        if direct():
+            self.arrived = swap(give)
+
+    def split(self):
+        rows, half, rest = self.rows, self.wide // 2, self.columns - self.wide
+        four = pl.BlockSpec((2, 1, rows, self.columns), lambda z: (0, z, 0, 0))
+        a_block = pl.BlockSpec((2, 1, rows, half), lambda z: (0, z, 0, 0))
+        b_block = pl.BlockSpec((1, rows, rest), lambda z: (z, 0, 0))
+        a_shape, b_shape = shape_of(2, 4, rows, half), shape_of(4, rows, rest)
+        self.a_keep, a_send, self.b_keep, b_send = pl.pallas_call(
+            functools.partial(split_kernel, self.wide),
+            grid=(4,),
+            out_shape=(a_shape, a_shape, b_shape, b_shape),
+            in_specs=[smem_spec(), four, four],
+            out_specs=(a_block, a_block, b_block, b_block),
+            compiler_params=params(),
+            cost_estimate=cost(5),
+            name="split",
+        )(self.order, self.keep, self.arrived)
+        self.a_arrived = other(a_send)
+        self.b_arrived = flip(b_send)
+        return a_send
+
+    def fold(self):
+        rows, half = self.rows, self.wide // 2
+        a_block = pl.BlockSpec((2, 1, rows, half), lambda z: (0, z, 0, 0))
+        x_block = pl.BlockSpec((1, rows, half), lambda z: (z, 0, 0))
+        x_shape = shape_of(4, rows, half)
+        self.x_keep, x_send = pl.pallas_call(
+            fold_kernel,
+            grid=(4,),
+            out_shape=(x_shape, x_shape),
+            in_specs=[a_block, a_block],
+            out_specs=(x_block, x_block),
+            compiler_params=params(),
+            cost_estimate=cost(4),
+            name="fold",
+        )(self.a_keep, self.a_arrived)
+        self.x_arrived = flip(x_send)
+        return x_send
+
+    def join(self):
+        shape = shape_of(self.rows, self.columns - self.wide // 2)
+        parts = pl.pallas_call(
+            join_kernel,
+            out_shape=(shape,) * 4,
+            in_specs=[vmem_spec()] * 4,
+            out_specs=(vmem_spec(),) * 4,
+            compiler_params=params(),
+            cost_estimate=cost(3),
+            name="join",
+        )(self.x_keep, self.x_arrived, self.b_keep, self.b_arrived)
+        self.turned = [parts[0]] + [turn(parts[step], -step) for step in (1, 2, 3)]
+        return parts[1]
+
+    def gather(self):
+        self.own = pl.pallas_call(
+            gather_sum_kernel,
+            out_shape=shape_of(self.rows, self.columns - self.wide // 2),
+            in_specs=[vmem_spec()] * 4,
+            out_specs=vmem_spec(),
+            compiler_params=params(),
+            cost_estimate=cost(2),
+            name="gather_sum",
+        )(*self.turned)
+        self.last = other(self.own)
+        return self.own
+
+    def final(self):
+        return pl.pallas_call(
+            functools.partial(final_kernel, self.wide, self.pieces),
+            out_shape=tuple(shape_of(self.rows, size, dtype=F32) for _, size in self.pieces),
+            in_specs=[smem_spec(), vmem_spec(), vmem_spec()],
+            out_specs=(vmem_spec(),) * len(self.pieces),
+            scratch_shapes=[pltpu.VMEM((self.rows, self.columns), F32)],
+            compiler_params=params(),
+            cost_estimate=cost(2),
+            name="final",
+        )(self.order, self.own, self.last)
+
+
+def bulk_final_kernel(own, arrived, inner, outer, small):
+    part, hidden = inner.shape
+    width = own.shape[1]
+    total = own[...].astype(F32) + arrived[...].astype(F32)
+    folds = hidden // width
+    for m in range(folds):
+        inner[:, m * width : (m + 1) * width] = total[m * part : (m + 1) * part]
+    outer[...] = total[folds * part : 2 * folds * part]
+    small[...] = total[2 * folds * part :]
+
+
+def plain_total(whole):
+    return rep_total(lax.psum_scatter(whole, "shard", scatter_dimension=0, tiled=True))
+
+
+def plain_scatter(blocks, parts):
+    keep, give = blocks
+    full = jnp.stack([keep, give]).transpose(2, 1, 0, 3, 4).reshape(SLOTS, keep.shape[2], keep.shape[3])
+    width = SLOTS * keep.shape[2]
+    return [plain_total(full[:, :, start:stop].reshape(width, -1)) for start, stop in parts]
 
 
 def rep_total(piece):
@@ -588,30 +971,69 @@
 
     tok = tokens.reshape(rows, width)
     cot = cotangent.reshape(rows, width)
-    tok_low = shift(tokens[:, tok_span - HALF :], 1).reshape(seqs * HALF, width)
-    tok_high = shift(tokens[:, :HALF], -1).reshape(seqs * HALF, width)
-
     vectors = [output_bias, first_gain, first_shift, outer_bias, second_gain, second_shift]
     part = width // device_count
-    small = jnp.concatenate(vectors + [inner_bias, conv_taps.reshape(-1)])
-    lanes = 128 * -(-small.shape[0] // (part * 128))
-    small = jnp.pad(small, (0, part * lanes - small.shape[0])).reshape(part, lanes)
-    lead = gathered(jnp.concatenate([query_proj, key_proj, value_proj, small], axis=1))
-    mid = gathered(jnp.concatenate([pooled_query, output_proj], axis=1))
-    up = gathered(inner_proj)
-    down = gathered(outer_proj)
-    order = jnp.arange(SLOTS, dtype=jnp.int32)
-
-    small_full = jnp.concatenate([stack[:, :, 3 * width :] for stack in lead], axis=0)
-    small_full = small_full.reshape(device_count, part * lanes).astype(F32)
-    vecs = jnp.stack([small_full[:, k * part : (k + 1) * part].reshape(width) for k in range(6)])
-    vecs = jnp.pad(vecs, ((0, 2), (0, 0)))
-    at = 6 * part
-    bias_in = small_full[:, at : at + hidden // device_count].reshape(1, hidden)
-    at = at + hidden // device_count
-    taps = small_full[:, at : at + 2 * KERNEL * part].reshape(device_count, KERNEL, 2, part)
-    taps = taps.transpose(1, 2, 0, 3).reshape(KERNEL, 2 * width)
-    taps = jnp.pad(taps, ((0, 8 - KERNEL), (0, 0)))
+    block = width // SLOTS
+    order = block_order()
+    if direct():
+        packed = pl.pallas_call(
+            pack_kernel,
+            out_shape=(
+                shape_of(part, 3 * width // 2 + 128),
+                shape_of(part, 3 * width // 2),
+                shape_of(part, width),
+                shape_of(part, width),
+                shape_of(2 * hidden // width * part, width),
+                shape_of(seqs, HALF, width),
+                shape_of(seqs, HALF, width),
+            ),
+            in_specs=[smem_spec()] + [vmem_spec()] * 16,
+            out_specs=(vmem_spec(),) * 7,
+            scratch_shapes=[pltpu.VMEM((part, 3 * width), BF16), pltpu.VMEM((128, 128), F32)],
+            compiler_params=params(),
+            cost_estimate=cost(3),
+            name="pack",
+        )(
+            order,
+            query_proj,
+            key_proj,
+            value_proj,
+            pooled_query,
+            output_proj,
+            inner_proj,
+            outer_proj,
+            tokens,
+            conv_taps,
+            *[vector.reshape(1, part) for vector in vectors],
+            inner_bias.reshape(4, part),
+        )
+        lead, mid = (Gather(None, packed[k], packed[k + 1]) for k in (0, 2))
+        tick = jnp.zeros((8, 128), F32)
+        tick = anchor(after(tick, packed[0]))
+        lead.turn()
+        bulk = lax.all_gather(after(packed[4], lead.along), "shard", axis=0, tiled=True)
+        tick = anchor(after(tick, lead.along))
+        lead.cross(tick)
+        tick = anchor(after(tick, lead.across))
+        lead.rep()
+        tok_low = shift(after(packed[5], tick), 1).reshape(seqs * HALF, width)
+        tok_high = shift(after(packed[6], tick), -1).reshape(seqs * HALF, width)
+        mid.turn(tick)
+        tick = anchor(after(tick, lead.second, mid.along))
+        lead, lead_table = lead.cores(tick)
+        mid.cross(tick)
+    else:
+        tok_low = shift(tokens[:, tok_span - HALF :], 1).reshape(seqs * HALF, width)
+        tok_high = shift(tokens[:, :HALF], -1).reshape(seqs * HALF, width)
+        small = jnp.concatenate(vectors + [conv_taps.reshape(-1), inner_bias]).reshape(SMALL, part).T
+        small = jnp.pad(small, ((0, 0), (0, 128 - SMALL)))
+        lead, lead_table = plain_gather(jnp.concatenate([query_proj, key_proj, value_proj], axis=1), small)
+        mid, mid_table = plain_gather(jnp.concatenate([pooled_query, output_proj], axis=1))
+        full = lax.all_gather(inner_proj, "shard", axis=0, tiled=True)
+        full = full.reshape(SLOTS, block, hidden // width, width).transpose(0, 2, 1, 3)
+        full = full.reshape(SLOTS, hidden // SLOTS, width)
+        down = lax.all_gather(outer_proj, "shard", axis=0, tiled=True)
+        bulk = jnp.concatenate([full, down.reshape(SLOTS, hidden // SLOTS, width)], axis=1).reshape(-1, width)
 
     row = jnp.arange(tok_span, dtype=jnp.int32)[:, None]
     lane = jnp.arange(WINDOW, dtype=jnp.int32)[None, :]
@@ -631,21 +1053,31 @@
     )
 
     n_lead = len(lead)
-    xext, queries, pairs, pooled = pl.pallas_call(
-        functools.partial(project_kernel, n_lead),
+    xext, queries, pairs, pooled, vecs = pl.pallas_call(
+        functools.partial(project_kernel, lead_table),
         out_shape=(
             shape_of(seqs * WIDE, width),
             shape_of(rows, width),
             shape_of(seqs * WIDE, 2 * width),
             shape_of(seqs * pools, 2 * width),
+            shape_of(24, width, dtype=F32),
         ),
-        in_specs=[smem_spec()] + [vmem_spec()] * 4 + [any_spec()] * n_lead,
-        out_specs=(vmem_spec(),) * 4,
-        scratch_shapes=[pltpu.VMEM((width, 3 * width), BF16), pltpu.SemaphoreType.DMA],
+        in_specs=[smem_spec()] + [vmem_spec()] * 3 + [any_spec()] * n_lead,
+        out_specs=(vmem_spec(),) * 5,
+        scratch_shapes=[
+            pltpu.VMEM((width, 3 * width), BF16),
+            pltpu.VMEM((width, 128), BF16),
+            pltpu.SemaphoreType.DMA,
+        ],
         compiler_params=params(),
+        cost_estimate=cost(15),
         name="project",
-    )(order, tok, tok_low, tok_high, taps, *lead)
-
+    )(order, tok, tok_low, tok_high, *lead)
+    bias_in = vecs[BIAS_ROW:SMALL].reshape(4, device_count, part).transpose(1, 0, 2).reshape(1, hidden)
+
+    if direct():
+        mid.rep(pooled)
+        mid, mid_table = mid.cores()
     pool_away = swap(pooled)
     pool_far = hop(pooled, True)
     pool_near = hop(pooled, False)
@@ -668,13 +1100,14 @@
         in_specs=[seq_block(tok_span, width), seq_block(WIDE, 2 * width), bias_block],
         out_specs=(seq_block(tok_span, width), prob_block),
         compiler_params=params(),
+        cost_estimate=cost(10),
         name="window",
     )(queries, pairs, bias_one)
 
     n_mid = len(mid)
     pool_specs = [seq_block(pools, 2 * width)] * 5
     second, mixed, probs_two = pl.pallas_call(
-        functools.partial(pooled_kernel, n_mid),
+        functools.partial(pooled_kernel, mid_table),
         grid=(seqs,),
         out_shape=(shape_of(rows, width), shape_of(rows, width), prob_shape),
         in_specs=[smem_spec(), smem_spec(), whole_block(rows, width), bias_block]
@@ -687,23 +1120,22 @@
             pltpu.SemaphoreType.DMA,
         ],
         compiler_params=params(),
+        cost_estimate=cost(14),
         name="pooled",
     )(order, places, attended, bias_two, *pool_blocks, *mid)
 
-    counts = (len(mid), len(up), len(down))
-    result, grad_resid, grad_attn, grad_in, grad_down, vec_grads, bias_grad = pl.pallas_call(
-        functools.partial(feed_kernel, counts),
+    each = 2 * hidden // SLOTS + SMALL_ROWS
+    result, grad_resid, grad_attn, grad_bulk, _ = pl.pallas_call(
+        functools.partial(feed_kernel, mid_table),
         out_shape=(
             shape_of(rows, width),
             shape_of(rows, width, dtype=F32),
             shape_of(rows, width),
-            shape_of(width, hidden),
-            shape_of(hidden, width),
+            shape_of(SLOTS * each, width),
             shape_of(8, width, dtype=F32),
-            shape_of(1, hidden, dtype=F32),
         ),
-        in_specs=[smem_spec()] + [vmem_spec()] * 5 + [any_spec()] * sum(counts),
-        out_specs=(vmem_spec(),) * 7,
+        in_specs=[smem_spec()] + [vmem_spec()] * 5 + [any_spec()] * (1 + n_mid),
+        out_specs=(vmem_spec(),) * 3 + (any_spec(), vmem_spec()),
         scratch_shapes=[
             pltpu.VMEM((width, width), BF16),
             pltpu.VMEM((width, hidden), BF16),
@@ -716,17 +1148,22 @@
             pltpu.VMEM((rows, hidden), BF16),
             pltpu.VMEM((rows, width), F32),
             pltpu.VMEM((rows, width), BF16),
-            pltpu.SemaphoreType.DMA((3,)),
+            pltpu.VMEM((width, hidden), BF16),
+            pltpu.VMEM((hidden, width), BF16),
+            pltpu.VMEM((1, hidden), F32),
+            pltpu.VMEM((SLOTS, SMALL_ROWS, width), BF16),
+            pltpu.SemaphoreType.DMA((4,)),
         ],
         compiler_params=params(),
+        cost_estimate=cost(45),
         name="feed",
-    )(order, tok, mixed, cot, vecs, bias_in, *mid, *up, *down)
-    own_down = scattered(grad_down)
-    own_in = scattered(grad_in)
+    )(order, tok, mixed, cot, vecs, bias_in, bulk, *mid)
+    if direct():
+        own_bulk = lax.psum_scatter(grad_bulk, "shard", scatter_dimension=0, tiled=True)
 
     back_shape = shape_of(seqs * pools, 2 * width)
     grad_mixed, grad_second, grad_out, pg_own, pg_away, pg_near, pg_far = pl.pallas_call(
-        functools.partial(pooled_back_kernel, n_mid),
+        functools.partial(pooled_back_kernel, mid_table),
         grid=(seqs,),
         out_shape=(
             shape_of(rows, width, dtype=F32),
@@ -764,6 +1201,7 @@
             pltpu.SemaphoreType.DMA,
         ],
         compiler_params=params(),
+        cost_estimate=cost(22),
         name="pooled_back",
     )(order, places, grad_attn, mixed, second, probs_two, *pool_blocks, *mid)
 
@@ -773,7 +1211,7 @@
     back_near = lax.ppermute(pg_near, "shard", back_route(device_count, False))
 
     grad_queries, grad_pairs, grad_pooled = pl.pallas_call(
-        functools.partial(window_back_kernel, n_mid),
+        functools.partial(window_back_kernel, mid_table),
         grid=(seqs,),
         out_shape=(shape_of(rows, width), shape_of(seqs * WIDE, 2 * width), shape_of(width, width)),
         in_specs=[
@@ -793,58 +1231,56 @@
             pltpu.SemaphoreType.DMA,
         ],
         compiler_params=params(),
+        cost_estimate=cost(22),
         name="window_back",
     )(order, grad_mixed, grad_second, attended, queries, pairs, probs_one, *mid)
 
     pair_total, tap_grads, edges = pl.pallas_call(
-        functools.partial(conv_back_kernel, n_lead),
+        functools.partial(conv_back_kernel, lead_table),
         out_shape=(
             shape_of(seqs * WIDE, 2 * width),
-            shape_of(8, 2 * width, dtype=F32),
+            shape_of(16, width, dtype=F32),
             shape_of(2 * seqs * HALF, width),
         ),
         in_specs=[smem_spec()] + [vmem_spec()] * 7 + [any_spec()] * n_lead,
         out_specs=(vmem_spec(),) * 3,
         scratch_shapes=[
-            pltpu.VMEM((width, 2 * width), BF16),
+            pltpu.VMEM((width, 3 * width), BF16),
             pltpu.VMEM((2 * seqs * HALF, 2 * width), BF16),
             pltpu.SemaphoreType.DMA,
         ],
         compiler_params=params(),
+        cost_estimate=cost(12),
         name="conv_back",
-    )(order, pg_own, pg_cross[0], back_near, back_far, taps, pairs, grad_pairs, *lead)
+    )(order, pg_own, pg_cross[0], back_near, back_far, vecs, pairs, grad_pairs, *lead)
 
     edge_high = shift(edges[: seqs * HALF], -1)
     edge_low = shift(edges[seqs * HALF :], 1)
 
-    grad_lead = pl.pallas_call(
+    lead_shape = shape_of(2, 4, block, 5 * width + 128)
+    lead_keep, lead_give = pl.pallas_call(
         weight_grad_kernel,
-        out_shape=shape_of(width, 3 * width),
-        in_specs=[vmem_spec()] * 4,
-        out_specs=vmem_spec(),
-        scratch_shapes=[pltpu.VMEM((width, rows), BF16), pltpu.VMEM((width, seqs * WIDE), BF16)],
+        out_shape=(lead_shape, lead_shape),
+        in_specs=[smem_spec()] + [vmem_spec()] * 7,
+        out_specs=(any_spec(),) * 2,
+        scratch_shapes=[
+            pltpu.VMEM((width, rows), BF16),
+            pltpu.VMEM((width, seqs * WIDE), BF16),
+            pltpu.VMEM((width, 3 * width), BF16),
+            pltpu.VMEM((width, 128), BF16),
+            pltpu.SemaphoreType.DMA,
+        ],
         compiler_params=params(),
+        cost_estimate=cost(14),
         name="weight_grad",
-    )(tok, xext, grad_queries, pair_total)
-
-    small_grads = jnp.concatenate(
-        [vec_grads[k].reshape(device_count, part) for k in range(6)]
-        + [
-            bias_grad.reshape(device_count, hidden // device_count),
-            tap_grads[:KERNEL]
-            .reshape(KERNEL, 2, device_count, part)
-            .transpose(2, 0, 1, 3)
-            .reshape(device_count, 2 * KERNEL * part),
-        ],
-        axis=1,
-    )
-    small_grads = jnp.pad(small_grads, ((0, 0), (0, part * lanes - small_grads.shape[1])))
-    small_grads = small_grads.reshape(width, lanes).astype(BF16)
-    own_mid = scattered(jnp.concatenate([grad_pooled, grad_out], axis=1))
-    own_lead = scattered(jnp.concatenate([grad_lead, small_grads], axis=1))
+    )(order, tok, xext, grad_queries, pair_total, tap_grads, grad_pooled, grad_out)
+    pieces = tuple((k * width, width) for k in range(5)) + ((5 * width, 128),)
+    lead_sum = Scatter(lead_keep, lead_give, order, 14 * 128, pieces)
+    if direct():
+        grad_resid = after(grad_resid, lead_sum.split())
 
     tokens_grad = pl.pallas_call(
-        functools.partial(token_grad_kernel, n_lead),
+        functools.partial(token_grad_kernel, lead_table),
         out_shape=shape_of(rows, width, dtype=F32),
         in_specs=[smem_spec()] + [vmem_spec()] * 5 + [any_spec()] * n_lead,
         out_specs=vmem_spec(),
@@ -854,27 +1290,52 @@
             pltpu.SemaphoreType.DMA,
         ],
         compiler_params=params(),
+        cost_estimate=cost(11),
         name="token_grad",
     )(order, grad_resid, grad_queries, pair_total, edge_low, edge_high, *lead)
 
-    own_down = rep_total(own_down)
-    own_in = rep_total(own_in)
-    own_mid = rep_total(own_mid)
-    own_lead = rep_total(own_lead)
-    small_own = own_lead[:, 3 * width :].reshape(-1)
-    vec_own = [small_own[k * part : (k + 1) * part] for k in range(6)]
-    at = 6 * part
-    bias_own = small_own[at : at + hidden // device_count]
-    at = at + hidden // device_count
-    taps_own = small_own[at : at + 2 * KERNEL * part].reshape(KERNEL, 2, part)
+    folds = hidden // width
+    if direct():
+        lead_sum.fold()
+        lead_sum.join()
+        lead_sum.gather()
+        own_in, own_down, small_own = pl.pallas_call(
+            bulk_final_kernel,
+            out_shape=(
+                shape_of(part, hidden, dtype=F32),
+                shape_of(folds * part, width, dtype=F32),
+                shape_of(SMALL_ROWS, width, dtype=F32),
+            ),
+            in_specs=[vmem_spec()] * 2,
+            out_specs=(vmem_spec(),) * 3,
+            compiler_params=params(),
+            cost_estimate=cost(2),
+            name="bulk_final",
+        )(own_bulk, other(own_bulk))
+        vec_own = [small_own[k, :part] for k in range(6)]
+        bias_own = small_own[8, : folds * part]
+        own_query, own_keys, own_values, own_pooled, own_out, taps_own = lead_sum.final()
+    else:
+        whole = grad_bulk.reshape(SLOTS, each, width)
+        inner_part = whole[:, : folds * block].reshape(SLOTS, folds, block, width).transpose(0, 2, 1, 3)
+        own_in = plain_total(inner_part.reshape(width, hidden))
+        own_down = plain_total(whole[:, folds * block : 2 * folds * block].reshape(hidden, width))
+        small = whole[:, 2 * folds * block :]
+        vec_own = [plain_total(small[:, k, :block].reshape(width)) for k in range(6)]
+        bias_own = plain_total(small[:, 8, : folds * block].reshape(hidden))
+        parts = [(k * width, (k + 1) * width) for k in range(5)] + [(5 * width, None)]
+        own_query, own_keys, own_values, own_pooled, own_out, taps_own = plain_scatter(
+            (lead_keep, lead_give), parts
+        )
+    taps_own = taps_own.T[: 2 * KERNEL].reshape(KERNEL, 2, part)
     return (
         result.reshape(tokens.shape),
         tokens_grad.reshape(tokens.shape),
-        own_lead[:, :width],
-        own_lead[:, width : 2 * width],
-        own_lead[:, 2 * width : 3 * width],
-        own_mid[:, :width],
-        own_mid[:, width:],
+        own_query,
+        own_keys,
+        own_values,
+        own_pooled,
+        own_out,
         taps_own,
         vec_own[0],
         vec_own[1],

time: 644 us -> 418 us (0.65)
  waiting for transfers between devices: 379 us -> 105 us
  starting transfers between devices: 41.8 us -> 83.2 us
  Pallas kernels: 167 us -> 186 us
  other arithmetic: 17.9 us -> 4.62 us
    reduce_scatter x4 -> x1, waiting for transfers between devices: 204 us -> 0.02 us  [shards(): lax.psum_scatter(grad_bulk, 'shard', scatter_dimension=0, tiled=True)]
    all_gather x4 -> x1, waiting for transfers between devices: 133 us -> 0.02 us  [shards(): lax.all_gather(after(packed[4], lead.along), 'shard', axis=0, tiled=True)]
    ppermute x4 -> x18, waiting for transfers between devices: 3.3 us -> 89.4 us  [the longest x4 37.4 us: flip(): return lax.ppermute(block, 'shard', [(i, i ^ 2) for i in range(SLOTS)])]
    ppermute x4 -> x18, starting transfers between devices: 5.67 us -> 39.5 us  [the longest x9 22 us: turn(): lax.ppermute(block, 'shard', [(i, (i - 4 * step) % SLOTS) for i in range(...]
    ppermute x1, starting transfers between devices: 3.71 us -> 23.6 us  [shards(): back_near = lax.ppermute(pg_near, 'shard', back_route(device_count, False))]
    pallas_call x8 -> x15, Pallas kernels: 157 us -> 175 us  [the longest x1 44.9 us: shards(): pl.pallas_call(functools.partial(feed_kernel, mid_table), out_shape=(shap...]
    ppermute x3 -> x8, starting transfers between devices: 16.4 us -> 3.09 us  [swap(): lax.ppermute(block, 'shard', [(i, i ^ 1) for i in range(lax.axis_size('sh...]
    ppermute x2, waiting for transfers between devices: 9.86 us -> 0.01 us  [hop(): lax.ppermute(block, 'shard', [(i, j) for i, j in route if 0 <= j < count])]
  transfers between devices with their start and end apart: 23 -> 36, of which waited for: 12 -> 16; matrix products, arithmetic and copies ran while one was open for 3% -> 3% of each run, Pallas kernels for 12% -> 33%
where the time goes in v2:
time: 418 us; the launch traced here: 417 us
  Pallas kernels  186 us (44%)
  waiting for transfers between devices  105 us (25%)
  starting transfers between devices  83.2 us (20%)
  local copies, waits for them, and re-layouts  23.5 us (6%)
  between operations  14.6 us (3%)
  other arithmetic  4.62 us (1%)
    pallas_call x1, Pallas kernels, shards(): pl.pallas_call(functools.partial(feed_kernel, mid_table), out_shape=(shap...  44.9 us
    ppermute x4, waiting for transfers between devices, flip(): return lax.ppermute(block, 'shard', [(i, i ^ 2) for i in range(SLOTS)])  37.4 us
    ppermute x9, waiting for transfers between devices, turn(): lax.ppermute(block, 'shard', [(i, (i - 4 * step) % SLOTS) for i in range(...  32.4 us
    ppermute x1, starting transfers between devices, shards(): back_near = lax.ppermute(pg_near, 'shard', back_route(device_count, False))  23.6 us
    pallas_call x1, Pallas kernels, shards(): pl.pallas_call(functools.partial(window_back_kernel, mid_table), grid=(se...  22.7 us
    pallas_call x1, Pallas kernels, shards(): pl.pallas_call(functools.partial(pooled_back_kernel, mid_table), grid=(se...  22.3 us
    ppermute x9, starting transfers between devices, turn(): lax.ppermute(block, 'shard', [(i, (i - 4 * step) % SLOTS) for i in range(...  22 us
    ppermute x5, waiting for transfers between devices, other(): return lax.ppermute(block, 'rep', [(0, 1), (1, 0)])  19.5 us
  transfers between devices with their start and end apart: 36, of which 16 were waited for; matrix products, arithmetic and copies ran while one was open for 3% of the time, Pallas kernels for 33%

profile of v2, /device:TPU:0, one launch (start us, length us, event | category | flops | bytes accessed | tf_op | source)
XLA Modules:
  0.0 416.8 jit_solution(3601281186179410323)
XLA Ops:
  9.2 3.0 pack.1
  12.1 3.0 collective-permute-start.2
  15.1 2.6 collective-permute-start.1
  20.0 1.6 collective-permute-done.2
  21.6 4.4 %collective-permute-done.1 = bf16[48,1280]{1,0:T(8,128)(2,1)S(1)} collective-permute-done((bf16[48,1280]{1,0:T(8,128)(2,1)}, bf16[48,1280]{1,0:T(8,128)(2,1)S(1)}, u32[]{:S(2)}, u32[]{:S(2)}) %collective-permute-start.1) | collective-permute-done | bytes 122912 | tf_op jit(solution)/shard_map/ppermute | solution.py:649
  27.1 1.6 collective-permute-start.3
  28.7 13.0 %collective-permute-done.3 = bf16[4,48,1280]{2,1,0:T(8,128)(2,1)S(1)} collective-permute-done((bf16[4,48,1280]{2,1,0:T(8,128)(2,1)S(1)}, bf16[4,48,1280]{2,1,0:T(8,128)(2,1)S(1)}, u32[]{:S(2)}, u32[]{:S(2)}) %collective-permute-start.3) | collective-permute-done | bytes 491552 | tf_op jit(solution)/shard_map/ppermute | solution.py:653
  43.1 4.9 %collective-permute-start.9 = (bf16[48,768]{1,0:T(8,128)(2,1)S(1)}, bf16[48,768]{1,0:T(8,128)(2,1)S(1)}, u32[]{:S(2)}, u32[]{:S(2)}) collective-permute-start(bf16[48,768]{1,0:T(8,128)(2,1)S(1)} %copy-done.22), channel_id=1, source_target_pairs={{0,4},{1,5},{2,6},{3,7},{4,8},{5,9},{6,10},{7,11},{8,12},{9,13},{1... | collective-permute-start | bytes 221192 | tf_op jit(solution)/shard_map/ppermute | solution.py:649
  48.0 2.4 collective-permute-start.7
  53.5 4.5 %collective-permute-done.8 = bf16[48,768]{1,0:T(8,128)(2,1)S(1)} collective-permute-done((bf16[48,768]{1,0:T(8,128)(2,1)S(1)}, bf16[48,768]{1,0:T(8,128)(2,1)S(1)}, u32[]{:S(2)}, u32[]{:S(2)}) %collective-permute-start.8) | collective-permute-done | bytes 73760 | tf_op jit(solution)/shard_map/ppermute | solution.py:649
  58.1 5.0 %collective-permute-done.6.refs_1_ = bf16[8,48,1280]{2,1,0:T(8,128)(2,1)S(1)} collective-permute-done((bf16[8,48,1280]{2,1,0:T(8,128)(2,1)S(1)}, bf16[8,48,1280]{2,1,0:T(8,128)(2,1)S(1)}, u32[]{:S(2)}, u32[]{:S(2)}) %collective-permute-start.6) | collective-permute-done | bytes 983072 | tf_op jit(solution)/shard_map/ppermute | solution.py:657
  63.6 2.0 collective-permute-start.16
  65.6 11.9 %collective-permute-done.16 = bf16[4,48,768]{2,1,0:T(8,128)(2,1)S(1)} collective-permute-done((bf16[4,48,768]{2,1,0:T(8,128)(2,1)S(1)}, bf16[4,48,768]{2,1,0:T(8,128)(2,1)S(1)}, u32[]{:S(2)}, u32[]{:S(2)}) %collective-permute-start.16) | collective-permute-done | bytes 294944 | tf_op jit(solution)/shard_map/ppermute | solution.py:653
  79.8 15.0 %project.1 = (bf16[1536,768]{1,0:T(8,128)(2,1)}, bf16[768,768]{1,0:T(8,128)(2,1)}, bf16[1536,1536]{1,0:T(8,128)(2,1)}, bf16[192,1536]{1,0:T(8,128)(2,1)}, f32[24,768]{1,0:T(8,128)}) custom-call(s32[17]{0:T(128)} %pad_add_fusion.order, bf16[768,768]{1,0:T(8,128)(2,1)} %bitcast.54, bf16[384,768]{1,0:T(8,128)(2,1)} %bitcast.59, bf16[384,768]{1,0:T(8,128)(2,1)} %bitcast.60, ...), custom_call_target="tpu_custom_call" | custom-call | flops 825000000 | bytes 2625000 | tf_op jit(solution)/shard_map/project/pallas_call | solution.py:1056
  98.3 1.9 collective-permute-start.18
  100.2 7.3 %collective-permute-start.15 = (bf16[192,1536]{1,0:T(8,128)(2,1)}, bf16[192,1536]{1,0:T(8,128)(2,1)S(1)}, u32[]{:S(2)}, u32[]{:S(2)}) collective-permute-start(bf16[192,1536]{1,0:T(8,128)(2,1)} %get-tuple-element.101.refs_0_), channel_id=1, source_target_pairs={{0,2},{2,4},{3,1},{4,6},{5,3},{6,8},{7,5},{8,10},{9,7},{10,12},{11... | collective-permute-start | bytes 1769480 | tf_op jit(solution)/shard_map/ppermute | solution.py:938
  113.6 1.5 reshape.274.bias_in
  115.1 10.4 %window.1 = (bf16[768,768]{1,0:T(8,128)(2,1)}, bf16[6,6,256,128]{3,2,1,0:T(8,128)(2,1)}) custom-call(bf16[768,768]{1,0:T(8,128)(2,1)} %get-tuple-element.98.queries, bf16[1536,1536]{1,0:T(8,128)(2,1)} %get-tuple-element.99.pairs, f32[6,128,128]{2,1,0:T(8,128)} %get-tuple-element.182.bias), custom_call_target="tpu_custom_call" | custom-call | flops 550000000 | bytes 1750000 | tf_op jit(solution)/shard_map/window/pallas_call | solution.py:1096
  126.7 13.9 %pooled.3 = (bf16[768,768]{1,0:T(8,128)(2,1)}, bf16[768,768]{1,0:T(8,128)(2,1)}, bf16[6,6,256,128]{3,2,1,0:T(8,128)(2,1)}) custom-call(s32[17]{0:T(128)} %pad_add_fusion.order, s32[5]{0:T(128)} %broadcast_select_fusion.places, bf16[768,768]{1,0:T(8,128)(2,1)} %get-tuple-element.100.attended.first, f32[6,128,128]{2,1,0:T(8,128)} %get-tuple-element.181.bias, ...), custom_call_target="tpu_custom_call" | custom-call | flops 770000000 | bytes 2450000 | tf_op jit(solution)/shard_map/pooled/pallas_call | solution.py:1109
  140.6 44.9 %feed.1 = (bf16[768,768]{1,0:T(8,128)(2,1)}, f32[768,768]{1,0:T(8,128)}, bf16[768,768]{1,0:T(8,128)(2,1)}, bf16[6400,768]{1,0:T(8,128)(2,1)}, f32[8,768]{1,0:T(8,128)}) custom-call(s32[17]{0:T(128)} %pad_add_fusion.order, bf16[768,768]{1,0:T(8,128)(2,1)} %bitcast.55, bf16[768,768]{1,0:T(8,128)(2,1)} %get-tuple-element.104.mixed, bf16[768,768]{1,0:T(8,128)(2,1)} %bitcast.58, ...), custom_call_target="tpu_custom_call" | custom-call | flops 2475000064 | bytes 7875000 | tf_op jit(solution)/shard_map/feed/pallas_call | solution.py:1128
  185.5 22.3 %pooled_back.1 = (f32[768,768]{1,0:T(8,128)}, bf16[768,768]{1,0:T(8,128)(2,1)}, bf16[768,768]{1,0:T(8,128)(2,1)}, bf16[192,1536]{1,0:T(8,128)(2,1)}, bf16[2,192,...) custom-call(s32[17]{0:T(128)} %pad_add_fusion.order, s32[5]{0:T(128)} %broadcast_select_fusion.places, ...), custom_call_target="tpu_custom_call" | custom-call | flops 1210000000 | bytes 3850000 | tf_op jit(solution)/shard_map/pooled_back/pallas_call | solution.py:1165
  209.3 1.7 collective-permute-done.20
  212.2 23.6 %collective-permute-start.21 = (bf16[192,1536]{1,0:T(8,128)(2,1)S(1)}, bf16[192,1536]{1,0:T(8,128)(2,1)S(1)}, u32[]{:S(2)}, u32[]{:S(2)}) collective-permute-start(bf16[192,1536]{1,0:T(8,128)(2,1)S(1)} %fusion), channel_id=1, source_target_pairs={{3,1},{0,2},{5,3},{2,4},{7,5},{4,6},{9,7},{6,8},{11,9},{8,10},{13,... | collective-permute-start | bytes 1769480 | tf_op jit(solution)/shard_map/ppermute | solution.py:1211
  235.8 22.7 %window_back.1 = (bf16[768,768]{1,0:T(8,128)(2,1)}, bf16[1536,1536]{1,0:T(8,128)(2,1)}, bf16[768,768]{1,0:T(8,128)(2,1)}) custom-call(s32[17]{0:T(128)} %pad_add_fusion.order, f32[768,768]{1,0:T(8,128)} %get-tuple-element.114.grad_mixed, bf16[768,768]{1,0:T(8,128)(2,1)} %get-tuple-element.115.grad_second, ...), custom_call_target="tpu_custom_call" | custom-call | flops 1210000000 | bytes 3850000 | tf_op jit(solution)/shard_map/window_back/pallas_call | solution.py:1213
  259.4 8.3 %collective-permute-done.21.near = bf16[192,1536]{1,0:T(8,128)(2,1)S(1)} collective-permute-done((bf16[192,1536]{1,0:T(8,128)(2,1)S(1)}, bf16[192,1536]{1,0:T(8,128)(2,1)S(1)}, u32[]{:S(2)}, u32[]{:S(2)}) %collective-permute-start.21) | collective-permute-done | bytes 589856 | tf_op jit(solution)/shard_map/ppermute | solution.py:1211
  268.5 12.3 %conv_back.1 = (bf16[1536,1536]{1,0:T(8,128)(2,1)}, f32[16,768]{1,0:T(8,128)}, bf16[768,768]{1,0:T(8,128)(2,1)}) custom-call(s32[17]{0:T(128)} %pad_add_fusion.order, bf16[192,1536]{1,0:T(8,128)(2,1)} %get-tuple-element.118.own, bf16[192,1536]{1,0:T(8,128)(2,1)} %slice_bitcast_fusion.1.away, bf16[192,1536]{1,0:T(8,128)(2,1)} %copy-done.20, ...), custom_call_target="tpu_custom_call" | custom-call | flops 660000000 | bytes 2100000 | tf_op jit(solution)/shard_map/conv_back/pallas_call | solution.py:1238
  280.8 13.4 %weight_grad.1 = (bf16[2,4,48,3968]{3,2,1,0:T(8,128)(2,1)}, bf16[2,4,48,3968]{3,2,1,0:T(8,128)(2,1)}) custom-call(s32[17]{0:T(128)} %pad_add_fusion.order, bf16[768,768]{1,0:T(8,128)(2,1)} %bitcast.56, bf16[1536,768]{1,0:T(8,128)(2,1)} %get-tuple-element.110.xext, bf16[768,768]{1,0:T(8,128)(2,1)} %get-tuple-element.117.grad_queries, ...), custom_call_target="tpu_custom_call" | custom-call | flops 770000000 | bytes 2450000 | tf_op jit(solution)/shard_map/weight_grad/pallas_call | solution.py:1261
  294.3 5.7 %collective-permute-done.23.arrived = bf16[2,4,48,3968]{3,2,1,0:T(8,128)(2,1)S(1)} collective-permute-done((bf16[2,4,48,3968]{3,2,1,0:T(8,128)(2,1)}, bf16[2,4,48,3968]{3,2,1,0:T(8,128)(2,1)S(1)}, u32[]{:S(2)}, u32[]{:S(2)}) %collective-permute-start.23) | collective-permute-done | bytes 3047456 | tf_op jit(solution)/shard_map/ppermute | solution.py:932
  300.0 1.6 copy-done.8
  301.6 4.9 %split.1 = (bf16[2,4,48,896]{3,2,1,0:T(8,128)(2,1)}, bf16[2,4,48,896]{3,2,1,0:T(8,128)(2,1)}, bf16[4,48,2176]{2,1,0:T(8,128)(2,1)}, bf16[4,48,2176]{2,1,0:T(8,128)(2,1)}) custom-call(s32[17]{0:T(128)} %pad_add_fusion.order, bf16[2,4,48,3968]{3,2,1,0:T(8,128)(2,1)} %get-tuple-element.127.keep, bf16[2,4,48,3968]{3,2,1,0:T(8,128)(2,1)} %copy-done.8), custom_call_target="tpu_custom_call" | custom-call | flops 275000000 | bytes 875000 | tf_op jit(solution)/shard_map/split/pallas_call | solution.py:821
  306.5 3.0 collective-permute-start.26
  309.5 2.8 collective-permute-start.28
  312.3 13.1 %collective-permute-done.26.arrived = bf16[2,4,48,896]{3,2,1,0:T(8,128)(2,1)S(1)} collective-permute-done((bf16[2,4,48,896]{3,2,1,0:T(8,128)(2,1)}, bf16[2,4,48,896]{3,2,1,0:T(8,128)(2,1)S(1)}, u32[]{:S(2)}, u32[]{:S(2)}) %collective-permute-start.26) | collective-permute-done | bytes 688160 | tf_op jit(solution)/shard_map/ppermute | solution.py:657
  326.3 3.4 fold.1
  329.7 2.8 collective-permute-start.27
  332.5 6.0 %collective-permute-done.28.b_arrived = bf16[4,48,2176]{2,1,0:T(8,128)(2,1)S(1)} collective-permute-done((bf16[4,48,2176]{2,1,0:T(8,128)(2,1)}, bf16[4,48,2176]{2,1,0:T(8,128)(2,1)S(1)}, u32[]{:S(2)}, u32[]{:S(2)}) %collective-permute-start.28) | collective-permute-done | bytes 835616 | tf_op jit(solution)/shard_map/ppermute | solution.py:653
  338.5 6.5 %collective-permute-done.27.x_arrived = bf16[4,48,896]{2,1,0:T(8,128)(2,1)S(1)} collective-permute-done((bf16[4,48,896]{2,1,0:T(8,128)(2,1)}, bf16[4,48,896]{2,1,0:T(8,128)(2,1)S(1)}, u32[]{:S(2)}, u32[]{:S(2)}) %collective-permute-start.27) | collective-permute-done | bytes 344096 | tf_op jit(solution)/shard_map/ppermute | solution.py:653
  345.7 2.7 join.1
  348.5 3.9 collective-permute-start.29
  353.7 3.1 collective-permute-start.24
  356.8 1.5 collective-permute-start.33
  358.4 2.4 collective-permute-start.30
  361.7 1.6 collective-permute-start.31
  363.3 20.4 %collective-permute-done.30.second = bf16[48,3072]{1,0:T(8,128)(2,1)S(1)} collective-permute-done((bf16[48,3072]{1,0:T(8,128)(2,1)}, bf16[48,3072]{1,0:T(8,128)(2,1)S(1)}, u32[]{:S(2)}, u32[]{:S(2)}) %collective-permute-start.30) | collective-permute-done | bytes 294944 | tf_op jit(solution)/shard_map/ppermute | solution.py:649
  384.4 2.1 gather_sum.1.own
  389.5 10.5 %token_grad.1 = f32[768,768]{1,0:T(8,128)} custom-call(s32[17]{0:T(128)} %pad_add_fusion.order, f32[768,768]{1,0:T(8,128)} %get-tuple-element.130.grad_resid, bf16[768,768]{1,0:T(8,128)(2,1)} %get-tuple-element.117.grad_queries, bf16[1536,1536]{1,0:T(8,128)(2,1)} %get-tuple-element.123.grad_pairs, bf16[384,768]{1,0:T(8,128)(2,1)} %copy-done.18, ...), custom_call_target="tpu_custom_call" | custom-call | flops 605000000 | bytes 1925000 | tf_op jit(solution)/shard_map/token_grad/pallas_call | solution.py:1282
  400.7 2.0 final.1
  404.9 2.3 bulk_final.1
  (133 shorter events, 40.9 us)
Async XLA Ops:
  7.2 133.4 %all-gather.2.cloned.1.call-start = ((), (), s32[]{:S(2)}) async-start(), calls=%async_computation.1 | async-start | bytes 10027008 | tf_op jit(solution)/shard_map/all_gather | solution.py:1014
  12.1 9.5 %collective-permute-start.2 = (bf16[48,1280]{1,0:T(8,128)(2,1)}, bf16[48,1280]{1,0:T(8,128)(2,1)S(1)}, u32[]{:S(2)}, u32[]{:S(2)}) collective-permute-start(bf16[48,1280]{1,0:T(8,128)(2,1)} %get-tuple-element.85), channel_id=1, source_target_pairs={{0,4},{1,5},{2,6},{3,7},{4,8},{5,9},{6,10},{7,11},{8,12},{9,13},{1... | collective-permute-start | bytes 368648 | tf_op jit(solution)/shard_map/ppermute | solution.py:649
  15.1 10.9 %collective-permute-start.1 = (bf16[48,1280]{1,0:T(8,128)(2,1)}, bf16[48,1280]{1,0:T(8,128)(2,1)S(1)}, u32[]{:S(2)}, u32[]{:S(2)}) collective-permute-start(bf16[48,1280]{1,0:T(8,128)(2,1)} %get-tuple-element.85), channel_id=1, source_target_pairs={{0,8},{1,9},{2,10},{3,11},{4,12},{5,13},{6,14},{7,15},{8,0},{9,1},... | collective-permute-start | bytes 368648 | tf_op jit(solution)/shard_map/ppermute | solution.py:649
  17.7 8.3 %collective-permute-start = (bf16[48,1280]{1,0:T(8,128)(2,1)}, bf16[48,1280]{1,0:T(8,128)(2,1)S(1)}, u32[]{:S(2)}, u32[]{:S(2)}) collective-permute-start(bf16[48,1280]{1,0:T(8,128)(2,1)} %get-tuple-element.85), channel_id=1, source_target_pairs={{0,12},{1,13},{2,14},{3,15},{4,0},{5,1},{6,2},{7,3},{8,4},{9,5},{1... | collective-permute-start | bytes 368648 | tf_op jit(solution)/shard_map/ppermute | solution.py:649
  27.0 16.1 %copy-start.22 = (bf16[48,768]{1,0:T(8,128)(2,1)S(1)}, bf16[48,768]{1,0:T(8,128)(2,1)}, u32[]{:S(2)}) copy-start(bf16[48,768]{1,0:T(8,128)(2,1)} %get-tuple-element.94) | copy-start | bytes 221188
  27.1 329.8 %reduce-scatter.2.cloned.1.call-start = ((), (), s32[]{:S(2)}) async-start(), calls=%async_computation.2 | async-start | bytes 10444800 | tf_op jit(solution)/shard_map/reduce_scatter | solution.py:1162
  27.1 14.6 %collective-permute-start.3 = (bf16[4,48,1280]{2,1,0:T(8,128)(2,1)S(1)}, bf16[4,48,1280]{2,1,0:T(8,128)(2,1)S(1)}, u32[]{:S(2)}, u32[]{:S(2)}) collective-permute-start(bf16[4,48,1280]{2,1,0:T(8,128)(2,1)S(1)} %pad_maximum_fusion), channel_id=1, source_target_pairs={{0,2},{1,3},{2,0},{3,1},{4,6},{5,7},{6,4},{7,5},{8,10},{9,11},{10,... | collective-permute-start | bytes 1474568 | tf_op jit(solution)/shard_map/ppermute | solution.py:653
  41.7 38.0 %copy-start.1 = (bf16[8,48,1280]{2,1,0:T(8,128)(2,1)}, bf16[8,48,1280]{2,1,0:T(8,128)(2,1)S(1)}, u32[]{:S(2)}) copy-start(bf16[8,48,1280]{2,1,0:T(8,128)(2,1)S(1)} %constant_dynamic-update-slice_fusion.refs_0_) | copy-start | bytes 2949124
  41.7 21.3 %collective-permute-start.6 = (bf16[8,48,1280]{2,1,0:T(8,128)(2,1)S(1)}, bf16[8,48,1280]{2,1,0:T(8,128)(2,1)S(1)}, u32[]{:S(2)}, u32[]{:S(2)}) collective-permute-start(bf16[8,48,1280]{2,1,0:T(8,128)(2,1)S(1)} %constant_dynamic-update-slice_fusion.refs_0_), channel_id=1, source_target_pairs={{0,16},{16,0},{1,17},{17,1},{2,18},{18,2},{3,19},{19,3},{4,20},{20... | collective-permute-start | bytes 2949128 | tf_op jit(solution)/shard_map/ppermute | solution.py:657
  43.1 9.0 %collective-permute-start.9 = (bf16[48,768]{1,0:T(8,128)(2,1)S(1)}, bf16[48,768]{1,0:T(8,128)(2,1)S(1)}, u32[]{:S(2)}, u32[]{:S(2)}) collective-permute-start(bf16[48,768]{1,0:T(8,128)(2,1)S(1)} %copy-done.22), channel_id=1, source_target_pairs={{0,4},{1,5},{2,6},{3,7},{4,8},{5,9},{6,10},{7,11},{8,12},{9,13},{1... | collective-permute-start | bytes 221192 | tf_op jit(solution)/shard_map/ppermute | solution.py:649
  48.0 10.0 %collective-permute-start.8 = (bf16[48,768]{1,0:T(8,128)(2,1)S(1)}, bf16[48,768]{1,0:T(8,128)(2,1)S(1)}, u32[]{:S(2)}, u32[]{:S(2)}) collective-permute-start(bf16[48,768]{1,0:T(8,128)(2,1)S(1)} %copy-done.22), channel_id=1, source_target_pairs={{0,8},{1,9},{2,10},{3,11},{4,12},{5,13},{6,14},{7,15},{8,0},{9,1},... | collective-permute-start | bytes 221192 | tf_op jit(solution)/shard_map/ppermute | solution.py:649
  48.0 10.0 %collective-permute-start.7 = (bf16[48,768]{1,0:T(8,128)(2,1)S(1)}, bf16[48,768]{1,0:T(8,128)(2,1)S(1)}, u32[]{:S(2)}, u32[]{:S(2)}) collective-permute-start(bf16[48,768]{1,0:T(8,128)(2,1)S(1)} %copy-done.22), channel_id=1, source_target_pairs={{0,12},{1,13},{2,14},{3,15},{4,0},{5,1},{6,2},{7,3},{8,4},{9,5},{1... | collective-permute-start | bytes 221192 | tf_op jit(solution)/shard_map/ppermute | solution.py:649
  50.4 27.2 %collective-permute-start.4 = (bf16[6,64,768]{2,1,0:T(8,128)(2,1)}, bf16[6,64,768]{2,1,0:T(8,128)(2,1)S(1)}, u32[]{:S(2)}, u32[]{:S(2)}) collective-permute-start(bf16[6,64,768]{2,1,0:T(8,128)(2,1)} %get-tuple-element.90), channel_id=1, source_target_pairs={{0,1},{1,2},{2,3},{3,4},{4,5},{5,6},{6,7},{7,8},{8,9},{9,10},{10,1... | collective-permute-start | bytes 1769480 | tf_op jit(solution)/shard_map/ppermute | solution.py:926
  52.2 25.4 %collective-permute-start.5 = (bf16[6,64,768]{2,1,0:T(8,128)(2,1)}, bf16[6,64,768]{2,1,0:T(8,128)(2,1)S(1)}, u32[]{:S(2)}, u32[]{:S(2)}) collective-permute-start(bf16[6,64,768]{2,1,0:T(8,128)(2,1)} %get-tuple-element.92), channel_id=1, source_target_pairs={{1,0},{2,1},{3,2},{4,3},{5,4},{6,5},{7,6},{8,7},{9,8},{10,9},{11,1... | collective-permute-start | bytes 1769480 | tf_op jit(solution)/shard_map/ppermute | solution.py:926
  63.1 16.7 %copy-start.5 = (bf16[8,48,1280]{2,1,0:T(8,128)(2,1)}, bf16[8,48,1280]{2,1,0:T(8,128)(2,1)S(1)}, u32[]{:S(2)}) copy-start(bf16[8,48,1280]{2,1,0:T(8,128)(2,1)S(1)} %collective-permute-done.6.refs_1_) | copy-start | bytes 2949124
  63.1 14.5 %collective-permute-start.10 = (bf16[8,48,1280]{2,1,0:T(8,128)(2,1)S(1)}, bf16[8,48,1280]{2,1,0:T(8,128)(2,1)S(1)}, u32[]{:S(2)}, u32[]{:S(2)}) collective-permute-start(bf16[8,48,1280]{2,1,0:T(8,128)(2,1)S(1)} %constant_dynamic-update-slice_fusion.refs_0_), channel_id=1, source_target_pairs={{0,1},{1,0},{2,3},{3,2},{4,5},{5,4},{6,7},{7,6},{8,9},{9,8},{10,11... | collective-permute-start | bytes 2949128 | tf_op jit(solution)/shard_map/ppermute | solution.py:932
  63.1 14.6 %collective-permute-start.11 = (bf16[8,48,1280]{2,1,0:T(8,128)(2,1)S(1)}, bf16[8,48,1280]{2,1,0:T(8,128)(2,1)S(1)}, u32[]{:S(2)}, u32[]{:S(2)}) collective-permute-start(bf16[8,48,1280]{2,1,0:T(8,128)(2,1)S(1)} %collective-permute-done.6.refs_1_), channel_id=1, source_target_pairs={{0,1},{1,0},{2,3},{3,2},{4,5},{5,4},{6,7},{7,6},{8,9},{9,8},{10,11... | collective-permute-start | bytes 2949128 | tf_op jit(solution)/shard_map/ppermute | solution.py:932
  63.6 13.9 %collective-permute-start.16 = (bf16[4,48,768]{2,1,0:T(8,128)(2,1)S(1)}, bf16[4,48,768]{2,1,0:T(8,128)(2,1)S(1)}, u32[]{:S(2)}, u32[]{:S(2)}) collective-permute-start(bf16[4,48,768]{2,1,0:T(8,128)(2,1)S(1)} %pad_maximum_fusion.1), channel_id=1, source_target_pairs={{0,2},{1,3},{2,0},{3,1},{4,6},{5,7},{6,4},{7,5},{8,10},{9,11},{10,... | collective-permute-start | bytes 884744 | tf_op jit(solution)/shard_map/ppermute | solution.py:653
  77.5 20.8 %copy-start = (bf16[8,48,768]{2,1,0:T(8,128)(2,1)}, bf16[8,48,768]{2,1,0:T(8,128)(2,1)S(1)}, u32[]{:S(2)}) copy-start(bf16[8,48,768]{2,1,0:T(8,128)(2,1)S(1)} %constant_dynamic-update-slice_fusion.5.refs_5_.refs_0_) | copy-start | bytes 1769476
  79.8 17.4 %copy-start.26 = (s32[6,2048]{1,0:T(8,128)S(1)}, s32[6,2048]{1,0:T(8,128)}, u32[]{:S(2)}) copy-start(s32[6,2048]{1,0:T(8,128)} %param.36) | copy-start | bytes 147460
  79.8 18.0 %copy-start.27 = (s32[5]{0:T(128)S(1)}, s32[5]{0:T(128)}, u32[]{:S(2)}) copy-start(s32[5]{0:T(128)} %constant.114.clone) | copy-start | bytes 64
  79.8 18.0 %copy-start.28 = (s32[5]{0:T(128)S(1)}, s32[5]{0:T(128)}, u32[]{:S(2)}) copy-start(s32[5]{0:T(128)} %constant.113.clone) | copy-start | bytes 64
  94.8 14.2 %collective-permute-start.17 = (bf16[8,48,768]{2,1,0:T(8,128)(2,1)S(1)}, bf16[8,48,768]{2,1,0:T(8,128)(2,1)S(1)}, u32[]{:S(2)}, u32[]{:S(2)}) collective-permute-start(bf16[8,48,768]{2,1,0:T(8,128)(2,1)S(1)} %constant_dynamic-update-slice_fusion.5.refs_5_.refs_0_), channel_id=1, source_target_pairs={{0,16},{16,0},{1,17},{17,1},{2,18},{18,2},{3,19},{19,3},{4,20},{20... | collective-permute-start | bytes 1769480 | tf_op jit(solution)/shard_map/ppermute | solution.py:657
  95.9 13.1 %collective-permute-start.13 = (bf16[192,1536]{1,0:T(8,128)(2,1)}, bf16[192,1536]{1,0:T(8,128)(2,1)S(1)}, u32[]{:S(2)}, u32[]{:S(2)}) collective-permute-start(bf16[192,1536]{1,0:T(8,128)(2,1)} %get-tuple-element.101.refs_0_), channel_id=1, source_target_pairs={{1,3},{2,0},{3,5},{4,2},{5,7},{6,4},{7,9},{8,6},{9,11},{10,8},{11,... | collective-permute-start | bytes 1769480 | tf_op jit(solution)/shard_map/ppermute | solution.py:938
  98.3 27.1 %collective-permute-start.18 = (bf16[8,48,768]{2,1,0:T(8,128)(2,1)S(1)}, bf16[8,48,768]{2,1,0:T(8,128)(2,1)S(1)}, u32[]{:S(2)}, u32[]{:S(2)}) collective-permute-start(bf16[8,48,768]{2,1,0:T(8,128)(2,1)S(1)} %constant_dynamic-update-slice_fusion.5.refs_5_.refs_0_), channel_id=1, source_target_pairs={{0,1},{1,0},{2,3},{3,2},{4,5},{5,4},{6,7},{7,6},{8,9},{9,8},{10,11... | collective-permute-start | bytes 1769480 | tf_op jit(solution)/shard_map/ppermute | solution.py:932
  100.2 25.3 %collective-permute-start.15 = (bf16[192,1536]{1,0:T(8,128)(2,1)}, bf16[192,1536]{1,0:T(8,128)(2,1)S(1)}, u32[]{:S(2)}, u32[]{:S(2)}) collective-permute-start(bf16[192,1536]{1,0:T(8,128)(2,1)} %get-tuple-element.101.refs_0_), channel_id=1, source_target_pairs={{0,2},{2,4},{3,1},{4,6},{5,3},{6,8},{7,5},{8,10},{9,7},{10,12},{11... | collective-permute-start | bytes 1769480 | tf_op jit(solution)/shard_map/ppermute | solution.py:938
  107.5 18.0 %collective-permute-start.12 = (bf16[192,1536]{1,0:T(8,128)(2,1)}, bf16[192,1536]{1,0:T(8,128)(2,1)}, u32[]{:S(2)}, u32[]{:S(2)}) collective-permute-start(bf16[192,1536]{1,0:T(8,128)(2,1)} %get-tuple-element.101.refs_0_), channel_id=1, source_target_pairs={{0,1},{1,0},{2,3},{3,2},{4,5},{5,4},{6,7},{7,6},{8,9},{9,8},{10,11... | collective-permute-start | bytes 1769480 | tf_op jit(solution)/shard_map/ppermute | solution.py:932
  109.0 16.5 %copy-start.2 = (bf16[8,48,768]{2,1,0:T(8,128)(2,1)}, bf16[8,48,768]{2,1,0:T(8,128)(2,1)S(1)}, u32[]{:S(2)}) copy-start(bf16[8,48,768]{2,1,0:T(8,128)(2,1)S(1)} %collective-permute-done.17.refs_6_.refs_1_) | copy-start | bytes 1769476
  109.0 16.5 %collective-permute-start.19 = (bf16[8,48,768]{2,1,0:T(8,128)(2,1)S(1)}, bf16[8,48,768]{2,1,0:T(8,128)(2,1)S(1)}, u32[]{:S(2)}, u32[]{:S(2)}) collective-permute-start(bf16[8,48,768]{2,1,0:T(8,128)(2,1)S(1)} %collective-permute-done.17.refs_6_.refs_1_), channel_id=1, source_target_pairs={{0,1},{1,0},{2,3},{3,2},{4,5},{5,4},{6,7},{7,6},{8,9},{9,8},{10,11... | collective-permute-start | bytes 1769480 | tf_op jit(solution)/shard_map/ppermute | solution.py:932
  109.0 16.5 %copy-start.9 = (bf16[192,1536]{1,0:T(8,128)(2,1)}, bf16[192,1536]{1,0:T(8,128)(2,1)S(1)}, u32[]{:S(2)}) copy-start(bf16[192,1536]{1,0:T(8,128)(2,1)S(1)} %collective-permute-done.13.refs_3_) | copy-start | bytes 1769476
  109.0 16.5 %collective-permute-start.14 = (bf16[192,1536]{1,0:T(8,128)(2,1)S(1)}, bf16[192,1536]{1,0:T(8,128)(2,1)}, u32[]{:S(2)}, u32[]{:S(2)}) collective-permute-start(bf16[192,1536]{1,0:T(8,128)(2,1)S(1)} %collective-permute-done.13.refs_3_), channel_id=1, source_target_pairs={{0,1},{1,0},{2,3},{3,2},{4,5},{5,4},{6,7},{7,6},{8,9},{9,8},{10,11... | collective-permute-start | bytes 1769480 | tf_op jit(solution)/shard_map/ppermute | solution.py:932
  207.9 3.1 collective-permute-start.20
  208.0 51.4 %collective-permute-start.22 = (bf16[192,1536]{1,0:T(8,128)(2,1)}, bf16[192,1536]{1,0:T(8,128)(2,1)S(1)}, u32[]{:S(2)}, u32[]{:S(2)}) collective-permute-start(bf16[192,1536]{1,0:T(8,128)(2,1)} %get-tuple-element.121), channel_id=1, source_target_pairs={{2,0},{4,2},{1,3},{6,4},{3,5},{8,6},{5,7},{10,8},{7,9},{12,10},{9,... | collective-permute-start | bytes 1769480 | tf_op jit(solution)/shard_map/ppermute | solution.py:1209
  212.2 55.5 %collective-permute-start.21 = (bf16[192,1536]{1,0:T(8,128)(2,1)S(1)}, bf16[192,1536]{1,0:T(8,128)(2,1)S(1)}, u32[]{:S(2)}, u32[]{:S(2)}) collective-permute-start(bf16[192,1536]{1,0:T(8,128)(2,1)S(1)} %fusion), channel_id=1, source_target_pairs={{3,1},{0,2},{5,3},{2,4},{7,5},{4,6},{9,7},{6,8},{11,9},{8,10},{13,... | collective-permute-start | bytes 1769480 | tf_op jit(solution)/shard_map/ppermute | solution.py:1211
  259.4 8.3 %copy-start.19 = (bf16[192,1536]{1,0:T(8,128)(2,1)}, bf16[192,1536]{1,0:T(8,128)(2,1)S(1)}, u32[]{:S(2)}) copy-start(bf16[192,1536]{1,0:T(8,128)(2,1)S(1)} %collective-permute-done.22.far) | copy-start | bytes 1769476
  294.2 5.8 %collective-permute-start.23 = (bf16[2,4,48,3968]{3,2,1,0:T(8,128)(2,1)}, bf16[2,4,48,3968]{3,2,1,0:T(8,128)(2,1)S(1)}, u32[]{:S(2)}, u32[]{:S(2)}) collective-permute-start(bf16[2,4,48,3968]{3,2,1,0:T(8,128)(2,1)} %get-tuple-element.128), channel_id=1, source_target_pairs={{0,1},{1,0},{2,3},{3,2},{4,5},{5,4},{6,7},{7,6},{8,9},{9,8},{10,11... | collective-permute-start | bytes 9142280 | tf_op jit(solution)/shard_map/ppermute | solution.py:932
  306.5 18.9 %collective-permute-start.26 = (bf16[2,4,48,896]{3,2,1,0:T(8,128)(2,1)}, bf16[2,4,48,896]{3,2,1,0:T(8,128)(2,1)S(1)}, u32[]{:S(2)}, u32[]{:S(2)}) collective-permute-start(bf16[2,4,48,896]{3,2,1,0:T(8,128)(2,1)} %get-tuple-element.129), channel_id=1, source_target_pairs={{0,16},{16,0},{1,17},{17,1},{2,18},{18,2},{3,19},{19,3},{4,20},{20... | collective-permute-start | bytes 2064392 | tf_op jit(solution)/shard_map/ppermute | solution.py:657
  309.5 29.0 %collective-permute-start.28 = (bf16[4,48,2176]{2,1,0:T(8,128)(2,1)}, bf16[4,48,2176]{2,1,0:T(8,128)(2,1)S(1)}, u32[]{:S(2)}, u32[]{:S(2)}) collective-permute-start(bf16[4,48,2176]{2,1,0:T(8,128)(2,1)} %get-tuple-element.136), channel_id=1, source_target_pairs={{0,2},{1,3},{2,0},{3,1},{4,6},{5,7},{6,4},{7,5},{8,10},{9,11},{10,... | collective-permute-start | bytes 2506760 | tf_op jit(solution)/shard_map/ppermute | solution.py:653
  329.7 15.3 %collective-permute-start.27 = (bf16[4,48,896]{2,1,0:T(8,128)(2,1)}, bf16[4,48,896]{2,1,0:T(8,128)(2,1)S(1)}, u32[]{:S(2)}, u32[]{:S(2)}) collective-permute-start(bf16[4,48,896]{2,1,0:T(8,128)(2,1)} %get-tuple-element.134), channel_id=1, source_target_pairs={{0,2},{1,3},{2,0},{3,1},{4,6},{5,7},{6,4},{7,5},{8,10},{9,11},{10,... | collective-permute-start | bytes 1032200 | tf_op jit(solution)/shard_map/ppermute | solution.py:653
  345.7 6.6 %copy-start.11 = (bf16[768,768]{1,0:T(8,128)(2,1)S(1)}, bf16[768,768]{1,0:T(8,128)(2,1)}, u32[]{:S(2)}) copy-start(bf16[768,768]{1,0:T(8,128)(2,1)} %get-tuple-element.131) | copy-start | bytes 3538948
  348.5 13.2 %collective-permute-start.29 = (bf16[48,3072]{1,0:T(8,128)(2,1)}, bf16[48,3072]{1,0:T(8,128)(2,1)S(1)}, u32[]{:S(2)}, u32[]{:S(2)}) collective-permute-start(bf16[48,3072]{1,0:T(8,128)(2,1)} %get-tuple-element.138), channel_id=1, source_target_pairs={{0,4},{1,5},{2,6},{3,7},{4,8},{5,9},{6,10},{7,11},{8,12},{9,13},{1... | collective-permute-start | bytes 884744 | tf_op jit(solution)/shard_map/ppermute | solution.py:649
  352.4 35.4 %collective-permute-start.25 = (bf16[384,768]{1,0:T(8,128)(2,1)S(1)}, bf16[384,768]{1,0:T(8,128)(2,1)S(1)}, u32[]{:S(2)}, u32[]{:S(2)}) collective-permute-start(bf16[384,768]{1,0:T(8,128)(2,1)S(1)} %get-tuple-element.168), channel_id=1, source_target_pairs={{1,0},{2,1},{3,2},{4,3},{5,4},{6,5},{7,6},{8,7},{9,8},{10,9},{11,1... | collective-permute-start | bytes 1769480 | tf_op jit(solution)/shard_map/ppermute | solution.py:926
  353.7 34.1 %collective-permute-start.24 = (bf16[384,768]{1,0:T(8,128)(2,1)S(1)}, bf16[384,768]{1,0:T(8,128)(2,1)S(1)}, u32[]{:S(2)}, u32[]{:S(2)}) collective-permute-start(bf16[384,768]{1,0:T(8,128)(2,1)S(1)} %get-tuple-element.169), channel_id=1, source_target_pairs={{0,1},{1,2},{2,3},{3,4},{4,5},{5,6},{6,7},{7,8},{8,9},{9,10},{10,1... | collective-permute-start | bytes 1769480 | tf_op jit(solution)/shard_map/ppermute | solution.py:926
  356.8 47.3 %collective-permute-start.33 = (bf16[400,768]{1,0:T(8,128)(2,1)}, bf16[400,768]{1,0:T(8,128)(2,1)S(1)}, u32[]{:S(2)}, u32[]{:S(2)}) collective-permute-start(bf16[400,768]{1,0:T(8,128)(2,1)} %reduce-scatter.2.cloned.1.call-done.own), channel_id=1, source_target_pairs={{0,16},{16,0},{1,17},{17,1},{2,18},{18,2},{3,19},{19,3},{4,20},{20... | collective-permute-start | bytes 1843208 | tf_op jit(solution)/shard_map/ppermute | solution.py:657
  358.4 25.3 %collective-permute-start.30 = (bf16[48,3072]{1,0:T(8,128)(2,1)}, bf16[48,3072]{1,0:T(8,128)(2,1)S(1)}, u32[]{:S(2)}, u32[]{:S(2)}) collective-permute-start(bf16[48,3072]{1,0:T(8,128)(2,1)} %get-tuple-element.139), channel_id=1, source_target_pairs={{0,8},{1,9},{2,10},{3,11},{4,12},{5,13},{6,14},{7,15},{8,0},{9,1},... | collective-permute-start | bytes 884744 | tf_op jit(solution)/shard_map/ppermute | solution.py:649
  361.7 22.0 %copy-start.24 = (bf16[48,3072]{1,0:T(8,128)(2,1)}, bf16[48,3072]{1,0:T(8,128)(2,1)S(1)}, u32[]{:S(2)}) copy-start(bf16[48,3072]{1,0:T(8,128)(2,1)S(1)} %collective-permute-done.29.first) | copy-start | bytes 884740
  361.7 22.0 %collective-permute-start.31 = (bf16[48,3072]{1,0:T(8,128)(2,1)}, bf16[48,3072]{1,0:T(8,128)(2,1)}, u32[]{:S(2)}, u32[]{:S(2)}) collective-permute-start(bf16[48,3072]{1,0:T(8,128)(2,1)} %get-tuple-element.140), channel_id=1, source_target_pairs={{0,12},{1,13},{2,14},{3,15},{4,0},{5,1},{6,2},{7,3},{8,4},{9,5},{1... | collective-permute-start | bytes 884744 | tf_op jit(solution)/shard_map/ppermute | solution.py:649
  386.5 13.5 %collective-permute-start.32 = (bf16[48,3072]{1,0:T(8,128)(2,1)}, bf16[48,3072]{1,0:T(8,128)(2,1)S(1)}, u32[]{:S(2)}, u32[]{:S(2)}) collective-permute-start(bf16[48,3072]{1,0:T(8,128)(2,1)} %gather_sum.1.own), channel_id=1, source_target_pairs={{0,16},{16,0},{1,17},{17,1},{2,18},{18,2},{3,19},{19,3},{4,20},{20... | collective-permute-start | bytes 884744 | tf_op jit(solution)/shard_map/ppermute | solution.py:657
  (17 other events, 24.0 us)
Sparse Core Ops, SparseCore 0:
  27.2 102.1 all-gather.1
  185.6 154.0 reduce-scatter.1

commit v3 on v2

--- a/solution.py
+++ b/solution.py
@@ -25,7 +25,7 @@
 PAIR = 2 * HEAD_DIM
 TILE = 256
 SLOTS = 16
-VMEM_LIMIT = 60 * 1024 * 1024
+VMEM_LIMIT = 58
 SCALE = 0.05
 
 
@@ -49,6 +49,10 @@
     return pl.BlockSpec(memory_space=pl.ANY)
 
 
+def hbm_spec():
+    return pl.BlockSpec(memory_space=pltpu.HBM)
+
+
 def vmem_spec():
     return pl.BlockSpec(memory_space=pltpu.VMEM)
 
@@ -57,8 +61,8 @@
     return pl.BlockSpec(memory_space=pltpu.SMEM)
 
 
-def params(**more):
-    return pltpu.CompilerParams(vmem_limit_bytes=VMEM_LIMIT, **more)
+def params(mebibytes=VMEM_LIMIT):
+    return pltpu.CompilerParams(vmem_limit_bytes=mebibytes * 1024 * 1024)
 
 
 def cost(microseconds):
@@ -102,13 +106,30 @@
     return copies
 
 
+def bulk_rows(width, hidden):
+    return (2 * width + 2 * hidden) // SLOTS
+
+
+def fetch_square(bulk, which, target, sem):
+    width = bulk.shape[1]
+    block = width // SLOTS
+    each = bulk.shape[0] // SLOTS
+    copies = []
+    for j in range(SLOTS):
+        source = bulk.at[pl.ds(j * each + which * block, block), :]
+        copies.append(pltpu.make_async_copy(source, target.at[pl.ds(j * block, block), :], sem))
+        copies[-1].start()
+    return copies
+
+
 def fetch_bulk(bulk, w_in, w_down, sems):
     width = bulk.shape[1]
     block = width // SLOTS
+    each = bulk.shape[0] // SLOTS
     folds = w_in.shape[1] // width
     first, second = [], []
     for j in range(SLOTS):
-        start = j * 2 * folds * block
+        start = j * each + 2 * block
         for m in range(folds):
             source = bulk.at[pl.ds(start + m * block, block), :]
             target = w_in.at[pl.ds(j * block, block), pl.ds(m * width, width)]
@@ -168,7 +189,7 @@
 
 
 def project_kernel(table, order, tok, low, high, *refs):
-    xext, queries, pairs, pooled, vecs, weights, narrow, sem = refs[-8:]
+    queries, pairs, pooled, vecs, xext, weights, narrow, sem = refs[-8:]
     stacks = refs[:-8]
     width = tok.shape[1]
     copies = fetch_all(order, stacks, table, 3 * width // 2, weights, sem)
@@ -224,9 +245,9 @@
 
 
 def side_masks(step):
-    row = lax.broadcasted_iota(jnp.int32, (2 * WINDOW, WINDOW), 0)
-    lane = lax.broadcasted_iota(jnp.int32, (2 * WINDOW, WINDOW), 1)
-    near = lane >= lax.bitwise_and(row, WINDOW - 1) // step
+    slot = lax.broadcasted_iota(jnp.int32, (WINDOW, 2 * WINDOW), 0)
+    query = lax.broadcasted_iota(jnp.int32, (WINDOW, 2 * WINDOW), 1)
+    near = slot >= lax.bitwise_and(query, WINDOW - 1) // step
     return near, jnp.where(near, 1.0, 0.0).astype(BF16), jnp.where(near, 0.0, 1.0).astype(BF16)
 
 
@@ -239,28 +260,28 @@
 
 
 def spread_sides(block, sides):
-    return jnp.concatenate([block * sides[1], block * sides[2]], axis=1)
+    return jnp.concatenate([block * sides[1], block * sides[2]], axis=0)
 
 
 def attend(queries, keys, values, bias, lanes, sides):
-    scores = product_back(stack_heads(queries, lanes), keys)
-    scores = jnp.where(sides[0], scores[:, :WINDOW], scores[:, WINDOW:]) + bias
-    weights = jnp.exp(scores - jnp.max(scores, axis=-1, keepdims=True))
-    probs = (weights * (1.0 / jnp.sum(weights, axis=-1, keepdims=True))).astype(BF16)
-    mixed = product(spread_sides(probs, sides), values)
+    scores = product_back(keys, stack_heads(queries, lanes))
+    scores = jnp.where(sides[0], scores[:WINDOW], scores[WINDOW:]) + bias
+    weights = jnp.exp(scores - jnp.max(scores, axis=0, keepdims=True))
+    probs = (weights * (1.0 / jnp.sum(weights, axis=0, keepdims=True))).astype(BF16)
+    mixed = outer_sum(spread_sides(probs, sides), values)
     return probs, merge_heads(mixed, lanes)
 
 
 def attend_back(queries, keys, values, probs, grad_out, lanes, sides):
     grad_stack = stack_heads(grad_out, lanes)
-    grad_probs = product_back(grad_stack, values)
-    grad_probs = jnp.where(sides[0], grad_probs[:, :WINDOW], grad_probs[:, WINDOW:])
+    grad_probs = product_back(values, grad_stack)
+    grad_probs = jnp.where(sides[0], grad_probs[:WINDOW], grad_probs[WINDOW:])
     probs_full = probs.astype(F32)
-    centre = jnp.sum(probs_full * grad_probs, axis=-1, keepdims=True)
+    centre = jnp.sum(probs_full * grad_probs, axis=0, keepdims=True)
     grad_scores = spread_sides((probs_full * (grad_probs - centre)).astype(BF16), sides)
-    grad_values = outer_sum(spread_sides(probs, sides), grad_stack)
-    grad_keys = outer_sum(grad_scores, stack_heads(queries, lanes))
-    grad_queries = merge_heads(product(grad_scores, keys), lanes) * HEAD_DIM**-0.5
+    grad_values = product(spread_sides(probs, sides), grad_stack)
+    grad_keys = product(grad_scores, stack_heads(queries, lanes))
+    grad_queries = merge_heads(outer_sum(grad_scores, keys), lanes) * HEAD_DIM**-0.5
     return grad_queries, grad_keys, grad_values
 
 
@@ -268,7 +289,7 @@
     width = queries.shape[1]
     lanes = lane_masks()
     sides = side_masks(1)
-    both = jnp.concatenate([bias[0], bias[0]], axis=0)
+    both = jnp.concatenate([bias[0], bias[0]], axis=1)
     for n in range(width // PAIR):
         cols = slice(n * PAIR, (n + 1) * PAIR)
         held, out = attend(
@@ -289,16 +310,15 @@
         field[span(places[k], pools), :] = block[...]
 
 
-def pooled_kernel(table, order, places, attended, bias, *refs):
+def pooled_kernel(places, attended, bias, bulk, *refs):
     blocks = refs[:5]
-    stacks = refs[5:-6]
-    queries, mixed, probs, field, weights, sem = refs[-6:]
+    queries, mixed, probs, weights, field, sem = refs[-6:]
     width = attended.shape[1]
     s = pl.program_id(0)
 
     @pl.when(s == 0)
     def _():
-        copies = fetch(order, stacks, table, 0, (0, width), weights, sem)
+        copies = fetch_square(bulk, 0, weights, sem)
         field[...] = jnp.zeros_like(field)
         settle(copies)
 
@@ -310,7 +330,7 @@
     lay_pooled(places, blocks, field)
     lanes = lane_masks()
     sides = side_masks(STRIDE)
-    both = jnp.concatenate([bias[0], bias[0]], axis=0)
+    both = jnp.concatenate([bias[0], bias[0]], axis=1)
     rows = span(s, WINDOW)
     for n in range(width // PAIR):
         cols = slice(n * PAIR, (n + 1) * PAIR)
@@ -327,16 +347,14 @@
         mixed[:, cols] = (first + out.astype(BF16).astype(F32)).astype(BF16)
 
 
-def feed_kernel(table, order, tok, mixed, cot, vecs, bias_in, bulk, *refs):
-    at = len(refs) - 21
-    mid_stacks = refs[:at]
+def feed_kernel(tok, mixed, cot, vecs, bias_in, bulk, *refs):
     (
         result,
         grad_resid,
         grad_attn,
         gone,
+        w_out,
         vec_grads,
-        w_out,
         w_in,
         w_down,
         centred,
@@ -352,10 +370,10 @@
         bias_grad,
         narrow,
         sems,
-    ) = refs[at:]
+    ) = refs
     rows, width = tok.shape
     hidden = w_in.shape[1]
-    first = fetch(order, mid_stacks, table, 1, (0, width), w_out, sems.at[0])
+    first = fetch_square(bulk, 1, w_out, sems.at[0])
     second, third = fetch_bulk(bulk, w_in, w_down, (sems.at[1], sems.at[2]))
     settle(first)
 
@@ -481,20 +499,17 @@
     settle(emits)
 
 
-def pooled_back_kernel(table, order, places, grad_attn, mixed, queries, probs, *refs):
+def pooled_back_kernel(places, grad_attn, mixed, queries, probs, weights, *refs):
     blocks = refs[:5]
-    stacks = refs[5:-12]
-    grad_mixed, grad_queries, grad_out, grad_own, grad_away, grad_near, grad_far = refs[-12:-5]
-    field, total, grad_low, weights, sem = refs[-5:]
+    grad_mixed, grad_queries, grad_out, grad_own, grad_away, grad_near, grad_far = refs[-10:-3]
+    field, total, grad_low = refs[-3:]
     width = grad_attn.shape[1]
     pools = blocks[0].shape[0]
     s = pl.program_id(0)
 
     @pl.when(s == 0)
     def _():
-        copies = fetch(order, stacks, table, 1, (0, width), weights, sem)
         field[...] = jnp.zeros_like(field)
-        settle(copies)
 
         @pl.loop(0, width // TILE)
         def _(n):
@@ -521,16 +536,13 @@
         target[...] = total[span(places[k], pools), :].astype(BF16)
 
 
-def window_back_kernel(table, order, grad_mixed, grad_second, first, queries, pairs, probs, *refs):
-    stacks = refs[:-6]
-    grad_queries, grad_pairs, grad_pooled, grad_low, weights, sem = refs[-6:]
+def window_back_kernel(grad_mixed, grad_second, first, queries, pairs, probs, weights, *refs):
+    grad_queries, grad_pairs, grad_pooled, grad_low = refs
     width = first.shape[1]
     s = pl.program_id(0)
 
     @pl.when(s == 0)
     def _():
-        settle(fetch(order, stacks, table, 0, (0, width), weights, sem))
-
         @pl.loop(0, width // TILE)
         def _(n):
             cols = span(n, TILE)
@@ -594,29 +606,45 @@
         edges[:, cols] = product_back(rim[...], weights[cols, width:]).astype(BF16)
 
 
-def weight_grad_kernel(order, tok, xext, grad_queries, grad_pairs, tap_grads, *refs):
-    grad_pooled, grad_out, keep, give, tok_t, xext_t, total, narrow, sem = refs
+def query_grad_kernel(order, tok, grad_queries, grad_pooled, grad_out, keep, give, tok_t, total, sem):
     width = tok.shape[1]
     block = width // SLOTS
     targets = (keep, give)
     copies = emit(order, grad_pooled, pl.ds(0, width), block, targets, 3 * width, sem)
     copies += emit(order, grad_out, pl.ds(0, width), block, targets, 4 * width, sem)
-    taps = jnp.concatenate([tap_grads[...], jnp.zeros((112, width), F32)], axis=0).T
-    narrow[...] = taps.astype(BF16)
-    copies += emit(order, narrow, pl.ds(0, 128), block, targets, 5 * width, sem)
     tok_t[...] = tok[...].T
-    xext_t[...] = xext[...].T
 
     @pl.loop(0, width // TILE)
     def _(n):
         cols = span(n, TILE)
         total[:, cols] = product(tok_t[...], grad_queries[:, cols]).astype(BF16)
 
+    copies += emit(order, total, pl.ds(0, width), block, targets, 0, sem)
+    settle(copies)
+
+
+def weight_grad_kernel(order, tok, low, high, grad_pairs, tap_grads, *refs):
+    keep, give, xext_t, total, narrow, sem = refs[2:]
+    width = tok.shape[1]
+    block = width // SLOTS
+    targets = (keep, give)
+    taps = jnp.concatenate([tap_grads[...], jnp.zeros((112, width), F32)], axis=0).T
+    narrow[...] = taps.astype(BF16)
+    copies = emit(order, narrow, pl.ds(0, 128), block, targets, 5 * width, sem)
+    for s in range(low.shape[0] // HALF):
+        parts = (
+            low[s * HALF : (s + 1) * HALF, :],
+            tok[s * WINDOW : (s + 1) * WINDOW, :],
+            high[s * HALF : (s + 1) * HALF, :],
+        )
+        xext_t[:, s * WIDE : (s + 1) * WIDE] = jnp.concatenate(parts, axis=0).T
+
     @pl.loop(0, 2 * width // TILE)
     def _(n):
-        total[:, span(n + width // TILE, TILE)] = product(xext_t[...], grad_pairs[:, span(n, TILE)]).astype(BF16)
-
-    copies += emit(order, total, pl.ds(0, 3 * width), block, targets, 0, sem)
+        cols = span(n, TILE)
+        total[:, cols] = product(xext_t[...], grad_pairs[:, cols]).astype(BF16)
+
+    copies += emit(order, total, pl.ds(0, 2 * width), block, targets, width, sem)
     settle(copies)
 
 
@@ -657,27 +685,23 @@
     return lax.ppermute(block, "rep", [(0, 1), (1, 0)])
 
 
+def gate_kernel(*refs):
+    del refs
+
+
 def after(value, *others):
-    if not direct():
+    if not direct() or not others:
         return value
-    return lax.optimization_barrier((value,) + others)[0]
-
-
-def anchor_kernel(source, out):
-    del source, out
-
-
-def anchor(value):
     return pl.pallas_call(
-        anchor_kernel,
+        gate_kernel,
         out_shape=jax.ShapeDtypeStruct(value.shape, value.dtype),
-        in_specs=[any_spec()],
+        in_specs=[any_spec()] * (1 + len(others)),
         out_specs=any_spec(),
         input_output_aliases={0: 0},
-        compiler_params=params(),
-        cost_estimate=cost(2000),
-        name="anchor",
-    )(value)
+        compiler_params=params(2),
+        cost_estimate=cost(0),
+        name="gate",
+    )(value, *others)
 
 
 def direct():
@@ -694,36 +718,29 @@
 
 
 class Gather:
-    def __init__(self, block, mine=None, rest=None):
-        self.block, self.mine, self.rest = block, mine, rest
+    def __init__(self, block):
+        self.block = block
 
     def turn(self, *gate):
-        own = self.block if self.mine is None else self.mine
-        own = after(own, *gate)
+        own = after(self.block, *gate)
         self.along = jnp.stack([own] + [turn(own, step) for step in (1, 2, 3)])
-        return self.along
 
     def cross(self, *gate):
-        self.across = flip(after(self.along, *gate))
-        return self.across
+        self.along = after(self.along, *gate)
+        self.across = flip(self.along)
 
     def rep(self, *gate):
+        self.across = after(self.across, *gate)
         self.first = jnp.concatenate([self.along, self.across], axis=0)
-        self.second = other(after(self.first, *gate))
-        return self.second
+        self.second = other(self.first)
 
     def cores(self, *gate):
-        if self.mine is None:
-            stacks = [self.along, self.across]
-            stacks = stacks + [swap(after(stack, *gate)) for stack in stacks]
-            table = [((2 * (k % 2) + k // 2 % 2, k // 4, 0),) for k in range(SLOTS)]
-        else:
-            stacks = [self.first, self.second]
-            stacks = stacks + [swap(after(stack, *gate)) for stack in stacks]
-            table = []
-            for k in range(SLOTS):
-                part = k // 2 % 2 * 4 + k // 4
-                table.append(((2 * (k % 2), part, 0), (2 * (k % 2) + 1, part, 0)))
+        stacks = [self.first, after(self.second, *gate)]
+        stacks = stacks + [swap(stack) for stack in stacks]
+        table = []
+        for k in range(SLOTS):
+            part = k // 2 % 2 * 4 + k // 4
+            table.append(((2 * (k % 2), part, 0), (2 * (k % 2) + 1, part, 0)))
         return stacks, tuple(table)
 
 
@@ -740,12 +757,12 @@
 
 def pack_kernel(order, query, key, value, pooled, out, inner, outer, tokens, taps, *refs):
     vectors, bias = refs[:6], refs[6]
-    lead, lead_rest, mid, mid_rest, bulk, low, high, joined, small = refs[7:]
+    lead, bulk, low, high, joined, small = refs[7:]
     part, width = query.shape
     half = 3 * width // 2
     for k, source in enumerate((query, key, value)):
         joined[:, k * width : (k + 1) * width] = source[...]
-    mine, rest = order[SLOTS], 1 - order[SLOTS]
+    mine = order[SLOTS]
     small[...] = jnp.zeros_like(small)
     for k, source in enumerate(vectors):
         small[k : k + 1, :part] = source[...].astype(F32)
@@ -754,14 +771,12 @@
     small[BIAS_ROW:SMALL, :part] = bias[...].astype(F32)
     lead[:, :half] = joined[:, span(mine, half)]
     lead[:, half:] = small[...].T[:part].astype(BF16)
-    lead_rest[...] = joined[:, span(rest, half)]
-    first = mine == 0
-    mid[...] = jnp.where(first, pooled[...], out[...])
-    mid_rest[...] = jnp.where(first, out[...], pooled[...])
+    bulk[:part, :] = pooled[...]
+    bulk[part : 2 * part, :] = out[...]
     folds = inner.shape[1] // width
     for m in range(folds):
-        bulk[m * part : (m + 1) * part, :] = inner[:, m * width : (m + 1) * width]
-    bulk[folds * part :, :] = outer[...]
+        bulk[(2 + m) * part : (3 + m) * part, :] = inner[:, m * width : (m + 1) * width]
+    bulk[(2 + folds) * part :, :] = outer[...]
     high[...] = tokens[:, :HALF, :]
     low[...] = tokens[:, tokens.shape[1] - HALF :, :]
 
@@ -824,7 +839,7 @@
             out_shape=(a_shape, a_shape, b_shape, b_shape),
             in_specs=[smem_spec(), four, four],
             out_specs=(a_block, a_block, b_block, b_block),
-            compiler_params=params(),
+            compiler_params=params(14),
             cost_estimate=cost(5),
             name="split",
         )(self.order, self.keep, self.arrived)
@@ -843,7 +858,7 @@
             out_shape=(x_shape, x_shape),
             in_specs=[a_block, a_block],
             out_specs=(x_block, x_block),
-            compiler_params=params(),
+            compiler_params=params(10),
             cost_estimate=cost(4),
             name="fold",
         )(self.a_keep, self.a_arrived)
@@ -857,7 +872,7 @@
             out_shape=(shape,) * 4,
             in_specs=[vmem_spec()] * 4,
             out_specs=(vmem_spec(),) * 4,
-            compiler_params=params(),
+            compiler_params=params(14),
             cost_estimate=cost(3),
             name="join",
         )(self.x_keep, self.x_arrived, self.b_keep, self.b_arrived)
@@ -870,7 +885,7 @@
             out_shape=shape_of(self.rows, self.columns - self.wide // 2),
             in_specs=[vmem_spec()] * 4,
             out_specs=vmem_spec(),
-            compiler_params=params(),
+            compiler_params=params(10),
             cost_estimate=cost(2),
             name="gather_sum",
         )(*self.turned)
@@ -884,7 +899,7 @@
             in_specs=[smem_spec(), vmem_spec(), vmem_spec()],
             out_specs=(vmem_spec(),) * len(self.pieces),
             scratch_shapes=[pltpu.VMEM((self.rows, self.columns), F32)],
-            compiler_params=params(),
+            compiler_params=params(12),
             cost_estimate=cost(2),
             name="final",
         )(self.order, self.own, self.last)
@@ -980,15 +995,12 @@
             pack_kernel,
             out_shape=(
                 shape_of(part, 3 * width // 2 + 128),
-                shape_of(part, 3 * width // 2),
-                shape_of(part, width),
-                shape_of(part, width),
-                shape_of(2 * hidden // width * part, width),
+                shape_of(bulk_rows(width, hidden), width),
                 shape_of(seqs, HALF, width),
                 shape_of(seqs, HALF, width),
             ),
             in_specs=[smem_spec()] + [vmem_spec()] * 16,
-            out_specs=(vmem_spec(),) * 7,
+            out_specs=(vmem_spec(),) * 4,
             scratch_shapes=[pltpu.VMEM((part, 3 * width), BF16), pltpu.VMEM((128, 128), F32)],
             compiler_params=params(),
             cost_estimate=cost(3),
@@ -1007,43 +1019,41 @@
             *[vector.reshape(1, part) for vector in vectors],
             inner_bias.reshape(4, part),
         )
-        lead, mid = (Gather(None, packed[k], packed[k + 1]) for k in (0, 2))
-        tick = jnp.zeros((8, 128), F32)
-        tick = anchor(after(tick, packed[0]))
+        lead = Gather(packed[0])
+        bulk = lax.all_gather(packed[1], "shard", axis=0, tiled=True)
         lead.turn()
-        bulk = lax.all_gather(after(packed[4], lead.along), "shard", axis=0, tiled=True)
-        tick = anchor(after(tick, lead.along))
-        lead.cross(tick)
-        tick = anchor(after(tick, lead.across))
+        lead.cross()
+        tick = after(jnp.zeros((8, 128), F32), lead.across)
         lead.rep()
-        tok_low = shift(after(packed[5], tick), 1).reshape(seqs * HALF, width)
-        tok_high = shift(after(packed[6], tick), -1).reshape(seqs * HALF, width)
-        mid.turn(tick)
-        tick = anchor(after(tick, lead.second, mid.along))
-        lead, lead_table = lead.cores(tick)
-        mid.cross(tick)
+        tok_low = shift(after(packed[2], tick), 1).reshape(seqs * HALF, width)
+        tok_high = shift(after(packed[3], tick), -1).reshape(seqs * HALF, width)
+        lead, lead_table = lead.cores(tok_low, tok_high)
     else:
         tok_low = shift(tokens[:, tok_span - HALF :], 1).reshape(seqs * HALF, width)
         tok_high = shift(tokens[:, :HALF], -1).reshape(seqs * HALF, width)
         small = jnp.concatenate(vectors + [conv_taps.reshape(-1), inner_bias]).reshape(SMALL, part).T
         small = jnp.pad(small, ((0, 0), (0, 128 - SMALL)))
         lead, lead_table = plain_gather(jnp.concatenate([query_proj, key_proj, value_proj], axis=1), small)
-        mid, mid_table = plain_gather(jnp.concatenate([pooled_query, output_proj], axis=1))
+        square = [
+            lax.all_gather(block_rows, "shard", axis=0, tiled=True).reshape(SLOTS, block, width)
+            for block_rows in (pooled_query, output_proj)
+        ]
         full = lax.all_gather(inner_proj, "shard", axis=0, tiled=True)
         full = full.reshape(SLOTS, block, hidden // width, width).transpose(0, 2, 1, 3)
         full = full.reshape(SLOTS, hidden // SLOTS, width)
         down = lax.all_gather(outer_proj, "shard", axis=0, tiled=True)
-        bulk = jnp.concatenate([full, down.reshape(SLOTS, hidden // SLOTS, width)], axis=1).reshape(-1, width)
-
-    row = jnp.arange(tok_span, dtype=jnp.int32)[:, None]
-    lane = jnp.arange(WINDOW, dtype=jnp.int32)[None, :]
-    query_ids = lax.dynamic_slice_in_dim(block_ids, device_index * tok_span, tok_span, 1)[:, :, None]
+        down = down.reshape(SLOTS, hidden // SLOTS, width)
+        bulk = jnp.concatenate(square + [full, down], axis=1).reshape(-1, width)
+
+    query = jnp.arange(tok_span, dtype=jnp.int32)[None, :]
+    slot = jnp.arange(WINDOW, dtype=jnp.int32)[:, None]
+    query_ids = lax.dynamic_slice_in_dim(block_ids, device_index * tok_span, tok_span, 1)[:, None, :]
 
     def bias_for(ids, start, length, step, reach):
         ids = lax.dynamic_slice_in_dim(jnp.pad(ids, ((0, 0), (reach, reach + WINDOW))), start, WIDE, 1)
-        near = lane >= row // step
-        place = start - reach + jnp.where(near, lane, lane + WINDOW)
-        key_ids = jnp.where(near[None], ids[:, None, :WINDOW], ids[:, None, WINDOW:])
+        near = slot >= query // step
+        place = start - reach + jnp.where(near, slot, slot + WINDOW)
+        key_ids = jnp.where(near[None], ids[:, :WINDOW, None], ids[:, WINDOW:, None])
         allowed = ((place >= 0) & (place < length))[None] & (key_ids <= query_ids)
         return jnp.where(allowed, 0.0, neg_fill)
 
@@ -1053,45 +1063,40 @@
     )
 
     n_lead = len(lead)
-    xext, queries, pairs, pooled, vecs = pl.pallas_call(
+    queries, pairs, pooled, vecs = pl.pallas_call(
         functools.partial(project_kernel, lead_table),
         out_shape=(
-            shape_of(seqs * WIDE, width),
             shape_of(rows, width),
             shape_of(seqs * WIDE, 2 * width),
             shape_of(seqs * pools, 2 * width),
             shape_of(24, width, dtype=F32),
         ),
-        in_specs=[smem_spec()] + [vmem_spec()] * 3 + [any_spec()] * n_lead,
-        out_specs=(vmem_spec(),) * 5,
+        in_specs=[smem_spec()] + [vmem_spec()] * 3 + [hbm_spec()] * n_lead,
+        out_specs=(vmem_spec(),) * 4,
         scratch_shapes=[
+            pltpu.VMEM((seqs * WIDE, width), BF16),
             pltpu.VMEM((width, 3 * width), BF16),
             pltpu.VMEM((width, 128), BF16),
             pltpu.SemaphoreType.DMA,
         ],
-        compiler_params=params(),
+        compiler_params=params(54),
         cost_estimate=cost(15),
         name="project",
     )(order, tok, tok_low, tok_high, *lead)
     bias_in = vecs[BIAS_ROW:SMALL].reshape(4, device_count, part).transpose(1, 0, 2).reshape(1, hidden)
 
-    if direct():
-        mid.rep(pooled)
-        mid, mid_table = mid.cores()
     pool_away = swap(pooled)
     pool_far = hop(pooled, True)
     pool_near = hop(pooled, False)
-    pool_cross = swap(pool_near)
-    pool_blocks = (pooled, pool_away, pool_cross, pool_near, pool_far)
     places = jnp.where(
         core == 0, jnp.array([2, 3, 1, 4, 0], jnp.int32), jnp.array([2, 1, 3, 0, 4], jnp.int32)
     )
 
     seq_block = lambda r, c: pl.BlockSpec((r, c), lambda s: (s, 0))
     whole_block = lambda r, c: pl.BlockSpec((r, c), lambda s: (0, 0))
-    bias_block = pl.BlockSpec((1, tok_span, WINDOW), lambda s: (s, 0, 0))
-    prob_block = pl.BlockSpec((1, n_pair, 2 * tok_span, WINDOW), lambda s: (s, 0, 0, 0))
-    prob_shape = shape_of(seqs, n_pair, 2 * tok_span, WINDOW)
+    bias_block = pl.BlockSpec((1, WINDOW, tok_span), lambda s: (s, 0, 0))
+    prob_block = pl.BlockSpec((1, n_pair, WINDOW, 2 * tok_span), lambda s: (s, 0, 0, 0))
+    prob_shape = shape_of(seqs, n_pair, WINDOW, 2 * tok_span)
 
     attended, probs_one = pl.pallas_call(
         window_kernel,
@@ -1099,45 +1104,45 @@
         out_shape=(shape_of(rows, width), prob_shape),
         in_specs=[seq_block(tok_span, width), seq_block(WIDE, 2 * width), bias_block],
         out_specs=(seq_block(tok_span, width), prob_block),
-        compiler_params=params(),
+        compiler_params=params(12),
         cost_estimate=cost(10),
         name="window",
     )(queries, pairs, bias_one)
 
-    n_mid = len(mid)
+    pool_near = after(pool_near, attended)
+    pool_blocks = (pooled, pool_away, swap(pool_near), pool_near, pool_far)
     pool_specs = [seq_block(pools, 2 * width)] * 5
-    second, mixed, probs_two = pl.pallas_call(
-        functools.partial(pooled_kernel, mid_table),
+    second, mixed, probs_two, pooled_weights = pl.pallas_call(
+        pooled_kernel,
         grid=(seqs,),
-        out_shape=(shape_of(rows, width), shape_of(rows, width), prob_shape),
-        in_specs=[smem_spec(), smem_spec(), whole_block(rows, width), bias_block]
-        + pool_specs
-        + [any_spec()] * n_mid,
-        out_specs=(whole_block(rows, width), seq_block(tok_span, width), prob_block),
-        scratch_shapes=[
-            pltpu.VMEM((WIDE, 2 * width), BF16),
-            pltpu.VMEM((width, width), BF16),
-            pltpu.SemaphoreType.DMA,
-        ],
-        compiler_params=params(),
+        out_shape=(shape_of(rows, width), shape_of(rows, width), prob_shape, shape_of(width, width)),
+        in_specs=[smem_spec(), whole_block(rows, width), bias_block, hbm_spec()] + pool_specs,
+        out_specs=(
+            whole_block(rows, width),
+            seq_block(tok_span, width),
+            prob_block,
+            whole_block(width, width),
+        ),
+        scratch_shapes=[pltpu.VMEM((WIDE, 2 * width), BF16), pltpu.SemaphoreType.DMA],
+        compiler_params=params(54),
         cost_estimate=cost(14),
         name="pooled",
-    )(order, places, attended, bias_two, *pool_blocks, *mid)
+    )(places, attended, bias_two, bulk, *pool_blocks)
 
     each = 2 * hidden // SLOTS + SMALL_ROWS
-    result, grad_resid, grad_attn, grad_bulk, _ = pl.pallas_call(
-        functools.partial(feed_kernel, mid_table),
+    result, grad_resid, grad_attn, grad_bulk, out_weights, _ = pl.pallas_call(
+        feed_kernel,
         out_shape=(
             shape_of(rows, width),
             shape_of(rows, width, dtype=F32),
             shape_of(rows, width),
             shape_of(SLOTS * each, width),
+            shape_of(width, width),
             shape_of(8, width, dtype=F32),
         ),
-        in_specs=[smem_spec()] + [vmem_spec()] * 5 + [any_spec()] * (1 + n_mid),
-        out_specs=(vmem_spec(),) * 3 + (any_spec(), vmem_spec()),
+        in_specs=[vmem_spec()] * 5 + [hbm_spec()],
+        out_specs=(vmem_spec(),) * 3 + (any_spec(), vmem_spec(), vmem_spec()),
         scratch_shapes=[
-            pltpu.VMEM((width, width), BF16),
             pltpu.VMEM((width, hidden), BF16),
             pltpu.VMEM((hidden, width), BF16),
             pltpu.VMEM((rows, width), F32),
@@ -1154,16 +1159,16 @@
             pltpu.VMEM((SLOTS, SMALL_ROWS, width), BF16),
             pltpu.SemaphoreType.DMA((4,)),
         ],
-        compiler_params=params(),
+        compiler_params=params(58),
         cost_estimate=cost(45),
         name="feed",
-    )(order, tok, mixed, cot, vecs, bias_in, bulk, *mid)
+    )(tok, mixed, cot, vecs, bias_in, bulk)
     if direct():
         own_bulk = lax.psum_scatter(grad_bulk, "shard", scatter_dimension=0, tiled=True)
 
     back_shape = shape_of(seqs * pools, 2 * width)
     grad_mixed, grad_second, grad_out, pg_own, pg_away, pg_near, pg_far = pl.pallas_call(
-        functools.partial(pooled_back_kernel, mid_table),
+        pooled_back_kernel,
         grid=(seqs,),
         out_shape=(
             shape_of(rows, width, dtype=F32),
@@ -1176,14 +1181,13 @@
         ),
         in_specs=[
             smem_spec(),
-            smem_spec(),
             whole_block(rows, width),
             whole_block(rows, width),
             seq_block(tok_span, width),
             prob_block,
+            whole_block(width, width),
         ]
-        + pool_specs
-        + [any_spec()] * n_mid,
+        + pool_specs,
         out_specs=(
             whole_block(rows, width),
             seq_block(tok_span, width),
@@ -1197,43 +1201,54 @@
             pltpu.VMEM((WIDE, 2 * width), BF16),
             pltpu.VMEM((WIDE, 2 * width), F32),
             pltpu.VMEM((rows, width), BF16),
-            pltpu.VMEM((width, width), BF16),
-            pltpu.SemaphoreType.DMA,
         ],
-        compiler_params=params(),
+        compiler_params=params(24),
         cost_estimate=cost(22),
         name="pooled_back",
-    )(order, places, grad_attn, mixed, second, probs_two, *pool_blocks, *mid)
+    )(places, grad_attn, mixed, second, probs_two, out_weights, *pool_blocks)
 
     pg_cross = swap(pg_away)
-    back_far = lax.ppermute(pg_far, "shard", back_route(device_count, True))
     pg_near = (pg_near.astype(F32) + pg_cross[1].astype(F32)).astype(BF16)
     back_near = lax.ppermute(pg_near, "shard", back_route(device_count, False))
+    back_far = lax.ppermute(pg_far, "shard", back_route(device_count, True))
+    grad_second = after(grad_second, pg_near)
 
     grad_queries, grad_pairs, grad_pooled = pl.pallas_call(
-        functools.partial(window_back_kernel, mid_table),
+        window_back_kernel,
         grid=(seqs,),
         out_shape=(shape_of(rows, width), shape_of(seqs * WIDE, 2 * width), shape_of(width, width)),
         in_specs=[
-            smem_spec(),
             whole_block(rows, width),
             whole_block(rows, width),
             whole_block(rows, width),
             seq_block(tok_span, width),
             seq_block(WIDE, 2 * width),
             prob_block,
-        ]
-        + [any_spec()] * n_mid,
+            whole_block(width, width),
+        ],
         out_specs=(seq_block(tok_span, width), seq_block(WIDE, 2 * width), whole_block(width, width)),
+        scratch_shapes=[pltpu.VMEM((rows, width), BF16)],
+        compiler_params=params(24),
+        cost_estimate=cost(22),
+        name="window_back",
+    )(grad_mixed, grad_second, attended, queries, pairs, probs_one, pooled_weights)
+
+    lead_shape = shape_of(2, 4, block, 5 * width + 128)
+    lead_keep, lead_give = pl.pallas_call(
+        query_grad_kernel,
+        out_shape=(lead_shape, lead_shape),
+        in_specs=[smem_spec()] + [vmem_spec()] * 4,
+        out_specs=(any_spec(),) * 2,
         scratch_shapes=[
-            pltpu.VMEM((rows, width), BF16),
+            pltpu.VMEM((width, rows), BF16),
             pltpu.VMEM((width, width), BF16),
             pltpu.SemaphoreType.DMA,
         ],
-        compiler_params=params(),
-        cost_estimate=cost(22),
-        name="window_back",
-    )(order, grad_mixed, grad_second, attended, queries, pairs, probs_one, *mid)
+        compiler_params=params(16),
+        cost_estimate=cost(5),
+        name="query_grad",
+    )(order, tok, grad_queries, grad_pooled, grad_out)
+    vecs = after(vecs, lead_keep)
 
     pair_total, tap_grads, edges = pl.pallas_call(
         functools.partial(conv_back_kernel, lead_table),
@@ -1242,14 +1257,14 @@
             shape_of(16, width, dtype=F32),
             shape_of(2 * seqs * HALF, width),
         ),
-        in_specs=[smem_spec()] + [vmem_spec()] * 7 + [any_spec()] * n_lead,
+        in_specs=[smem_spec()] + [vmem_spec()] * 7 + [hbm_spec()] * n_lead,
         out_specs=(vmem_spec(),) * 3,
         scratch_shapes=[
             pltpu.VMEM((width, 3 * width), BF16),
             pltpu.VMEM((2 * seqs * HALF, 2 * width), BF16),
             pltpu.SemaphoreType.DMA,
         ],
-        compiler_params=params(),
+        compiler_params=params(34),
         cost_estimate=cost(12),
         name="conv_back",
     )(order, pg_own, pg_cross[0], back_near, back_far, vecs, pairs, grad_pairs, *lead)
@@ -1257,45 +1272,47 @@
     edge_high = shift(edges[: seqs * HALF], -1)
     edge_low = shift(edges[seqs * HALF :], 1)
 
-    lead_shape = shape_of(2, 4, block, 5 * width + 128)
     lead_keep, lead_give = pl.pallas_call(
         weight_grad_kernel,
         out_shape=(lead_shape, lead_shape),
-        in_specs=[smem_spec()] + [vmem_spec()] * 7,
+        in_specs=[smem_spec()] + [vmem_spec()] * 5 + [any_spec()] * 2,
         out_specs=(any_spec(),) * 2,
+        input_output_aliases={6: 0, 7: 1},
         scratch_shapes=[
-            pltpu.VMEM((width, rows), BF16),
             pltpu.VMEM((width, seqs * WIDE), BF16),
-            pltpu.VMEM((width, 3 * width), BF16),
+            pltpu.VMEM((width, 2 * width), BF16),
             pltpu.VMEM((width, 128), BF16),
             pltpu.SemaphoreType.DMA,
         ],
-        compiler_params=params(),
-        cost_estimate=cost(14),
+        compiler_params=params(32),
+        cost_estimate=cost(10),
         name="weight_grad",
-    )(order, tok, xext, grad_queries, pair_total, tap_grads, grad_pooled, grad_out)
+    )(order, tok, tok_low, tok_high, pair_total, tap_grads, lead_keep, lead_give)
+    lead_give = after(lead_give, edge_low, edge_high)
     pieces = tuple((k * width, width) for k in range(5)) + ((5 * width, 128),)
     lead_sum = Scatter(lead_keep, lead_give, order, 14 * 128, pieces)
     if direct():
-        grad_resid = after(grad_resid, lead_sum.split())
+        lead_sum.split()
+        edge_low = after(edge_low, lead_sum.b_keep)
 
     tokens_grad = pl.pallas_call(
         functools.partial(token_grad_kernel, lead_table),
         out_shape=shape_of(rows, width, dtype=F32),
-        in_specs=[smem_spec()] + [vmem_spec()] * 5 + [any_spec()] * n_lead,
+        in_specs=[smem_spec()] + [vmem_spec()] * 5 + [hbm_spec()] * n_lead,
         out_specs=vmem_spec(),
         scratch_shapes=[
             pltpu.VMEM((width, 3 * width), BF16),
             pltpu.VMEM((rows, 3 * width), BF16),
             pltpu.SemaphoreType.DMA,
         ],
-        compiler_params=params(),
+        compiler_params=params(30),
         cost_estimate=cost(11),
         name="token_grad",
     )(order, grad_resid, grad_queries, pair_total, edge_low, edge_high, *lead)
 
     folds = hidden // width
     if direct():
+        lead_sum.a_keep = after(lead_sum.a_keep, tokens_grad)
         lead_sum.fold()
         lead_sum.join()
         lead_sum.gather()
@@ -1308,7 +1325,7 @@
             ),
             in_specs=[vmem_spec()] * 2,
             out_specs=(vmem_spec(),) * 3,
-            compiler_params=params(),
+            compiler_params=params(10),
             cost_estimate=cost(2),
             name="bulk_final",
         )(own_bulk, other(own_bulk))

time: 418 us -> 383 us (0.916); the launches traced: 417 us -> 377 us
  Pallas kernels: 186 us -> 141 us
  starting transfers between devices: 83.2 us -> 69.2 us
  waiting for transfers between devices: 105 us -> 119 us
  local copies, waits for them, and re-layouts: 23.5 us -> 29.7 us
    ppermute x4 -> x3, waiting for transfers between devices: 37.4 us -> 18 us  [flip(): return lax.ppermute(block, 'shard', [(i, i ^ 2) for i in range(SLOTS)])]
    ppermute x1, starting transfers between devices: 23.6 us -> 6.87 us  [shards(): back_near = lax.ppermute(pg_near, 'shard', back_route(device_count, False))]
    pallas_call x4 -> x15, Pallas kernels: 104 us -> 89.1 us  [the longest x1 45.2 us: shards(): pl.pallas_call(feed_kernel, out_shape=(shape_of(rows, width), shape_of(ro...]
    ppermute x8 -> x6, starting transfers between devices: 3.09 us -> 16.2 us  [swap(): lax.ppermute(block, 'shard', [(i, i ^ 1) for i in range(lax.axis_size('sh...]
    reduce_scatter x1, waiting for transfers between devices: 0.02 us -> 12.1 us  [shards(): lax.psum_scatter(grad_bulk, 'shard', scatter_dimension=0, tiled=True)]
    unnamed x66 -> x98, local copies, waits for them, and re-layouts: 12.3 us -> 24.3 us
    all_gather x1, waiting for transfers between devices: 0.02 us -> 10.9 us  [shards(): bulk = lax.all_gather(packed[1], 'shard', axis=0, tiled=True)]
    ppermute x9 -> x6, waiting for transfers between devices: 32.4 us -> 22.1 us  [turn(): lax.ppermute(block, 'shard', [(i, (i - 4 * step) % SLOTS) for i in range(...]
  transfers between devices with their start and end apart: 36 -> 29, of which waited for: 16 -> 17; matrix products, arithmetic and copies ran while one was open for 3% -> 2% of each run, Pallas kernels for 33% -> 21%
where the time goes in v3:
time: 383 us; the launch traced here: 377 us
  Pallas kernels  141 us (37%)
  waiting for transfers between devices  119 us (31%)
  starting transfers between devices  69.2 us (18%)
  local copies, waits for them, and re-layouts  29.7 us (8%)
  between operations  14.8 us (4%)
    pallas_call x1, Pallas kernels, shards(): pl.pallas_call(feed_kernel, out_shape=(shape_of(rows, width), shape_of(ro...  45.2 us
    ppermute x4, waiting for transfers between devices, other(): return lax.ppermute(block, 'rep', [(0, 1), (1, 0)])  28.6 us
    unnamed x98, local copies, waits for them, and re-layouts  24.3 us
    ppermute x6, waiting for transfers between devices, turn(): lax.ppermute(block, 'shard', [(i, (i - 4 * step) % SLOTS) for i in range(...  22.1 us
    ppermute x3, waiting for transfers between devices, flip(): return lax.ppermute(block, 'shard', [(i, i ^ 2) for i in range(SLOTS)])  18 us
    ppermute x1, waiting for transfers between devices, shards(): back_near = lax.ppermute(pg_near, 'shard', back_route(device_count, False))  16.8 us
    ppermute x6, starting transfers between devices, swap(): lax.ppermute(block, 'shard', [(i, i ^ 1) for i in range(lax.axis_size('sh...  16.2 us
    pallas_call x1, Pallas kernels, shards(): pl.pallas_call(pooled_back_kernel, grid=(seqs,), out_shape=(shape_of(rows...  14.6 us
  transfers between devices with their start and end apart: 29, of which 17 were waited for; matrix products, arithmetic and copies ran while one was open for 2% of the time, Pallas kernels for 21%

profile of v3, /device:TPU:0, one launch (start us, length us, event | category | flops | bytes accessed | tf_op | source)
XLA Modules:
  0.0 377.2 jit_solution(248605780470962676)
XLA Ops:
  9.2 3.0 pack.1
  12.2 3.1 collective-permute-start.2
  15.3 2.6 collective-permute-start.1
  20.1 1.6 collective-permute-done.2
  21.7 4.4 %collective-permute-done.1 = bf16[48,1280]{1,0:T(8,128)(2,1)S(1)} collective-permute-done((bf16[48,1280]{1,0:T(8,128)(2,1)}, bf16[48,1280]{1,0:T(8,128)(2,1)S(1)}, u32[]{:S(2)}, u32[]{:S(2)}) %collective-permute-start.1) | collective-permute-done | bytes 122912 | tf_op jit(solution)/shard_map/ppermute | solution.py:677
  27.2 1.6 collective-permute-start.3
  28.8 15.5 %collective-permute-done.3.refs_1_ = bf16[4,48,1280]{2,1,0:T(8,128)(2,1)S(1)} collective-permute-done((bf16[4,48,1280]{2,1,0:T(8,128)(2,1)S(1)}, bf16[4,48,1280]{2,1,0:T(8,128)(2,1)S(1)}, u32[]{:S(2)}, u32[]{:S(2)}) %collective-permute-start.3) | collective-permute-done | bytes 491552 | tf_op jit(solution)/shard_map/ppermute | solution.py:681
  44.3 1.5 collective-permute-start.6
  45.9 1.5 collective-permute-start.4
  48.7 1.7 collective-permute-start.7
  51.9 16.0 %collective-permute-done.6.refs_0_ = bf16[8,48,1280]{2,1,0:T(8,128)(2,1)S(1)} collective-permute-done((bf16[8,48,1280]{2,1,0:T(8,128)(2,1)S(1)}, bf16[8,48,1280]{2,1,0:T(8,128)(2,1)S(1)}, u32[]{:S(2)}, u32[]{:S(2)}) %collective-permute-start.6) | collective-permute-done | bytes 983072 | tf_op jit(solution)/shard_map/ppermute | solution.py:685
  70.7 14.1 %project.1 = (bf16[768,768]{1,0:T(8,128)(2,1)}, bf16[1536,1536]{1,0:T(8,128)(2,1)}, bf16[192,1536]{1,0:T(8,128)(2,1)}, f32[24,768]{1,0:T(8,128)}) custom-call(s32[17]{0:T(128)} %pad_add_fusion.order, bf16[768,768]{1,0:T(8,128)(2,1)} %bitcast.48, bf16[384,768]{1,0:T(8,128)(2,1)} %bitcast.56, bf16[384,768]{1,0:T(8,128)(2,1)} %bitcast.59, ...), custom_call_target="tpu_custom_call" | custom-call | flops 825000000 | bytes 2625000 | tf_op jit(solution)/shard_map/project/pallas_call | solution.py:1066
  87.6 10.0 %collective-permute-start.12 = (bf16[192,1536]{1,0:T(8,128)(2,1)}, bf16[192,1536]{1,0:T(8,128)(2,1)S(1)}, u32[]{:S(2)}, u32[]{:S(2)}) collective-permute-start(bf16[192,1536]{1,0:T(8,128)(2,1)} %get-tuple-element.79.refs_0_), channel_id=1, source_target_pairs={{0,2},{2,4},{3,1},{4,6},{5,3},{6,8},{7,5},{8,10},{9,7},{10,12},{11... | collective-permute-start | bytes 1769480 | tf_op jit(solution)/shard_map/ppermute | solution.py:953
  97.7 2.3 copy-done
  101.3 7.1 %window.1 = (bf16[768,768]{1,0:T(8,128)(2,1)S(1)}, bf16[6,6,128,256]{3,2,1,0:T(8,128)(2,1)S(1)}) custom-call(bf16[768,768]{1,0:T(8,128)(2,1)S(1)} %copy-done.18, bf16[1536,1536]{1,0:T(8,128)(2,1)S(1)} %copy-done, f32[6,128,128]{2,1,0:T(8,128)S(1)} %get-tuple-element.158.bias), custom_call_target="tpu_custom_call" | custom-call | flops 550000000 | bytes 1750000 | tf_op jit(solution)/shard_map/window/pallas_call | solution.py:1101
  108.4 1.5 copy-done.27
  114.0 10.9 %all-gather.2.cloned.1.call-done.bulk = bf16[7680,768]{1,0:T(8,128)(2,1)} async-done(((bf16[480,768]{1,0:T(8,128)(2,1)}), bf16[7680,768]{1,0:T(8,128)(2,1)}) %all-gather.2.cloned.1.call-update) | async-done | bytes 11796496 | tf_op jit(solution)/shard_map/all_gather | solution.py:1023
  124.9 12.7 %pooled.3 = (bf16[768,768]{1,0:T(8,128)(2,1)}, bf16[768,768]{1,0:T(8,128)(2,1)}, bf16[6,6,128,256]{3,2,1,0:T(8,128)(2,1)}, bf16[768,768]{1,0:T(8,128)(2,1)}) custom-call(s32[5]{0:T(128)} %broadcast_select_fusion.places, bf16[768,768]{1,0:T(8,128)(2,1)} %copy-done.6, f32[6,128,128]{2,1,0:T(8,128)} %get-tuple-element.157.bias, ...), custom_call_target="tpu_custom_call" | custom-call | flops 770000000 | bytes 2450000 | tf_op jit(solution)/shard_map/pooled/pallas_call | solution.py:1115
  137.6 45.2 %feed.1 = (bf16[768,768]{1,0:T(8,128)(2,1)}, f32[768,768]{1,0:T(8,128)}, bf16[768,768]{1,0:T(8,128)(2,1)}, bf16[6400,768]{1,0:T(8,128)(2,1)}, bf16[768,768]{1,0:T(8,128)(2,1)}, /*index=5*/f32[8,768]{1,0:T(8,128)}) custom-call(bf16[768,768]{1,0:T(8,128)(2,1)} %bitcast.49, bf16[768,768]{1,0:T(8,128)(2,1)} %get-tuple-element.80.mixed, ...), custom_call_target="tpu_custom_call" | custom-call | flops 2475000064 | bytes 7875000 | tf_op jit(solution)/shard_map/feed/pallas_call | solution.py:1133
  185.6 1.7 copy-done.29
  189.8 1.5 copy-done.33
  191.4 14.6 %pooled_back.1 = (f32[768,768]{1,0:T(8,128)S(1)}, bf16[768,768]{1,0:T(8,128)(2,1)S(1)}, bf16[768,768]{1,0:T(8,128)(2,1)S(1)}, bf16[192,1536]{1,0:T(8,128)(2,1)S(...) custom-call(s32[5]{0:T(128)S(1)} %copy-done.39, ...), custom_call_target="tpu_custom_call" | custom-call | flops 1210000000 | bytes 3850000 | tf_op jit(solution)/shard_map/pooled_back/pallas_call | solution.py:1170
  207.7 1.7 collective-permute-done.13
  209.5 6.9 %collective-permute-start.14 = (bf16[192,1536]{1,0:T(8,128)(2,1)S(1)}, bf16[192,1536]{1,0:T(8,128)(2,1)S(1)}, u32[]{:S(2)}, u32[]{:S(2)}) collective-permute-start(bf16[192,1536]{1,0:T(8,128)(2,1)S(1)} %fusion.refs_1_), channel_id=1, source_target_pairs={{3,1},{0,2},{5,3},{2,4},{7,5},{4,6},{9,7},{6,8},{11,9},{8,10},{13,... | collective-permute-start | bytes 1769480 | tf_op jit(solution)/shard_map/ppermute | solution.py:1212
  218.0 13.3 %window_back.1 = (bf16[768,768]{1,0:T(8,128)(2,1)S(1)}, bf16[1536,1536]{1,0:T(8,128)(2,1)S(1)}, bf16[768,768]{1,0:T(8,128)(2,1)S(1)}) custom-call(f32[768,768]{1,0:T(8,128)S(1)} %get-tuple-element.88.grad_mixed, bf16[768,768]{1,0:T(8,128)(2,1)S(1)} %gate.15.grad_second, bf16[768,768]{1,0:T(8,128)(2,1)S(1)} %copy-done.7, bf16[768,768]{1,0:T(8,128)(2,1)S(1)} %copy-done.19, ...), custom_call_target="tpu_custom_call" | custom-call | flops 1210000000 | bytes 3850000 | tf_op jit(solution)/shard_map/window_back/pallas_call | solution.py:1216
  231.4 3.3 query_grad.1
  234.7 16.8 %collective-permute-done.14.near = bf16[192,1536]{1,0:T(8,128)(2,1)S(1)} collective-permute-done((bf16[192,1536]{1,0:T(8,128)(2,1)S(1)}, bf16[192,1536]{1,0:T(8,128)(2,1)S(1)}, u32[]{:S(2)}, u32[]{:S(2)}) %collective-permute-start.14) | collective-permute-done | bytes 589856 | tf_op jit(solution)/shard_map/ppermute | solution.py:1212
  251.5 8.8 %conv_back.1 = (bf16[1536,1536]{1,0:T(8,128)(2,1)S(1)}, f32[16,768]{1,0:T(8,128)S(1)}, bf16[768,768]{1,0:T(8,128)(2,1)S(1)}) custom-call(s32[17]{0:T(128)S(1)} %copy-done.38, bf16[192,1536]{1,0:T(8,128)(2,1)S(1)} %get-tuple-element.95.own, bf16[192,1536]{1,0:T(8,128)(2,1)S(1)} %slice_bitcast_fusion.away, bf16[192,1536]{1,0:T(8,128)(2,1)S(1)} %collective-permute-done.14.near, ...), custom_call_target="tpu_custom_call" | custom-call | flops 660000000 | bytes 2100000 | tf_op jit(solution)/shard_map/conv_back/pallas_call | solution.py:1253
  260.3 2.2 copy-done.2
  264.0 3.1 collective-permute-start.16
  267.1 2.5 copy-done.3
  269.6 6.6 %weight_grad.1 = (bf16[2,4,48,3968]{3,2,1,0:T(8,128)(2,1)S(1)}, bf16[2,4,48,3968]{3,2,1,0:T(8,128)(2,1)S(1)}) custom-call(s32[17]{0:T(128)S(1)} %copy-done.38, bf16[768,768]{1,0:T(8,128)(2,1)S(1)} %bitcast.51, bf16[384,768]{1,0:T(8,128)(2,1)S(1)} %bitcast.57, bf16[384,768]{1,0:T(8,128)(2,1)S(1)} %bitcast.60, ...), custom_call_target="tpu_custom_call", output_to_operand_aliasing={{0}: (6, {}), {1}: (7, {})} | custom-call | flops 550000000 | bytes 1750000 | tf_op jit(solution)/shard_map/weight_grad/pallas_call | solution.py:1275
  276.3 13.4 %collective-permute-start.18 = (bf16[2,4,48,3968]{3,2,1,0:T(8,128)(2,1)S(1)}, bf16[2,4,48,3968]{3,2,1,0:T(8,128)(2,1)S(1)}, u32[]{:S(2)}, u32[]{:S(2)}) collective-permute-start(bf16[2,4,48,3968]{3,2,1,0:T(8,128)(2,1)S(1)} %gate.17), channel_id=1, source_target_pairs={{0,1},{1,0},{2,3},{3,2},{4,5},{5,4},{6,7},{7,6},{8,9},{9,8},{10,11... | collective-permute-start | bytes 9142280 | tf_op jit(solution)/shard_map/ppermute | solution.py:947
  289.7 5.1 %collective-permute-done.18.arrived = bf16[2,4,48,3968]{3,2,1,0:T(8,128)(2,1)S(1)} collective-permute-done((bf16[2,4,48,3968]{3,2,1,0:T(8,128)(2,1)S(1)}, bf16[2,4,48,3968]{3,2,1,0:T(8,128)(2,1)S(1)}, u32[]{:S(2)}, u32[]{:S(2)}) %collective-permute-start.18) | collective-permute-done | bytes 3047456 | tf_op jit(solution)/shard_map/ppermute | solution.py:947
  294.9 2.5 split.1
  298.5 2.7 collective-permute-start.21
  301.2 7.1 %token_grad.1.refs_1_ = f32[768,768]{1,0:T(8,128)} custom-call(s32[17]{0:T(128)S(1)} %copy-done.38, f32[768,768]{1,0:T(8,128)S(1)} %copy-done.21, bf16[768,768]{1,0:T(8,128)(2,1)S(1)} %get-tuple-element.94.grad_queries, bf16[1536,1536]{1,0:T(8,128)(2,1)S(1)} %bitcast.53, bf16[384,768]{1,0:T(8,128)(2,1)S(1)} %gate.18.low, ...), custom_call_target="tpu_custom_call" | custom-call | flops 605000000 | bytes 1925000 | tf_op jit(solution)/shard_map/token_grad/pallas_call | solution.py:1298
  308.3 1.7 copy-done.10
  310.0 5.1 %collective-permute-done.19.arrived = bf16[2,4,48,896]{3,2,1,0:T(8,128)(2,1)S(1)} collective-permute-done((bf16[2,4,48,896]{3,2,1,0:T(8,128)(2,1)S(1)}, bf16[2,4,48,896]{3,2,1,0:T(8,128)(2,1)S(1)}, u32[]{:S(2)}, u32[]{:S(2)}) %collective-permute-start.19) | collective-permute-done | bytes 688160 | tf_op jit(solution)/shard_map/ppermute | solution.py:685
  315.4 2.6 collective-permute-start.20
  318.0 12.1 %reduce-scatter.2.cloned.1.call-done.own = bf16[400,768]{1,0:T(8,128)(2,1)} async-done(((bf16[6400,768]{1,0:T(8,128)(2,1)}), bf16[400,768]{1,0:T(8,128)(2,1)}) %reduce-scatter.2.cloned.1.call-update) | async-done | bytes 614416 | tf_op jit(solution)/shard_map/reduce_scatter | solution.py:1167
  331.5 2.5 collective-permute-done.20.x_arrived
  334.1 2.7 collective-permute-start.22
  338.1 2.8 collective-permute-start.24
  340.9 5.2 %collective-permute-done.22.first = bf16[48,3072]{1,0:T(8,128)(2,1)S(1)} collective-permute-done((bf16[48,3072]{1,0:T(8,128)(2,1)S(1)}, bf16[48,3072]{1,0:T(8,128)(2,1)S(1)}, u32[]{:S(2)}, u32[]{:S(2)}) %collective-permute-start.22) | collective-permute-done | bytes 294944 | tf_op jit(solution)/shard_map/ppermute | solution.py:677
  346.1 10.9 %collective-permute-done.23.second = bf16[48,3072]{1,0:T(8,128)(2,1)S(1)} collective-permute-done((bf16[48,3072]{1,0:T(8,128)(2,1)S(1)}, bf16[48,3072]{1,0:T(8,128)(2,1)S(1)}, u32[]{:S(2)}, u32[]{:S(2)}) %collective-permute-start.23) | collective-permute-done | bytes 294944 | tf_op jit(solution)/shard_map/ppermute | solution.py:677
  358.5 7.5 %collective-permute-done.25.arrived = bf16[48,3072]{1,0:T(8,128)(2,1)S(1)} collective-permute-done((bf16[48,3072]{1,0:T(8,128)(2,1)S(1)}, bf16[48,3072]{1,0:T(8,128)(2,1)S(1)}, u32[]{:S(2)}, u32[]{:S(2)}) %collective-permute-start.25) | collective-permute-done | bytes 294944 | tf_op jit(solution)/shard_map/ppermute | solution.py:685
  366.0 1.4 final.1
  (163 shorter events, 37.8 us)
Async XLA Ops:
  7.2 117.7 %all-gather.2.cloned.1.call-start = ((), (), s32[]{:S(2)}) async-start(), calls=%async_computation.1 | async-start | bytes 12533760 | tf_op jit(solution)/shard_map/all_gather | solution.py:1023
  12.1 318.0 %reduce-scatter.2.cloned.1.call-start = ((), (), s32[]{:S(2)}) async-start(), calls=%async_computation.2 | async-start | bytes 10444800 | tf_op jit(solution)/shard_map/reduce_scatter | solution.py:1167
  12.2 9.6 %collective-permute-start.2 = (bf16[48,1280]{1,0:T(8,128)(2,1)}, bf16[48,1280]{1,0:T(8,128)(2,1)S(1)}, u32[]{:S(2)}, u32[]{:S(2)}) collective-permute-start(bf16[48,1280]{1,0:T(8,128)(2,1)} %get-tuple-element.73), channel_id=1, source_target_pairs={{0,4},{1,5},{2,6},{3,7},{4,8},{5,9},{6,10},{7,11},{8,12},{9,13},{1... | collective-permute-start | bytes 368648 | tf_op jit(solution)/shard_map/ppermute | solution.py:677
  15.3 10.9 %collective-permute-start.1 = (bf16[48,1280]{1,0:T(8,128)(2,1)}, bf16[48,1280]{1,0:T(8,128)(2,1)S(1)}, u32[]{:S(2)}, u32[]{:S(2)}) collective-permute-start(bf16[48,1280]{1,0:T(8,128)(2,1)} %get-tuple-element.73), channel_id=1, source_target_pairs={{0,8},{1,9},{2,10},{3,11},{4,12},{5,13},{6,14},{7,15},{8,0},{9,1},... | collective-permute-start | bytes 368648 | tf_op jit(solution)/shard_map/ppermute | solution.py:677
  17.9 8.3 %collective-permute-start = (bf16[48,1280]{1,0:T(8,128)(2,1)}, bf16[48,1280]{1,0:T(8,128)(2,1)S(1)}, u32[]{:S(2)}, u32[]{:S(2)}) collective-permute-start(bf16[48,1280]{1,0:T(8,128)(2,1)} %get-tuple-element.73), channel_id=1, source_target_pairs={{0,12},{1,13},{2,14},{3,15},{4,0},{5,1},{6,2},{7,3},{8,4},{9,5},{1... | collective-permute-start | bytes 368648 | tf_op jit(solution)/shard_map/ppermute | solution.py:677
  27.2 18.7 %copy-start.37 = (bf16[6,64,768]{2,1,0:T(8,128)(2,1)S(1)}, bf16[6,64,768]{2,1,0:T(8,128)(2,1)}, u32[]{:S(2)}) copy-start(bf16[6,64,768]{2,1,0:T(8,128)(2,1)} %get-tuple-element.74.refs_0_) | copy-start | bytes 1769476
  27.2 17.1 %collective-permute-start.3 = (bf16[4,48,1280]{2,1,0:T(8,128)(2,1)S(1)}, bf16[4,48,1280]{2,1,0:T(8,128)(2,1)S(1)}, u32[]{:S(2)}, u32[]{:S(2)}) collective-permute-start(bf16[4,48,1280]{2,1,0:T(8,128)(2,1)S(1)} %pad_maximum_fusion), channel_id=1, source_target_pairs={{0,2},{1,3},{2,0},{3,1},{4,6},{5,7},{6,4},{7,5},{8,10},{9,11},{10,... | collective-permute-start | bytes 1474568 | tf_op jit(solution)/shard_map/ppermute | solution.py:681
  28.8 17.1 %copy-start.36 = (bf16[6,64,768]{2,1,0:T(8,128)(2,1)S(1)}, bf16[6,64,768]{2,1,0:T(8,128)(2,1)}, u32[]{:S(2)}) copy-start(bf16[6,64,768]{2,1,0:T(8,128)(2,1)} %get-tuple-element.72.refs_0_) | copy-start | bytes 1769476
  44.3 23.6 %collective-permute-start.6 = (bf16[8,48,1280]{2,1,0:T(8,128)(2,1)S(1)}, bf16[8,48,1280]{2,1,0:T(8,128)(2,1)S(1)}, u32[]{:S(2)}, u32[]{:S(2)}) collective-permute-start(bf16[8,48,1280]{2,1,0:T(8,128)(2,1)S(1)} %constant_dynamic-update-slice_fusion.refs_0_), channel_id=1, source_target_pairs={{0,16},{16,0},{1,17},{17,1},{2,18},{18,2},{3,19},{19,3},{4,20},{20... | collective-permute-start | bytes 2949128 | tf_op jit(solution)/shard_map/ppermute | solution.py:685
  45.9 4.6 %collective-permute-start.4 = (bf16[6,64,768]{2,1,0:T(8,128)(2,1)S(1)}, bf16[6,64,768]{2,1,0:T(8,128)(2,1)S(1)}, u32[]{:S(2)}, u32[]{:S(2)}) collective-permute-start(bf16[6,64,768]{2,1,0:T(8,128)(2,1)S(1)} %gate.11), channel_id=1, source_target_pairs={{0,1},{1,2},{2,3},{3,4},{4,5},{5,6},{6,7},{7,8},{8,9},{9,10},{10,1... | collective-permute-start | bytes 1769480 | tf_op jit(solution)/shard_map/ppermute | solution.py:941
  47.4 4.5 %collective-permute-start.5 = (bf16[6,64,768]{2,1,0:T(8,128)(2,1)S(1)}, bf16[6,64,768]{2,1,0:T(8,128)(2,1)S(1)}, u32[]{:S(2)}, u32[]{:S(2)}) collective-permute-start(bf16[6,64,768]{2,1,0:T(8,128)(2,1)S(1)} %gate.12), channel_id=1, source_target_pairs={{1,0},{2,1},{3,2},{4,3},{5,4},{6,5},{7,6},{8,7},{9,8},{10,9},{11,1... | collective-permute-start | bytes 1769480 | tf_op jit(solution)/shard_map/ppermute | solution.py:941
  48.7 20.6 %collective-permute-start.7 = (bf16[8,48,1280]{2,1,0:T(8,128)(2,1)S(1)}, bf16[8,48,1280]{2,1,0:T(8,128)(2,1)}, u32[]{:S(2)}, u32[]{:S(2)}) collective-permute-start(bf16[8,48,1280]{2,1,0:T(8,128)(2,1)S(1)} %constant_dynamic-update-slice_fusion.refs_0_), channel_id=1, source_target_pairs={{0,1},{1,0},{2,3},{3,2},{4,5},{5,4},{6,7},{7,6},{8,9},{9,8},{10,11... | collective-permute-start | bytes 2949128 | tf_op jit(solution)/shard_map/ppermute | solution.py:947
  50.5 17.4 %copy-start.11 = (bf16[6,64,768]{2,1,0:T(8,128)(2,1)}, bf16[6,64,768]{2,1,0:T(8,128)(2,1)S(1)}, u32[]{:S(2)}) copy-start(bf16[6,64,768]{2,1,0:T(8,128)(2,1)S(1)} %collective-permute-done.4) | copy-start | bytes 1769476
  51.9 16.1 %copy-start.13 = (bf16[6,64,768]{2,1,0:T(8,128)(2,1)}, bf16[6,64,768]{2,1,0:T(8,128)(2,1)S(1)}, u32[]{:S(2)}) copy-start(bf16[6,64,768]{2,1,0:T(8,128)(2,1)S(1)} %collective-permute-done.5) | copy-start | bytes 1769476
  68.0 2.8 collective-permute-start.8
  84.9 25.0 %collective-permute-start.10 = (bf16[192,1536]{1,0:T(8,128)(2,1)}, bf16[192,1536]{1,0:T(8,128)(2,1)S(1)}, u32[]{:S(2)}, u32[]{:S(2)}) collective-permute-start(bf16[192,1536]{1,0:T(8,128)(2,1)} %get-tuple-element.79.refs_0_), channel_id=1, source_target_pairs={{1,3},{2,0},{3,5},{4,2},{5,7},{6,4},{7,9},{8,6},{9,11},{10,8},{11,... | collective-permute-start | bytes 1769480 | tf_op jit(solution)/shard_map/ppermute | solution.py:953
  87.6 25.9 %collective-permute-start.12 = (bf16[192,1536]{1,0:T(8,128)(2,1)}, bf16[192,1536]{1,0:T(8,128)(2,1)S(1)}, u32[]{:S(2)}, u32[]{:S(2)}) collective-permute-start(bf16[192,1536]{1,0:T(8,128)(2,1)} %get-tuple-element.79.refs_0_), channel_id=1, source_target_pairs={{0,2},{2,4},{3,1},{4,6},{5,3},{6,8},{7,5},{8,10},{9,7},{10,12},{11... | collective-permute-start | bytes 1769480 | tf_op jit(solution)/shard_map/ppermute | solution.py:953
  97.6 15.9 %collective-permute-start.9 = (bf16[192,1536]{1,0:T(8,128)(2,1)}, bf16[192,1536]{1,0:T(8,128)(2,1)S(1)}, u32[]{:S(2)}, u32[]{:S(2)}) collective-permute-start(bf16[192,1536]{1,0:T(8,128)(2,1)} %get-tuple-element.79.refs_0_), channel_id=1, source_target_pairs={{0,1},{1,0},{2,3},{3,2},{4,5},{5,4},{6,7},{7,6},{8,9},{9,8},{10,11... | collective-permute-start | bytes 1769480 | tf_op jit(solution)/shard_map/ppermute | solution.py:947
  110.9 14.0 %copy-start.15 = (bf16[192,1536]{1,0:T(8,128)(2,1)}, bf16[192,1536]{1,0:T(8,128)(2,1)S(1)}, u32[]{:S(2)}) copy-start(bf16[192,1536]{1,0:T(8,128)(2,1)S(1)} %gate.14.refs_3_) | copy-start | bytes 1769476
  110.9 3.0 collective-permute-start.11
  113.5 11.4 %copy-start.23 = (bf16[192,1536]{1,0:T(8,128)(2,1)}, bf16[192,1536]{1,0:T(8,128)(2,1)S(1)}, u32[]{:S(2)}) copy-start(bf16[192,1536]{1,0:T(8,128)(2,1)S(1)} %collective-permute-done.12.refs_4_) | copy-start | bytes 1769476
  113.5 11.4 %copy-start.25 = (bf16[192,1536]{1,0:T(8,128)(2,1)}, bf16[192,1536]{1,0:T(8,128)(2,1)S(1)}, u32[]{:S(2)}) copy-start(bf16[192,1536]{1,0:T(8,128)(2,1)S(1)} %collective-permute-done.9.refs_1_) | copy-start | bytes 1769476
  182.8 33.6 %slice-start = ((s8[4718592]{0:T(1024)(128)(4,1)}), s8[524288]{0:T(1024)(128)(4,1)S(1)}, s32[]{:S(2)}) async-start(s8[4718592]{0:T(1024)(128)(4,1)} %bitcast.46), calls=%async_computation.3 | async-start | bytes 1048576
  191.3 25.1 %slice-start.1 = ((s8[4718592]{0:T(1024)(128)(4,1)}), s8[4194304]{0:T(1024)(128)(4,1)S(1)}, s32[]{:S(2)}) async-start(s8[4718592]{0:T(1024)(128)(4,1)} %bitcast.46), calls=%async_computation.4 | async-start | bytes 8388608
  191.3 25.1 %copy-start.30 = (bf16[768,768]{1,0:T(8,128)(2,1)S(1)}, bf16[768,768]{1,0:T(8,128)(2,1)}, u32[]{:S(2)}) copy-start(bf16[768,768]{1,0:T(8,128)(2,1)} %get-tuple-element.93.weights) | copy-start | bytes 3538948
  206.0 3.4 collective-permute-start.13
  206.4 28.3 %collective-permute-start.15 = (bf16[192,1536]{1,0:T(8,128)(2,1)S(1)}, bf16[192,1536]{1,0:T(8,128)(2,1)S(1)}, u32[]{:S(2)}, u32[]{:S(2)}) collective-permute-start(bf16[192,1536]{1,0:T(8,128)(2,1)S(1)} %get-tuple-element.96), channel_id=1, source_target_pairs={{2,0},{4,2},{1,3},{6,4},{3,5},{8,6},{5,7},{10,8},{7,9},{12,10},{9,... | collective-permute-start | bytes 1769480 | tf_op jit(solution)/shard_map/ppermute | solution.py:1213
  209.4 7.1 %copy-start.28 = (bf16[6,6,128,256]{3,2,1,0:T(8,128)(2,1)S(1)}, bf16[6,6,128,256]{3,2,1,0:T(8,128)(2,1)}, u32[]{:S(2)}) copy-start(bf16[6,6,128,256]{3,2,1,0:T(8,128)(2,1)} %copy-done.27) | copy-start | bytes 7077892
  209.5 42.0 %collective-permute-start.14 = (bf16[192,1536]{1,0:T(8,128)(2,1)S(1)}, bf16[192,1536]{1,0:T(8,128)(2,1)S(1)}, u32[]{:S(2)}, u32[]{:S(2)}) collective-permute-start(bf16[192,1536]{1,0:T(8,128)(2,1)S(1)} %fusion.refs_1_), channel_id=1, source_target_pairs={{3,1},{0,2},{5,3},{2,4},{7,5},{4,6},{9,7},{6,8},{11,9},{8,10},{13,... | collective-permute-start | bytes 1769480 | tf_op jit(solution)/shard_map/ppermute | solution.py:1212
  218.0 13.3 %copy-start.1 = (bf16[6,128,768]{2,1,0:T(8,128)(2,1)S(1)}, bf16[6,128,768]{2,1,0:T(8,128)(2,1)}, u32[]{:S(2)}) copy-start(bf16[6,128,768]{2,1,0:T(8,128)(2,1)} %tokens.1) | copy-start | bytes 3538948
  218.0 13.3 %copy-start.38 = (s32[17]{0:T(128)S(1)}, s32[17]{0:T(128)}, u32[]{:S(2)}) copy-start(s32[17]{0:T(128)} %pad_add_fusion.order) | copy-start | bytes 208
  234.7 16.8 %copy-start.9 = (bf16[8,48,1280]{2,1,0:T(8,128)(2,1)S(1)}, bf16[8,48,1280]{2,1,0:T(8,128)(2,1)}, u32[]{:S(2)}) copy-start(bf16[8,48,1280]{2,1,0:T(8,128)(2,1)} %copy-done.8) | copy-start | bytes 2949124
  234.7 16.8 %copy-start.5 = (bf16[8,48,1280]{2,1,0:T(8,128)(2,1)S(1)}, bf16[8,48,1280]{2,1,0:T(8,128)(2,1)}, u32[]{:S(2)}) copy-start(bf16[8,48,1280]{2,1,0:T(8,128)(2,1)} %copy-done.4) | copy-start | bytes 2949124
  262.6 13.7 %collective-permute-start.17 = (bf16[384,768]{1,0:T(8,128)(2,1)S(1)}, bf16[384,768]{1,0:T(8,128)(2,1)S(1)}, u32[]{:S(2)}, u32[]{:S(2)}) collective-permute-start(bf16[384,768]{1,0:T(8,128)(2,1)S(1)} %get-tuple-element.144), channel_id=1, source_target_pairs={{1,0},{2,1},{3,2},{4,3},{5,4},{6,5},{7,6},{8,7},{9,8},{10,9},{11,1... | collective-permute-start | bytes 1769480 | tf_op jit(solution)/shard_map/ppermute | solution.py:941
  264.0 12.3 %collective-permute-start.16 = (bf16[384,768]{1,0:T(8,128)(2,1)S(1)}, bf16[384,768]{1,0:T(8,128)(2,1)S(1)}, u32[]{:S(2)}, u32[]{:S(2)}) collective-permute-start(bf16[384,768]{1,0:T(8,128)(2,1)S(1)} %get-tuple-element.145), channel_id=1, source_target_pairs={{0,1},{1,2},{2,3},{3,4},{4,5},{5,6},{6,7},{7,8},{8,9},{9,10},{10,1... | collective-permute-start | bytes 1769480 | tf_op jit(solution)/shard_map/ppermute | solution.py:941
  276.3 24.9 %slice-start.2 = ((s8[4718592]{0:T(1024)(128)(4,1)}), s8[4194304]{0:T(1024)(128)(4,1)S(1)}, s32[]{:S(2)}) async-start(s8[4718592]{0:T(1024)(128)(4,1)} %bitcast.52), calls=%async_computation.5 | async-start | bytes 8388608
  276.3 18.6 %collective-permute-start.18 = (bf16[2,4,48,3968]{3,2,1,0:T(8,128)(2,1)S(1)}, bf16[2,4,48,3968]{3,2,1,0:T(8,128)(2,1)S(1)}, u32[]{:S(2)}, u32[]{:S(2)}) collective-permute-start(bf16[2,4,48,3968]{3,2,1,0:T(8,128)(2,1)S(1)} %gate.17), channel_id=1, source_target_pairs={{0,1},{1,0},{2,3},{3,2},{4,5},{5,4},{6,7},{7,6},{8,9},{9,8},{10,11... | collective-permute-start | bytes 9142280 | tf_op jit(solution)/shard_map/ppermute | solution.py:947
  294.9 6.3 %slice-start.3 = ((s8[4718592]{0:T(1024)(128)(4,1)}), s8[524288]{0:T(1024)(128)(4,1)S(1)}, s32[]{:S(2)}) async-start(s8[4718592]{0:T(1024)(128)(4,1)} %bitcast.52), calls=%async_computation.6 | async-start | bytes 1048576
  294.9 6.3 %copy-start.21 = (f32[768,768]{1,0:T(8,128)S(1)}, f32[768,768]{1,0:T(8,128)}, u32[]{:S(2)}) copy-start(f32[768,768]{1,0:T(8,128)} %get-tuple-element.83.grad_resid) | copy-start | bytes 7077892
  297.4 17.7 %collective-permute-start.19 = (bf16[2,4,48,896]{3,2,1,0:T(8,128)(2,1)S(1)}, bf16[2,4,48,896]{3,2,1,0:T(8,128)(2,1)S(1)}, u32[]{:S(2)}, u32[]{:S(2)}) collective-permute-start(bf16[2,4,48,896]{3,2,1,0:T(8,128)(2,1)S(1)} %get-tuple-element.109), channel_id=1, source_target_pairs={{0,16},{16,0},{1,17},{17,1},{2,18},{18,2},{3,19},{19,3},{4,20},{20... | collective-permute-start | bytes 2064392 | tf_op jit(solution)/shard_map/ppermute | solution.py:685
  298.5 33.0 %collective-permute-start.21 = (bf16[4,48,2176]{2,1,0:T(8,128)(2,1)}, bf16[4,48,2176]{2,1,0:T(8,128)(2,1)S(1)}, u32[]{:S(2)}, u32[]{:S(2)}) collective-permute-start(bf16[4,48,2176]{2,1,0:T(8,128)(2,1)} %get-tuple-element.112), channel_id=1, source_target_pairs={{0,2},{1,3},{2,0},{3,1},{4,6},{5,7},{6,4},{7,5},{8,10},{9,11},{10,... | collective-permute-start | bytes 2506760 | tf_op jit(solution)/shard_map/ppermute | solution.py:681
  315.4 18.6 %collective-permute-start.20 = (bf16[4,48,896]{2,1,0:T(8,128)(2,1)S(1)}, bf16[4,48,896]{2,1,0:T(8,128)(2,1)S(1)}, u32[]{:S(2)}, u32[]{:S(2)}) collective-permute-start(bf16[4,48,896]{2,1,0:T(8,128)(2,1)S(1)} %get-tuple-element.111), channel_id=1, source_target_pairs={{0,2},{1,3},{2,0},{3,1},{4,6},{5,7},{6,4},{7,5},{8,10},{9,11},{10,... | collective-permute-start | bytes 1032200 | tf_op jit(solution)/shard_map/ppermute | solution.py:681
  330.1 38.1 %collective-permute-start.26 = (bf16[400,768]{1,0:T(8,128)(2,1)}, bf16[400,768]{1,0:T(8,128)(2,1)S(1)}, u32[]{:S(2)}, u32[]{:S(2)}) collective-permute-start(bf16[400,768]{1,0:T(8,128)(2,1)} %reduce-scatter.2.cloned.1.call-done.own), channel_id=1, source_target_pairs={{0,16},{16,0},{1,17},{17,1},{2,18},{18,2},{3,19},{19,3},{4,20},{20... | collective-permute-start | bytes 1843208 | tf_op jit(solution)/shard_map/ppermute | solution.py:685
  334.1 34.0 %copy-start.35 = (bf16[400,768]{1,0:T(8,128)(2,1)S(1)}, bf16[400,768]{1,0:T(8,128)(2,1)}, u32[]{:S(2)}) copy-start(bf16[400,768]{1,0:T(8,128)(2,1)} %reduce-scatter.2.cloned.1.call-done.own) | copy-start | bytes 1843204
  334.1 11.9 %collective-permute-start.22 = (bf16[48,3072]{1,0:T(8,128)(2,1)S(1)}, bf16[48,3072]{1,0:T(8,128)(2,1)S(1)}, u32[]{:S(2)}, u32[]{:S(2)}) collective-permute-start(bf16[48,3072]{1,0:T(8,128)(2,1)S(1)} %get-tuple-element.114), channel_id=1, source_target_pairs={{0,4},{1,5},{2,6},{3,7},{4,8},{5,9},{6,10},{7,11},{8,12},{9,13},{1... | collective-permute-start | bytes 884744 | tf_op jit(solution)/shard_map/ppermute | solution.py:677
  336.8 20.2 %collective-permute-start.23 = (bf16[48,3072]{1,0:T(8,128)(2,1)S(1)}, bf16[48,3072]{1,0:T(8,128)(2,1)S(1)}, u32[]{:S(2)}, u32[]{:S(2)}) collective-permute-start(bf16[48,3072]{1,0:T(8,128)(2,1)S(1)} %get-tuple-element.115), channel_id=1, source_target_pairs={{0,8},{1,9},{2,10},{3,11},{4,12},{5,13},{6,14},{7,15},{8,0},{9,1},... | collective-permute-start | bytes 884744 | tf_op jit(solution)/shard_map/ppermute | solution.py:677
  338.1 18.9 %collective-permute-start.24 = (bf16[48,3072]{1,0:T(8,128)(2,1)S(1)}, bf16[48,3072]{1,0:T(8,128)(2,1)S(1)}, u32[]{:S(2)}, u32[]{:S(2)}) collective-permute-start(bf16[48,3072]{1,0:T(8,128)(2,1)S(1)} %get-tuple-element.116), channel_id=1, source_target_pairs={{0,12},{1,13},{2,14},{3,15},{4,0},{5,1},{6,2},{7,3},{8,4},{9,5},{1... | collective-permute-start | bytes 884744 | tf_op jit(solution)/shard_map/ppermute | solution.py:677
  357.1 8.9 %collective-permute-start.25 = (bf16[48,3072]{1,0:T(8,128)(2,1)S(1)}, bf16[48,3072]{1,0:T(8,128)(2,1)S(1)}, u32[]{:S(2)}, u32[]{:S(2)}) collective-permute-start(bf16[48,3072]{1,0:T(8,128)(2,1)S(1)} %gather_sum.1.own), channel_id=1, source_target_pairs={{0,16},{16,0},{1,17},{17,1},{2,18},{18,2},{3,19},{19,3},{4,20},{20... | collective-permute-start | bytes 884744 | tf_op jit(solution)/shard_map/ppermute | solution.py:685
  (28 other events, 56.7 us)
Sparse Core Ops, SparseCore 0:
  12.3 112.6 all-gather.1
  183.0 147.0 reduce-scatter.1

commit v4 on v3

--- a/solution.py
+++ b/solution.py
@@ -1202,7 +1202,7 @@
             pltpu.VMEM((WIDE, 2 * width), F32),
             pltpu.VMEM((rows, width), BF16),
         ],
-        compiler_params=params(24),
+        compiler_params=params(20),
         cost_estimate=cost(22),
         name="pooled_back",
     )(places, grad_attn, mixed, second, probs_two, out_weights, *pool_blocks)
@@ -1228,7 +1228,7 @@
         ],
         out_specs=(seq_block(tok_span, width), seq_block(WIDE, 2 * width), whole_block(width, width)),
         scratch_shapes=[pltpu.VMEM((rows, width), BF16)],
-        compiler_params=params(24),
+        compiler_params=params(20),
         cost_estimate=cost(22),
         name="window_back",
     )(grad_mixed, grad_second, attended, queries, pairs, probs_one, pooled_weights)
@@ -1244,7 +1244,7 @@
             pltpu.VMEM((width, width), BF16),
             pltpu.SemaphoreType.DMA,
         ],
-        compiler_params=params(16),
+        compiler_params=params(12),
         cost_estimate=cost(5),
         name="query_grad",
     )(order, tok, grad_queries, grad_pooled, grad_out)
@@ -1264,13 +1264,10 @@
             pltpu.VMEM((2 * seqs * HALF, 2 * width), BF16),
             pltpu.SemaphoreType.DMA,
         ],
-        compiler_params=params(34),
+        compiler_params=params(28),
         cost_estimate=cost(12),
         name="conv_back",
     )(order, pg_own, pg_cross[0], back_near, back_far, vecs, pairs, grad_pairs, *lead)
-
-    edge_high = shift(edges[: seqs * HALF], -1)
-    edge_low = shift(edges[seqs * HALF :], 1)
 
     lead_keep, lead_give = pl.pallas_call(
         weight_grad_kernel,
@@ -1284,16 +1281,17 @@
             pltpu.VMEM((width, 128), BF16),
             pltpu.SemaphoreType.DMA,
         ],
-        compiler_params=params(32),
+        compiler_params=params(18),
         cost_estimate=cost(10),
         name="weight_grad",
     )(order, tok, tok_low, tok_high, pair_total, tap_grads, lead_keep, lead_give)
-    lead_give = after(lead_give, edge_low, edge_high)
     pieces = tuple((k * width, width) for k in range(5)) + ((5 * width, 128),)
-    lead_sum = Scatter(lead_keep, lead_give, order, 14 * 128, pieces)
+    lead_sum = Scatter(lead_keep, lead_give, order, 24 * 128, pieces)
     if direct():
         lead_sum.split()
-        edge_low = after(edge_low, lead_sum.b_keep)
+        edges = after(edges, lead_sum.b_keep)
+    edge_high = shift(edges[: seqs * HALF], -1)
+    edge_low = shift(edges[seqs * HALF :], 1)
 
     tokens_grad = pl.pallas_call(
         functools.partial(token_grad_kernel, lead_table),
@@ -1305,16 +1303,17 @@
             pltpu.VMEM((rows, 3 * width), BF16),
             pltpu.SemaphoreType.DMA,
         ],
-        compiler_params=params(30),
+        compiler_params=params(22),
         cost_estimate=cost(11),
         name="token_grad",
     )(order, grad_resid, grad_queries, pair_total, edge_low, edge_high, *lead)
 
     folds = hidden // width
     if direct():
-        lead_sum.a_keep = after(lead_sum.a_keep, tokens_grad)
+        lead_sum.a_keep = after(lead_sum.a_keep, tokens_grad, lead_sum.b_arrived)
         lead_sum.fold()
         lead_sum.join()
+        own_bulk = after(own_bulk, lead_sum.turned[0])
         lead_sum.gather()
         own_in, own_down, small_own = pl.pallas_call(
             bulk_final_kernel,

time: 383 us -> 366 us (0.956)
  starting transfers between devices: 69.2 us -> 55.5 us
  waiting for transfers between devices: 119 us -> 124 us
  local copies, waits for them, and re-layouts: 29.7 us -> 25 us
    ppermute x3, waiting for transfers between devices: 18 us -> 37.7 us  [flip(): return lax.ppermute(block, 'shard', [(i, i ^ 2) for i in range(SLOTS)])]
    ppermute x6, starting transfers between devices: 16.2 us -> 2.84 us  [swap(): lax.ppermute(block, 'shard', [(i, i ^ 1) for i in range(lax.axis_size('sh...]
    reduce_scatter x1, waiting for transfers between devices: 12.1 us -> 1.95 us  [shards(): lax.psum_scatter(grad_bulk, 'shard', scatter_dimension=0, tiled=True)]
    unnamed x98 -> x86, local copies, waits for them, and re-layouts: 24.3 us -> 19.6 us
where the time goes in v4:
time: 366 us; the launch traced here: 362 us
  Pallas kernels  140 us (38%)
  waiting for transfers between devices  124 us (34%)
  starting transfers between devices  55.5 us (15%)
  local copies, waits for them, and re-layouts  25 us (7%)
  between operations  14.7 us (4%)
  other arithmetic  3.69 us (1%)
    pallas_call x1, Pallas kernels, shards(): pl.pallas_call(feed_kernel, out_shape=(shape_of(rows, width), shape_of(ro...  45.2 us
    ppermute x3, waiting for transfers between devices, flip(): return lax.ppermute(block, 'shard', [(i, i ^ 2) for i in range(SLOTS)])  37.7 us
    ppermute x4, waiting for transfers between devices, other(): return lax.ppermute(block, 'rep', [(0, 1), (1, 0)])  26 us
    ppermute x6, waiting for transfers between devices, turn(): lax.ppermute(block, 'shard', [(i, (i - 4 * step) % SLOTS) for i in range(...  20 us
    unnamed x86, local copies, waits for them, and re-layouts  19.6 us
    ppermute x1, waiting for transfers between devices, shards(): back_near = lax.ppermute(pg_near, 'shard', back_route(device_count, False))  16.7 us
    pallas_call x1, Pallas kernels, shards(): pl.pallas_call(pooled_back_kernel, grid=(seqs,), out_shape=(shape_of(rows...  14.7 us
    pallas_call x1, Pallas kernels, shards(): pl.pallas_call(functools.partial(project_kernel, lead_table), out_shape=(...  14.1 us
  transfers between devices with their start and end apart: 29, of which 17 were waited for; matrix products, arithmetic and copies ran while one was open for 2% of the time, Pallas kernels for 21%

profile of v4, /device:TPU:0, one launch (start us, length us, event | category | flops | bytes accessed | tf_op | source)
XLA Modules:
  0.0 362.3 jit_solution(12554679736032903572)
XLA Ops:
  9.2 3.0 pack.1
  12.2 3.1 collective-permute-start.2
  15.3 2.6 collective-permute-start.1
  20.1 1.6 collective-permute-done.2
  21.7 4.4 %collective-permute-done.1 = bf16[48,1280]{1,0:T(8,128)(2,1)S(1)} collective-permute-done((bf16[48,1280]{1,0:T(8,128)(2,1)}, bf16[48,1280]{1,0:T(8,128)(2,1)S(1)}, u32[]{:S(2)}, u32[]{:S(2)}) %collective-permute-start.1) | collective-permute-done | bytes 122912 | tf_op jit(solution)/shard_map/ppermute | solution.py:677
  27.2 1.6 collective-permute-start.3
  28.8 15.5 %collective-permute-done.3.refs_1_ = bf16[4,48,1280]{2,1,0:T(8,128)(2,1)S(1)} collective-permute-done((bf16[4,48,1280]{2,1,0:T(8,128)(2,1)S(1)}, bf16[4,48,1280]{2,1,0:T(8,128)(2,1)S(1)}, u32[]{:S(2)}, u32[]{:S(2)}) %collective-permute-start.3) | collective-permute-done | bytes 491552 | tf_op jit(solution)/shard_map/ppermute | solution.py:681
  44.3 1.5 collective-permute-start.6
  45.9 1.5 collective-permute-start.4
  48.7 1.7 collective-permute-start.7
  51.9 16.0 %collective-permute-done.6.refs_0_ = bf16[8,48,1280]{2,1,0:T(8,128)(2,1)S(1)} collective-permute-done((bf16[8,48,1280]{2,1,0:T(8,128)(2,1)S(1)}, bf16[8,48,1280]{2,1,0:T(8,128)(2,1)S(1)}, u32[]{:S(2)}, u32[]{:S(2)}) %collective-permute-start.6) | collective-permute-done | bytes 983072 | tf_op jit(solution)/shard_map/ppermute | solution.py:685
  70.7 14.1 %project.1 = (bf16[768,768]{1,0:T(8,128)(2,1)}, bf16[1536,1536]{1,0:T(8,128)(2,1)}, bf16[192,1536]{1,0:T(8,128)(2,1)}, f32[24,768]{1,0:T(8,128)}) custom-call(s32[17]{0:T(128)} %pad_add_fusion.order, bf16[768,768]{1,0:T(8,128)(2,1)} %bitcast.48, bf16[384,768]{1,0:T(8,128)(2,1)} %bitcast.54, bf16[384,768]{1,0:T(8,128)(2,1)} %bitcast.57, ...), custom_call_target="tpu_custom_call" | custom-call | flops 825000000 | bytes 2625000 | tf_op jit(solution)/shard_map/project/pallas_call | solution.py:1066
  87.6 10.0 %collective-permute-start.12 = (bf16[192,1536]{1,0:T(8,128)(2,1)}, bf16[192,1536]{1,0:T(8,128)(2,1)S(1)}, u32[]{:S(2)}, u32[]{:S(2)}) collective-permute-start(bf16[192,1536]{1,0:T(8,128)(2,1)} %get-tuple-element.79.refs_0_), channel_id=1, source_target_pairs={{0,2},{2,4},{3,1},{4,6},{5,3},{6,8},{7,5},{8,10},{9,7},{10,12},{11... | collective-permute-start | bytes 1769480 | tf_op jit(solution)/shard_map/ppermute | solution.py:953
  97.7 2.3 copy-done
  101.3 6.9 %window.1 = (bf16[768,768]{1,0:T(8,128)(2,1)S(1)}, bf16[6,6,128,256]{3,2,1,0:T(8,128)(2,1)S(1)}) custom-call(bf16[768,768]{1,0:T(8,128)(2,1)S(1)} %copy-done.16, bf16[1536,1536]{1,0:T(8,128)(2,1)S(1)} %copy-done, f32[6,128,128]{2,1,0:T(8,128)S(1)} %get-tuple-element.158.bias), custom_call_target="tpu_custom_call" | custom-call | flops 550000000 | bytes 1750000 | tf_op jit(solution)/shard_map/window/pallas_call | solution.py:1101
  108.2 1.5 copy-done.24
  113.4 11.5 %all-gather.2.cloned.1.call-done.bulk = bf16[7680,768]{1,0:T(8,128)(2,1)} async-done(((bf16[480,768]{1,0:T(8,128)(2,1)}), bf16[7680,768]{1,0:T(8,128)(2,1)}) %all-gather.2.cloned.1.call-update) | async-done | bytes 11796496 | tf_op jit(solution)/shard_map/all_gather | solution.py:1023
  124.9 12.7 %pooled.3 = (bf16[768,768]{1,0:T(8,128)(2,1)}, bf16[768,768]{1,0:T(8,128)(2,1)}, bf16[6,6,128,256]{3,2,1,0:T(8,128)(2,1)}, bf16[768,768]{1,0:T(8,128)(2,1)}) custom-call(s32[5]{0:T(128)} %broadcast_select_fusion.places, bf16[768,768]{1,0:T(8,128)(2,1)} %copy-done.4, f32[6,128,128]{2,1,0:T(8,128)} %get-tuple-element.157.bias, ...), custom_call_target="tpu_custom_call" | custom-call | flops 770000000 | bytes 2450000 | tf_op jit(solution)/shard_map/pooled/pallas_call | solution.py:1115
  137.6 45.2 %feed.1 = (bf16[768,768]{1,0:T(8,128)(2,1)}, f32[768,768]{1,0:T(8,128)}, bf16[768,768]{1,0:T(8,128)(2,1)}, bf16[6400,768]{1,0:T(8,128)(2,1)}, bf16[768,768]{1,0:T(8,128)(2,1)}, /*index=5*/f32[8,768]{1,0:T(8,128)}) custom-call(bf16[768,768]{1,0:T(8,128)(2,1)} %bitcast.49, bf16[768,768]{1,0:T(8,128)(2,1)} %get-tuple-element.80.mixed, ...), custom_call_target="tpu_custom_call" | custom-call | flops 2475000064 | bytes 7875000 | tf_op jit(solution)/shard_map/feed/pallas_call | solution.py:1133
  185.7 1.7 copy-done.26
  189.9 1.5 copy-done.30
  191.4 14.7 %pooled_back.1 = (f32[768,768]{1,0:T(8,128)S(1)}, bf16[768,768]{1,0:T(8,128)(2,1)S(1)}, bf16[768,768]{1,0:T(8,128)(2,1)S(1)}, bf16[192,1536]{1,0:T(8,128)(2,1)S(...) custom-call(s32[5]{0:T(128)S(1)} %copy-done.35, ...), custom_call_target="tpu_custom_call" | custom-call | flops 1210000000 | bytes 3850000 | tf_op jit(solution)/shard_map/pooled_back/pallas_call | solution.py:1170
  207.7 1.7 collective-permute-done.13
  209.6 6.9 %collective-permute-start.14 = (bf16[192,1536]{1,0:T(8,128)(2,1)S(1)}, bf16[192,1536]{1,0:T(8,128)(2,1)S(1)}, u32[]{:S(2)}, u32[]{:S(2)}) collective-permute-start(bf16[192,1536]{1,0:T(8,128)(2,1)S(1)} %fusion.refs_1_), channel_id=1, source_target_pairs={{3,1},{0,2},{5,3},{2,4},{7,5},{4,6},{9,7},{6,8},{11,9},{8,10},{13,... | collective-permute-start | bytes 1769480 | tf_op jit(solution)/shard_map/ppermute | solution.py:1212
  218.1 13.3 %window_back.1 = (bf16[768,768]{1,0:T(8,128)(2,1)S(1)}, bf16[1536,1536]{1,0:T(8,128)(2,1)S(1)}, bf16[768,768]{1,0:T(8,128)(2,1)S(1)}) custom-call(f32[768,768]{1,0:T(8,128)S(1)} %get-tuple-element.88.grad_mixed, bf16[768,768]{1,0:T(8,128)(2,1)S(1)} %gate.15.grad_second, bf16[768,768]{1,0:T(8,128)(2,1)S(1)} %copy-done.5, bf16[768,768]{1,0:T(8,128)(2,1)S(1)} %copy-done.17, ...), custom_call_target="tpu_custom_call" | custom-call | flops 1210000000 | bytes 3850000 | tf_op jit(solution)/shard_map/window_back/pallas_call | solution.py:1216
  231.5 3.3 query_grad.1
  234.9 16.7 %collective-permute-done.14.near = bf16[192,1536]{1,0:T(8,128)(2,1)S(1)} collective-permute-done((bf16[192,1536]{1,0:T(8,128)(2,1)S(1)}, bf16[192,1536]{1,0:T(8,128)(2,1)S(1)}, u32[]{:S(2)}, u32[]{:S(2)}) %collective-permute-start.14) | collective-permute-done | bytes 589856 | tf_op jit(solution)/shard_map/ppermute | solution.py:1212
  251.6 7.2 %conv_back.1 = (bf16[1536,1536]{1,0:T(8,128)(2,1)S(1)}, f32[16,768]{1,0:T(8,128)S(1)}, bf16[768,768]{1,0:T(8,128)(2,1)S(1)}) custom-call(s32[17]{0:T(128)S(1)} %copy-done.34, bf16[192,1536]{1,0:T(8,128)(2,1)S(1)} %get-tuple-element.95.own, bf16[192,1536]{1,0:T(8,128)(2,1)S(1)} %slice_bitcast_fusion.away, bf16[192,1536]{1,0:T(8,128)(2,1)S(1)} %collective-permute-done.14.near, ...), custom_call_target="tpu_custom_call" | custom-call | flops 660000000 | bytes 2100000 | tf_op jit(solution)/shard_map/conv_back/pallas_call | solution.py:1253
  258.8 6.6 %weight_grad.1 = (bf16[2,4,48,3968]{3,2,1,0:T(8,128)(2,1)S(1)}, bf16[2,4,48,3968]{3,2,1,0:T(8,128)(2,1)S(1)}) custom-call(s32[17]{0:T(128)S(1)} %copy-done.34, bf16[768,768]{1,0:T(8,128)(2,1)S(1)} %bitcast.51, bf16[384,768]{1,0:T(8,128)(2,1)S(1)} %bitcast.55, bf16[384,768]{1,0:T(8,128)(2,1)S(1)} %bitcast.58, ...), custom_call_target="tpu_custom_call", output_to_operand_aliasing={{0}: (6, {}), {1}: (7, {})} | custom-call | flops 550000000 | bytes 1750000 | tf_op jit(solution)/shard_map/weight_grad/pallas_call | solution.py:1272
  265.5 5.5 %collective-permute-done.16.arrived = bf16[2,4,48,3968]{3,2,1,0:T(8,128)(2,1)S(1)} collective-permute-done((bf16[2,4,48,3968]{3,2,1,0:T(8,128)(2,1)S(1)}, bf16[2,4,48,3968]{3,2,1,0:T(8,128)(2,1)S(1)}, u32[]{:S(2)}, u32[]{:S(2)}) %collective-permute-start.16) | collective-permute-done | bytes 3047456 | tf_op jit(solution)/shard_map/ppermute | solution.py:947
  271.0 1.5 split.1
  274.1 3.1 collective-permute-start.17
  277.2 2.5 collective-permute-start.19
  279.7 7.0 %token_grad.1.refs_1_ = f32[768,768]{1,0:T(8,128)} custom-call(s32[17]{0:T(128)S(1)} %copy-done.34, f32[768,768]{1,0:T(8,128)S(1)} %copy-done.18, bf16[768,768]{1,0:T(8,128)(2,1)S(1)} %get-tuple-element.94.grad_queries, bf16[1536,1536]{1,0:T(8,128)(2,1)S(1)} %get-tuple-element.101.grad_pairs, bf16[384,768]{1,0:T(8,128)(2,1)S(1)} %collective-permute-done.17.low, ...), custom_call_target="tpu_custom_call" | custom-call | flops 605000000 | bytes 1925000 | tf_op jit(solution)/shard_map/token_grad/pallas_call | solution.py:1296
  286.7 9.2 %collective-permute-done.19.refs_2_.b_arrived = bf16[4,48,896]{2,1,0:T(8,128)(2,1)S(1)} collective-permute-done((bf16[4,48,896]{2,1,0:T(8,128)(2,1)S(1)}, bf16[4,48,896]{2,1,0:T(8,128)(2,1)S(1)}, u32[]{:S(2)}, u32[]{:S(2)}) %collective-permute-start.19) | collective-permute-done | bytes 344096 | tf_op jit(solution)/shard_map/ppermute | solution.py:681
  295.9 1.7 copy-done.8
  297.6 2.9 collective-permute-done.20.arrived
  300.9 5.9 %collective-permute-start.21 = (bf16[4,48,1536]{2,1,0:T(8,128)(2,1)S(1)}, bf16[4,48,1536]{2,1,0:T(8,128)(2,1)S(1)}, u32[]{:S(2)}, u32[]{:S(2)}) collective-permute-start(bf16[4,48,1536]{2,1,0:T(8,128)(2,1)S(1)} %get-tuple-element.112), channel_id=1, source_target_pairs={{0,2},{1,3},{2,0},{3,1},{4,6},{5,7},{6,4},{7,5},{8,10},{9,11},{10,... | collective-permute-start | bytes 1769480 | tf_op jit(solution)/shard_map/ppermute | solution.py:681
  306.8 12.9 %collective-permute-done.21.x_arrived = bf16[4,48,1536]{2,1,0:T(8,128)(2,1)S(1)} collective-permute-done((bf16[4,48,1536]{2,1,0:T(8,128)(2,1)S(1)}, bf16[4,48,1536]{2,1,0:T(8,128)(2,1)S(1)}, u32[]{:S(2)}, u32[]{:S(2)}) %collective-permute-start.21) | collective-permute-done | bytes 589856 | tf_op jit(solution)/shard_map/ppermute | solution.py:681
  319.9 2.0 reduce-scatter.2.cloned.1.call-done.refs_0_
  321.8 1.5 collective-permute-start.26
  323.3 1.6 collective-permute-start.22
  326.0 2.4 collective-permute-start.24
  328.4 5.5 %collective-permute-done.22.first = bf16[48,2432]{1,0:T(8,128)(2,1)S(1)} collective-permute-done((bf16[48,2432]{1,0:T(8,128)(2,1)S(1)}, bf16[48,2432]{1,0:T(8,128)(2,1)S(1)}, u32[]{:S(2)}, u32[]{:S(2)}) %collective-permute-start.22) | collective-permute-done | bytes 233504 | tf_op jit(solution)/shard_map/ppermute | solution.py:677
  333.9 8.4 %collective-permute-done.23.second = bf16[48,2432]{1,0:T(8,128)(2,1)S(1)} collective-permute-done((bf16[48,2432]{1,0:T(8,128)(2,1)S(1)}, bf16[48,2432]{1,0:T(8,128)(2,1)S(1)}, u32[]{:S(2)}, u32[]{:S(2)}) %collective-permute-start.23) | collective-permute-done | bytes 233504 | tf_op jit(solution)/shard_map/ppermute | solution.py:677
  343.0 7.0 %collective-permute-done.25.arrived = bf16[48,2432]{1,0:T(8,128)(2,1)S(1)} collective-permute-done((bf16[48,2432]{1,0:T(8,128)(2,1)S(1)}, bf16[48,2432]{1,0:T(8,128)(2,1)S(1)}, u32[]{:S(2)}, u32[]{:S(2)}) %collective-permute-start.25) | collective-permute-done | bytes 233504 | tf_op jit(solution)/shard_map/ppermute | solution.py:685
  350.0 1.5 final.1
  352.2 2.2 bulk_final.1
  (150 shorter events, 33.1 us)
Async XLA Ops:
  7.2 117.7 %all-gather.2.cloned.1.call-start = ((), (), s32[]{:S(2)}) async-start(), calls=%async_computation.1 | async-start | bytes 12533760 | tf_op jit(solution)/shard_map/all_gather | solution.py:1023
  12.1 309.7 %reduce-scatter.2.cloned.1.call-start = ((), (), s32[]{:S(2)}) async-start(), calls=%async_computation.2 | async-start | bytes 10444800 | tf_op jit(solution)/shard_map/reduce_scatter | solution.py:1167
  12.2 9.6 %collective-permute-start.2 = (bf16[48,1280]{1,0:T(8,128)(2,1)}, bf16[48,1280]{1,0:T(8,128)(2,1)S(1)}, u32[]{:S(2)}, u32[]{:S(2)}) collective-permute-start(bf16[48,1280]{1,0:T(8,128)(2,1)} %get-tuple-element.73), channel_id=1, source_target_pairs={{0,4},{1,5},{2,6},{3,7},{4,8},{5,9},{6,10},{7,11},{8,12},{9,13},{1... | collective-permute-start | bytes 368648 | tf_op jit(solution)/shard_map/ppermute | solution.py:677
  15.3 10.9 %collective-permute-start.1 = (bf16[48,1280]{1,0:T(8,128)(2,1)}, bf16[48,1280]{1,0:T(8,128)(2,1)S(1)}, u32[]{:S(2)}, u32[]{:S(2)}) collective-permute-start(bf16[48,1280]{1,0:T(8,128)(2,1)} %get-tuple-element.73), channel_id=1, source_target_pairs={{0,8},{1,9},{2,10},{3,11},{4,12},{5,13},{6,14},{7,15},{8,0},{9,1},... | collective-permute-start | bytes 368648 | tf_op jit(solution)/shard_map/ppermute | solution.py:677
  17.9 8.3 %collective-permute-start = (bf16[48,1280]{1,0:T(8,128)(2,1)}, bf16[48,1280]{1,0:T(8,128)(2,1)S(1)}, u32[]{:S(2)}, u32[]{:S(2)}) collective-permute-start(bf16[48,1280]{1,0:T(8,128)(2,1)} %get-tuple-element.73), channel_id=1, source_target_pairs={{0,12},{1,13},{2,14},{3,15},{4,0},{5,1},{6,2},{7,3},{8,4},{9,5},{1... | collective-permute-start | bytes 368648 | tf_op jit(solution)/shard_map/ppermute | solution.py:677
  27.2 18.7 %copy-start.33 = (bf16[6,64,768]{2,1,0:T(8,128)(2,1)S(1)}, bf16[6,64,768]{2,1,0:T(8,128)(2,1)}, u32[]{:S(2)}) copy-start(bf16[6,64,768]{2,1,0:T(8,128)(2,1)} %get-tuple-element.74.refs_0_) | copy-start | bytes 1769476
  27.2 17.1 %collective-permute-start.3 = (bf16[4,48,1280]{2,1,0:T(8,128)(2,1)S(1)}, bf16[4,48,1280]{2,1,0:T(8,128)(2,1)S(1)}, u32[]{:S(2)}, u32[]{:S(2)}) collective-permute-start(bf16[4,48,1280]{2,1,0:T(8,128)(2,1)S(1)} %pad_maximum_fusion), channel_id=1, source_target_pairs={{0,2},{1,3},{2,0},{3,1},{4,6},{5,7},{6,4},{7,5},{8,10},{9,11},{10,... | collective-permute-start | bytes 1474568 | tf_op jit(solution)/shard_map/ppermute | solution.py:681
  28.8 17.1 %copy-start.32 = (bf16[6,64,768]{2,1,0:T(8,128)(2,1)S(1)}, bf16[6,64,768]{2,1,0:T(8,128)(2,1)}, u32[]{:S(2)}) copy-start(bf16[6,64,768]{2,1,0:T(8,128)(2,1)} %get-tuple-element.72.refs_0_) | copy-start | bytes 1769476
  44.3 4.4 %copy-start.6 = (bf16[8,48,1280]{2,1,0:T(8,128)(2,1)}, bf16[8,48,1280]{2,1,0:T(8,128)(2,1)S(1)}, u32[]{:S(2)}) copy-start(bf16[8,48,1280]{2,1,0:T(8,128)(2,1)S(1)} %constant_dynamic-update-slice_fusion.refs_0_) | copy-start | bytes 2949124
  44.3 23.6 %collective-permute-start.6 = (bf16[8,48,1280]{2,1,0:T(8,128)(2,1)S(1)}, bf16[8,48,1280]{2,1,0:T(8,128)(2,1)S(1)}, u32[]{:S(2)}, u32[]{:S(2)}) collective-permute-start(bf16[8,48,1280]{2,1,0:T(8,128)(2,1)S(1)} %constant_dynamic-update-slice_fusion.refs_0_), channel_id=1, source_target_pairs={{0,16},{16,0},{1,17},{17,1},{2,18},{18,2},{3,19},{19,3},{4,20},{20... | collective-permute-start | bytes 2949128 | tf_op jit(solution)/shard_map/ppermute | solution.py:685
  45.9 4.6 %collective-permute-start.4 = (bf16[6,64,768]{2,1,0:T(8,128)(2,1)S(1)}, bf16[6,64,768]{2,1,0:T(8,128)(2,1)S(1)}, u32[]{:S(2)}, u32[]{:S(2)}) collective-permute-start(bf16[6,64,768]{2,1,0:T(8,128)(2,1)S(1)} %gate.11), channel_id=1, source_target_pairs={{0,1},{1,2},{2,3},{3,4},{4,5},{5,6},{6,7},{7,8},{8,9},{9,10},{10,1... | collective-permute-start | bytes 1769480 | tf_op jit(solution)/shard_map/ppermute | solution.py:941
  47.4 4.5 %collective-permute-start.5 = (bf16[6,64,768]{2,1,0:T(8,128)(2,1)S(1)}, bf16[6,64,768]{2,1,0:T(8,128)(2,1)S(1)}, u32[]{:S(2)}, u32[]{:S(2)}) collective-permute-start(bf16[6,64,768]{2,1,0:T(8,128)(2,1)S(1)} %gate.12), channel_id=1, source_target_pairs={{1,0},{2,1},{3,2},{4,3},{5,4},{6,5},{7,6},{8,7},{9,8},{10,9},{11,1... | collective-permute-start | bytes 1769480 | tf_op jit(solution)/shard_map/ppermute | solution.py:941
  48.7 20.6 %collective-permute-start.7 = (bf16[8,48,1280]{2,1,0:T(8,128)(2,1)S(1)}, bf16[8,48,1280]{2,1,0:T(8,128)(2,1)}, u32[]{:S(2)}, u32[]{:S(2)}) collective-permute-start(bf16[8,48,1280]{2,1,0:T(8,128)(2,1)S(1)} %constant_dynamic-update-slice_fusion.refs_0_), channel_id=1, source_target_pairs={{0,1},{1,0},{2,3},{3,2},{4,5},{5,4},{6,7},{7,6},{8,9},{9,8},{10,11... | collective-permute-start | bytes 2949128 | tf_op jit(solution)/shard_map/ppermute | solution.py:947
  50.5 17.4 %copy-start.9 = (bf16[6,64,768]{2,1,0:T(8,128)(2,1)}, bf16[6,64,768]{2,1,0:T(8,128)(2,1)S(1)}, u32[]{:S(2)}) copy-start(bf16[6,64,768]{2,1,0:T(8,128)(2,1)S(1)} %collective-permute-done.4) | copy-start | bytes 1769476
  51.9 16.1 %copy-start.11 = (bf16[6,64,768]{2,1,0:T(8,128)(2,1)}, bf16[6,64,768]{2,1,0:T(8,128)(2,1)S(1)}, u32[]{:S(2)}) copy-start(bf16[6,64,768]{2,1,0:T(8,128)(2,1)S(1)} %collective-permute-done.5) | copy-start | bytes 1769476
  68.0 2.8 collective-permute-start.8
  84.9 24.9 %collective-permute-start.10 = (bf16[192,1536]{1,0:T(8,128)(2,1)}, bf16[192,1536]{1,0:T(8,128)(2,1)S(1)}, u32[]{:S(2)}, u32[]{:S(2)}) collective-permute-start(bf16[192,1536]{1,0:T(8,128)(2,1)} %get-tuple-element.79.refs_0_), channel_id=1, source_target_pairs={{1,3},{2,0},{3,5},{4,2},{5,7},{6,4},{7,9},{8,6},{9,11},{10,8},{11,... | collective-permute-start | bytes 1769480 | tf_op jit(solution)/shard_map/ppermute | solution.py:953
  87.6 25.8 %collective-permute-start.12 = (bf16[192,1536]{1,0:T(8,128)(2,1)}, bf16[192,1536]{1,0:T(8,128)(2,1)S(1)}, u32[]{:S(2)}, u32[]{:S(2)}) collective-permute-start(bf16[192,1536]{1,0:T(8,128)(2,1)} %get-tuple-element.79.refs_0_), channel_id=1, source_target_pairs={{0,2},{2,4},{3,1},{4,6},{5,3},{6,8},{7,5},{8,10},{9,7},{10,12},{11... | collective-permute-start | bytes 1769480 | tf_op jit(solution)/shard_map/ppermute | solution.py:953
  97.6 15.7 %collective-permute-start.9 = (bf16[192,1536]{1,0:T(8,128)(2,1)}, bf16[192,1536]{1,0:T(8,128)(2,1)S(1)}, u32[]{:S(2)}, u32[]{:S(2)}) collective-permute-start(bf16[192,1536]{1,0:T(8,128)(2,1)} %get-tuple-element.79.refs_0_), channel_id=1, source_target_pairs={{0,1},{1,0},{2,3},{3,2},{4,5},{5,4},{6,7},{7,6},{8,9},{9,8},{10,11... | collective-permute-start | bytes 1769480 | tf_op jit(solution)/shard_map/ppermute | solution.py:947
  110.8 14.1 %copy-start.13 = (bf16[192,1536]{1,0:T(8,128)(2,1)}, bf16[192,1536]{1,0:T(8,128)(2,1)S(1)}, u32[]{:S(2)}) copy-start(bf16[192,1536]{1,0:T(8,128)(2,1)S(1)} %gate.14.refs_3_) | copy-start | bytes 1769476
  110.8 2.6 collective-permute-start.11
  113.4 11.6 %copy-start.20 = (bf16[192,1536]{1,0:T(8,128)(2,1)}, bf16[192,1536]{1,0:T(8,128)(2,1)S(1)}, u32[]{:S(2)}) copy-start(bf16[192,1536]{1,0:T(8,128)(2,1)S(1)} %collective-permute-done.12.refs_4_) | copy-start | bytes 1769476
  113.4 11.6 %copy-start.22 = (bf16[192,1536]{1,0:T(8,128)(2,1)}, bf16[192,1536]{1,0:T(8,128)(2,1)S(1)}, u32[]{:S(2)}) copy-start(bf16[192,1536]{1,0:T(8,128)(2,1)S(1)} %collective-permute-done.9.refs_1_) | copy-start | bytes 1769476
  182.9 33.7 %slice-start = ((s8[4718592]{0:T(1024)(128)(4,1)}), s8[524288]{0:T(1024)(128)(4,1)S(1)}, s32[]{:S(2)}) async-start(s8[4718592]{0:T(1024)(128)(4,1)} %bitcast.46), calls=%async_computation.3 | async-start | bytes 1048576
  191.4 25.1 %slice-start.1 = ((s8[4718592]{0:T(1024)(128)(4,1)}), s8[4194304]{0:T(1024)(128)(4,1)S(1)}, s32[]{:S(2)}) async-start(s8[4718592]{0:T(1024)(128)(4,1)} %bitcast.46), calls=%async_computation.4 | async-start | bytes 8388608
  191.4 25.2 %copy-start.27 = (bf16[768,768]{1,0:T(8,128)(2,1)S(1)}, bf16[768,768]{1,0:T(8,128)(2,1)}, u32[]{:S(2)}) copy-start(bf16[768,768]{1,0:T(8,128)(2,1)} %get-tuple-element.93.weights) | copy-start | bytes 3538948
  206.1 3.4 collective-permute-start.13
  206.5 28.4 %collective-permute-start.15 = (bf16[192,1536]{1,0:T(8,128)(2,1)S(1)}, bf16[192,1536]{1,0:T(8,128)(2,1)S(1)}, u32[]{:S(2)}, u32[]{:S(2)}) collective-permute-start(bf16[192,1536]{1,0:T(8,128)(2,1)S(1)} %get-tuple-element.96), channel_id=1, source_target_pairs={{2,0},{4,2},{1,3},{6,4},{3,5},{8,6},{5,7},{10,8},{7,9},{12,10},{9,... | collective-permute-start | bytes 1769480 | tf_op jit(solution)/shard_map/ppermute | solution.py:1213
  209.4 7.1 %copy-start.25 = (bf16[6,6,128,256]{3,2,1,0:T(8,128)(2,1)S(1)}, bf16[6,6,128,256]{3,2,1,0:T(8,128)(2,1)}, u32[]{:S(2)}) copy-start(bf16[6,6,128,256]{3,2,1,0:T(8,128)(2,1)} %copy-done.24) | copy-start | bytes 7077892
  209.6 41.9 %collective-permute-start.14 = (bf16[192,1536]{1,0:T(8,128)(2,1)S(1)}, bf16[192,1536]{1,0:T(8,128)(2,1)S(1)}, u32[]{:S(2)}, u32[]{:S(2)}) collective-permute-start(bf16[192,1536]{1,0:T(8,128)(2,1)S(1)} %fusion.refs_1_), channel_id=1, source_target_pairs={{3,1},{0,2},{5,3},{2,4},{7,5},{4,6},{9,7},{6,8},{11,9},{8,10},{13,... | collective-permute-start | bytes 1769480 | tf_op jit(solution)/shard_map/ppermute | solution.py:1212
  218.1 13.3 %copy-start.1 = (bf16[6,128,768]{2,1,0:T(8,128)(2,1)S(1)}, bf16[6,128,768]{2,1,0:T(8,128)(2,1)}, u32[]{:S(2)}) copy-start(bf16[6,128,768]{2,1,0:T(8,128)(2,1)} %tokens.1) | copy-start | bytes 3538948
  218.1 13.4 %copy-start.34 = (s32[17]{0:T(128)S(1)}, s32[17]{0:T(128)}, u32[]{:S(2)}) copy-start(s32[17]{0:T(128)} %pad_add_fusion.order) | copy-start | bytes 208
  234.8 16.8 %copy-start.7 = (bf16[8,48,1280]{2,1,0:T(8,128)(2,1)S(1)}, bf16[8,48,1280]{2,1,0:T(8,128)(2,1)}, u32[]{:S(2)}) copy-start(bf16[8,48,1280]{2,1,0:T(8,128)(2,1)} %copy-done.6) | copy-start | bytes 2949124
  234.8 16.8 %copy-start.3 = (bf16[8,48,1280]{2,1,0:T(8,128)(2,1)S(1)}, bf16[8,48,1280]{2,1,0:T(8,128)(2,1)}, u32[]{:S(2)}) copy-start(bf16[8,48,1280]{2,1,0:T(8,128)(2,1)} %copy-done.2) | copy-start | bytes 2949124
  251.6 7.2 %copy-start.10 = (bf16[6,64,768]{2,1,0:T(8,128)(2,1)S(1)}, bf16[6,64,768]{2,1,0:T(8,128)(2,1)}, u32[]{:S(2)}) copy-start(bf16[6,64,768]{2,1,0:T(8,128)(2,1)} %copy-done.9) | copy-start | bytes 1769476
  251.6 7.2 %copy-start.12 = (bf16[6,64,768]{2,1,0:T(8,128)(2,1)S(1)}, bf16[6,64,768]{2,1,0:T(8,128)(2,1)}, u32[]{:S(2)}) copy-start(bf16[6,64,768]{2,1,0:T(8,128)(2,1)} %copy-done.11) | copy-start | bytes 1769476
  265.4 5.6 %collective-permute-start.16 = (bf16[2,4,48,3968]{3,2,1,0:T(8,128)(2,1)S(1)}, bf16[2,4,48,3968]{3,2,1,0:T(8,128)(2,1)S(1)}, u32[]{:S(2)}, u32[]{:S(2)}) collective-permute-start(bf16[2,4,48,3968]{3,2,1,0:T(8,128)(2,1)S(1)} %get-tuple-element.106), channel_id=1, source_target_pairs={{0,1},{1,0},{2,3},{3,2},{4,5},{5,4},{6,7},{7,6},{8,9},{9,8},{10,11... | collective-permute-start | bytes 9142280 | tf_op jit(solution)/shard_map/ppermute | solution.py:947
  272.5 28.1 %collective-permute-start.20 = (bf16[2,4,48,1536]{3,2,1,0:T(8,128)(2,1)S(1)}, bf16[2,4,48,1536]{3,2,1,0:T(8,128)(2,1)S(1)}, u32[]{:S(2)}, u32[]{:S(2)}) collective-permute-start(bf16[2,4,48,1536]{3,2,1,0:T(8,128)(2,1)S(1)} %get-tuple-element.110), channel_id=1, source_target_pairs={{0,16},{16,0},{1,17},{17,1},{2,18},{18,2},{3,19},{19,3},{4,20},{20... | collective-permute-start | bytes 3538952 | tf_op jit(solution)/shard_map/ppermute | solution.py:685
  272.6 7.1 %copy-start.18 = (f32[768,768]{1,0:T(8,128)S(1)}, f32[768,768]{1,0:T(8,128)}, u32[]{:S(2)}) copy-start(f32[768,768]{1,0:T(8,128)} %get-tuple-element.83.grad_resid) | copy-start | bytes 7077892
  272.7 7.0 %collective-permute-start.18 = (bf16[384,768]{1,0:T(8,128)(2,1)S(1)}, bf16[384,768]{1,0:T(8,128)(2,1)S(1)}, u32[]{:S(2)}, u32[]{:S(2)}) collective-permute-start(bf16[384,768]{1,0:T(8,128)(2,1)S(1)} %get-tuple-element.144), channel_id=1, source_target_pairs={{1,0},{2,1},{3,2},{4,3},{5,4},{6,5},{7,6},{8,7},{9,8},{10,9},{11,1... | collective-permute-start | bytes 1769480 | tf_op jit(solution)/shard_map/ppermute | solution.py:941
  274.1 5.6 %collective-permute-start.17 = (bf16[384,768]{1,0:T(8,128)(2,1)S(1)}, bf16[384,768]{1,0:T(8,128)(2,1)S(1)}, u32[]{:S(2)}, u32[]{:S(2)}) collective-permute-start(bf16[384,768]{1,0:T(8,128)(2,1)S(1)} %get-tuple-element.145), channel_id=1, source_target_pairs={{0,1},{1,2},{2,3},{3,4},{4,5},{5,6},{6,7},{7,8},{8,9},{9,10},{10,1... | collective-permute-start | bytes 1769480 | tf_op jit(solution)/shard_map/ppermute | solution.py:941
  277.2 18.8 %collective-permute-start.19 = (bf16[4,48,896]{2,1,0:T(8,128)(2,1)S(1)}, bf16[4,48,896]{2,1,0:T(8,128)(2,1)S(1)}, u32[]{:S(2)}, u32[]{:S(2)}) collective-permute-start(bf16[4,48,896]{2,1,0:T(8,128)(2,1)S(1)} %get-tuple-element.109), channel_id=1, source_target_pairs={{0,2},{1,3},{2,0},{3,1},{4,6},{5,7},{6,4},{7,5},{8,10},{9,11},{10,... | collective-permute-start | bytes 1032200 | tf_op jit(solution)/shard_map/ppermute | solution.py:681
  300.9 18.8 %collective-permute-start.21 = (bf16[4,48,1536]{2,1,0:T(8,128)(2,1)S(1)}, bf16[4,48,1536]{2,1,0:T(8,128)(2,1)S(1)}, u32[]{:S(2)}, u32[]{:S(2)}) collective-permute-start(bf16[4,48,1536]{2,1,0:T(8,128)(2,1)S(1)} %get-tuple-element.112), channel_id=1, source_target_pairs={{0,2},{1,3},{2,0},{3,1},{4,6},{5,7},{6,4},{7,5},{8,10},{9,11},{10,... | collective-permute-start | bytes 1769480 | tf_op jit(solution)/shard_map/ppermute | solution.py:681
  321.8 30.3 %collective-permute-start.26 = (bf16[400,768]{1,0:T(8,128)(2,1)}, bf16[400,768]{1,0:T(8,128)(2,1)S(1)}, u32[]{:S(2)}, u32[]{:S(2)}) collective-permute-start(bf16[400,768]{1,0:T(8,128)(2,1)} %gate.19.own), channel_id=1, source_target_pairs={{0,16},{16,0},{1,17},{17,1},{2,18},{18,2},{3,19},{19,3},{4,20},{20... | collective-permute-start | bytes 1843208 | tf_op jit(solution)/shard_map/ppermute | solution.py:685
  323.3 10.6 %collective-permute-start.22 = (bf16[48,2432]{1,0:T(8,128)(2,1)S(1)}, bf16[48,2432]{1,0:T(8,128)(2,1)S(1)}, u32[]{:S(2)}, u32[]{:S(2)}) collective-permute-start(bf16[48,2432]{1,0:T(8,128)(2,1)S(1)} %get-tuple-element.114), channel_id=1, source_target_pairs={{0,4},{1,5},{2,6},{3,7},{4,8},{5,9},{6,10},{7,11},{8,12},{9,13},{1... | collective-permute-start | bytes 700424 | tf_op jit(solution)/shard_map/ppermute | solution.py:677
  324.9 17.4 %collective-permute-start.23 = (bf16[48,2432]{1,0:T(8,128)(2,1)S(1)}, bf16[48,2432]{1,0:T(8,128)(2,1)S(1)}, u32[]{:S(2)}, u32[]{:S(2)}) collective-permute-start(bf16[48,2432]{1,0:T(8,128)(2,1)S(1)} %get-tuple-element.115), channel_id=1, source_target_pairs={{0,8},{1,9},{2,10},{3,11},{4,12},{5,13},{6,14},{7,15},{8,0},{9,1},... | collective-permute-start | bytes 700424 | tf_op jit(solution)/shard_map/ppermute | solution.py:677
  326.0 16.3 %collective-permute-start.24 = (bf16[48,2432]{1,0:T(8,128)(2,1)S(1)}, bf16[48,2432]{1,0:T(8,128)(2,1)S(1)}, u32[]{:S(2)}, u32[]{:S(2)}) collective-permute-start(bf16[48,2432]{1,0:T(8,128)(2,1)S(1)} %get-tuple-element.116), channel_id=1, source_target_pairs={{0,12},{1,13},{2,14},{3,15},{4,0},{5,1},{6,2},{7,3},{8,4},{9,5},{1... | collective-permute-start | bytes 700424 | tf_op jit(solution)/shard_map/ppermute | solution.py:677
  342.4 7.6 %collective-permute-start.25 = (bf16[48,2432]{1,0:T(8,128)(2,1)S(1)}, bf16[48,2432]{1,0:T(8,128)(2,1)S(1)}, u32[]{:S(2)}, u32[]{:S(2)}) collective-permute-start(bf16[48,2432]{1,0:T(8,128)(2,1)S(1)} %gather_sum.1.own), channel_id=1, source_target_pairs={{0,16},{16,0},{1,17},{17,1},{2,18},{18,2},{3,19},{19,3},{4,20},{20... | collective-permute-start | bytes 700424 | tf_op jit(solution)/shard_map/ppermute | solution.py:685
  (22 other events, 35.1 us)
Sparse Core Ops, SparseCore 0:
  12.3 112.5 all-gather.1
  183.0 138.7 reduce-scatter.1

commit v5 on v4

--- a/solution.py
+++ b/solution.py
@@ -351,10 +351,10 @@
     (
         result,
         grad_resid,
-        grad_attn,
+        grad_mixed,
         gone,
+        vec_grads,
         w_out,
-        vec_grads,
         w_in,
         w_down,
         centred,
@@ -367,6 +367,7 @@
         grad_outer,
         grad_in,
         grad_down,
+        grad_out,
         bias_grad,
         narrow,
         sems,
@@ -377,14 +378,14 @@
     second, third = fetch_bulk(bulk, w_in, w_down, (sems.at[1], sems.at[2]))
     settle(first)
 
-    @pl.loop(0, width // TILE)
+    @pl.loop(0, width // TILE, unroll=3)
     def _(n):
         cols = span(n, TILE)
         field[:, cols] = tok[:, cols].astype(F32) + product(mixed[...], w_out[:, cols]) + vecs[0:1, cols]
 
     blocks = rows // WINDOW
 
-    @pl.loop(0, blocks)
+    @pl.loop(0, blocks, unroll=2)
     def _(b):
         part = span(b, WINDOW)
         resid = field[part, :]
@@ -399,7 +400,7 @@
 
     settle(second)
 
-    @pl.loop(0, hidden // TILE)
+    @pl.loop(0, hidden // TILE, unroll=3)
     def _(n):
         cols = span(n, TILE)
         inner = product(normed[...], w_in[:, cols]) + bias_in[0:1, cols]
@@ -409,7 +410,7 @@
 
     settle(third)
 
-    @pl.loop(0, width // TILE)
+    @pl.loop(0, width // TILE, unroll=3)
     def _(n):
         cols = span(n, TILE)
         unit = centred[:, cols] * vecs[1:2, cols] + vecs[2:3, cols]
@@ -420,7 +421,7 @@
     def add_row(k, value):
         vec_grads[k : k + 1, :] += jnp.sum(value, axis=0, keepdims=True)
 
-    @pl.loop(0, blocks)
+    @pl.loop(0, blocks, unroll=2)
     def _(b):
         part = span(b, WINDOW)
         summed = field[part, :]
@@ -439,7 +440,7 @@
         grad_outer[part, :] = low
         add_row(3, low.astype(F32))
 
-    @pl.loop(0, hidden // TILE)
+    @pl.loop(0, hidden // TILE, unroll=3)
     def _(n):
         cols = span(n, TILE)
         grad = product_back(grad_outer[...], w_down[cols, :]).astype(BF16).astype(F32)
@@ -464,12 +465,12 @@
     for copy in emits:
         copy.start()
 
-    @pl.loop(0, width // TILE)
+    @pl.loop(0, width // TILE, unroll=3)
     def _(n):
         cols = span(n, TILE)
         field[:, cols] += product_back(slope[...], w_in[cols, :])
 
-    @pl.loop(0, blocks)
+    @pl.loop(0, blocks, unroll=2)
     def _(b):
         part = span(b, WINDOW)
         grad = field[part, :]
@@ -481,8 +482,24 @@
         grad = rstd[part, 0:1] * (u - jnp.mean(u, axis=-1, keepdims=True) - unit * lean)
         grad_resid[part, :] = grad
         low = grad.astype(BF16)
-        grad_attn[part, :] = low
+        grad_outer[part, :] = low
         add_row(0, low.astype(F32))
+
+    @pl.loop(0, width // TILE, unroll=3)
+    def _(n):
+        cols = span(n, TILE)
+        grad_out[cols, :] = outer_sum(mixed[:, cols], grad_outer[...]).astype(BF16)
+
+    for j in range(SLOTS):
+        source = grad_out.at[pl.ds(j * block, block), :]
+        target = gone.at[pl.ds(j * each + 2 * folds * block, block), :]
+        emits.append(pltpu.make_async_copy(source, target, sems.at[3]))
+        emits[-1].start()
+
+    @pl.loop(0, width // TILE, unroll=3)
+    def _(n):
+        cols = span(n, TILE)
+        grad_mixed[:, cols] = product_back(grad_outer[...], w_out[cols, :]).astype(BF16)
 
     narrow[...] = jnp.zeros_like(narrow)
     small = narrow.shape[1]
@@ -499,35 +516,25 @@
     settle(emits)
 
 
-def pooled_back_kernel(places, grad_attn, mixed, queries, probs, weights, *refs):
+def pooled_back_kernel(places, grad_mixed, queries, probs, *refs):
     blocks = refs[:5]
-    grad_mixed, grad_queries, grad_out, grad_own, grad_away, grad_near, grad_far = refs[-10:-3]
-    field, total, grad_low = refs[-3:]
-    width = grad_attn.shape[1]
+    grad_queries, grad_own, grad_away, grad_near, grad_far = refs[5:10]
+    field, total = refs[10:]
+    width = grad_mixed.shape[1]
     pools = blocks[0].shape[0]
-    s = pl.program_id(0)
-
-    @pl.when(s == 0)
+
+    @pl.when(pl.program_id(0) == 0)
     def _():
         field[...] = jnp.zeros_like(field)
-
-        @pl.loop(0, width // TILE)
-        def _(n):
-            cols = span(n, TILE)
-            grad = product_back(grad_attn[...], weights[cols, :])
-            grad_mixed[:, cols] = grad
-            grad_low[:, cols] = grad.astype(BF16)
-            grad_out[cols, :] = outer_sum(mixed[:, cols], grad_attn[...]).astype(BF16)
 
     lay_pooled(places, blocks, field)
     lanes = lane_masks()
     sides = side_masks(STRIDE)
-    rows = span(s, WINDOW)
     for n in range(width // PAIR):
         cols = slice(n * PAIR, (n + 1) * PAIR)
         others = slice(width + n * PAIR, width + (n + 1) * PAIR)
         grad_q, grad_k, grad_v = attend_back(
-            queries[:, cols], field[:, cols], field[:, others], probs[0, n], grad_low[rows, cols], lanes, sides
+            queries[:, cols], field[:, cols], field[:, others], probs[0, n], grad_mixed[:, cols], lanes, sides
         )
         grad_queries[:, cols] = grad_q.astype(BF16)
         total[:, cols] = grad_k
@@ -546,7 +553,7 @@
         @pl.loop(0, width // TILE)
         def _(n):
             cols = span(n, TILE)
-            grad = grad_mixed[:, cols] + product_back(grad_second[...], weights[cols, :])
+            grad = grad_mixed[:, cols].astype(F32) + product_back(grad_second[...], weights[cols, :])
             grad_low[:, cols] = grad.astype(BF16)
             grad_pooled[cols, :] = outer_sum(first[:, cols], grad_second[...]).astype(BF16)
 
@@ -606,12 +613,11 @@
         edges[:, cols] = product_back(rim[...], weights[cols, width:]).astype(BF16)
 
 
-def query_grad_kernel(order, tok, grad_queries, grad_pooled, grad_out, keep, give, tok_t, total, sem):
+def query_grad_kernel(order, tok, grad_queries, grad_pooled, keep, give, tok_t, total, sem):
     width = tok.shape[1]
     block = width // SLOTS
     targets = (keep, give)
     copies = emit(order, grad_pooled, pl.ds(0, width), block, targets, 3 * width, sem)
-    copies += emit(order, grad_out, pl.ds(0, width), block, targets, 4 * width, sem)
     tok_t[...] = tok[...].T
 
     @pl.loop(0, width // TILE)
@@ -630,7 +636,7 @@
     targets = (keep, give)
     taps = jnp.concatenate([tap_grads[...], jnp.zeros((112, width), F32)], axis=0).T
     narrow[...] = taps.astype(BF16)
-    copies = emit(order, narrow, pl.ds(0, 128), block, targets, 5 * width, sem)
+    copies = emit(order, narrow, pl.ds(0, 128), block, targets, 4 * width, sem)
     for s in range(low.shape[0] // HALF):
         parts = (
             low[s * HALF : (s + 1) * HALF, :],
@@ -905,7 +911,7 @@
         )(self.order, self.own, self.last)
 
 
-def bulk_final_kernel(own, arrived, inner, outer, small):
+def bulk_final_kernel(own, arrived, inner, outer, square, small):
     part, hidden = inner.shape
     width = own.shape[1]
     total = own[...].astype(F32) + arrived[...].astype(F32)
@@ -913,7 +919,8 @@
     for m in range(folds):
         inner[:, m * width : (m + 1) * width] = total[m * part : (m + 1) * part]
     outer[...] = total[folds * part : 2 * folds * part]
-    small[...] = total[2 * folds * part :]
+    square[...] = total[2 * folds * part : (2 * folds + 1) * part]
+    small[...] = total[(2 * folds + 1) * part :]
 
 
 def plain_total(whole):
@@ -1129,20 +1136,20 @@
         name="pooled",
     )(places, attended, bias_two, bulk, *pool_blocks)
 
-    each = 2 * hidden // SLOTS + SMALL_ROWS
-    result, grad_resid, grad_attn, grad_bulk, out_weights, _ = pl.pallas_call(
+    each = (2 * hidden + width) // SLOTS + SMALL_ROWS
+    result, grad_resid, grad_mixed, grad_bulk, _ = pl.pallas_call(
         feed_kernel,
         out_shape=(
             shape_of(rows, width),
             shape_of(rows, width, dtype=F32),
             shape_of(rows, width),
             shape_of(SLOTS * each, width),
-            shape_of(width, width),
             shape_of(8, width, dtype=F32),
         ),
         in_specs=[vmem_spec()] * 5 + [hbm_spec()],
-        out_specs=(vmem_spec(),) * 3 + (any_spec(), vmem_spec(), vmem_spec()),
+        out_specs=(vmem_spec(),) * 3 + (any_spec(), vmem_spec()),
         scratch_shapes=[
+            pltpu.VMEM((width, width), BF16),
             pltpu.VMEM((width, hidden), BF16),
             pltpu.VMEM((hidden, width), BF16),
             pltpu.VMEM((rows, width), F32),
@@ -1155,6 +1162,7 @@
             pltpu.VMEM((rows, width), BF16),
             pltpu.VMEM((width, hidden), BF16),
             pltpu.VMEM((hidden, width), BF16),
+            pltpu.VMEM((width, width), BF16),
             pltpu.VMEM((1, hidden), F32),
             pltpu.VMEM((SLOTS, SMALL_ROWS, width), BF16),
             pltpu.SemaphoreType.DMA((4,)),
@@ -1167,13 +1175,11 @@
         own_bulk = lax.psum_scatter(grad_bulk, "shard", scatter_dimension=0, tiled=True)
 
     back_shape = shape_of(seqs * pools, 2 * width)
-    grad_mixed, grad_second, grad_out, pg_own, pg_away, pg_near, pg_far = pl.pallas_call(
+    grad_second, pg_own, pg_away, pg_near, pg_far = pl.pallas_call(
         pooled_back_kernel,
         grid=(seqs,),
         out_shape=(
-            shape_of(rows, width, dtype=F32),
             shape_of(rows, width),
-            shape_of(width, width),
             back_shape,
             shape_of(2, seqs * pools, 2 * width),
             back_shape,
@@ -1181,31 +1187,23 @@
         ),
         in_specs=[
             smem_spec(),
-            whole_block(rows, width),
-            whole_block(rows, width),
+            seq_block(tok_span, width),
             seq_block(tok_span, width),
             prob_block,
-            whole_block(width, width),
         ]
         + pool_specs,
         out_specs=(
-            whole_block(rows, width),
             seq_block(tok_span, width),
-            whole_block(width, width),
             seq_block(pools, 2 * width),
             pl.BlockSpec((2, pools, 2 * width), lambda s: (0, s, 0)),
             seq_block(pools, 2 * width),
             seq_block(pools, 2 * width),
         ),
-        scratch_shapes=[
-            pltpu.VMEM((WIDE, 2 * width), BF16),
-            pltpu.VMEM((WIDE, 2 * width), F32),
-            pltpu.VMEM((rows, width), BF16),
-        ],
-        compiler_params=params(20),
-        cost_estimate=cost(22),
+        scratch_shapes=[pltpu.VMEM((WIDE, 2 * width), BF16), pltpu.VMEM((WIDE, 2 * width), F32)],
+        compiler_params=params(56),
+        cost_estimate=cost(15),
         name="pooled_back",
-    )(places, grad_attn, mixed, second, probs_two, out_weights, *pool_blocks)
+    )(places, grad_mixed, second, probs_two, *pool_blocks)
 
     pg_cross = swap(pg_away)
     pg_near = (pg_near.astype(F32) + pg_cross[1].astype(F32)).astype(BF16)
@@ -1233,11 +1231,11 @@
         name="window_back",
     )(grad_mixed, grad_second, attended, queries, pairs, probs_one, pooled_weights)
 
-    lead_shape = shape_of(2, 4, block, 5 * width + 128)
+    lead_shape = shape_of(2, 4, block, 4 * width + 128)
     lead_keep, lead_give = pl.pallas_call(
         query_grad_kernel,
         out_shape=(lead_shape, lead_shape),
-        in_specs=[smem_spec()] + [vmem_spec()] * 4,
+        in_specs=[smem_spec()] + [vmem_spec()] * 3,
         out_specs=(any_spec(),) * 2,
         scratch_shapes=[
             pltpu.VMEM((width, rows), BF16),
@@ -1247,7 +1245,7 @@
         compiler_params=params(12),
         cost_estimate=cost(5),
         name="query_grad",
-    )(order, tok, grad_queries, grad_pooled, grad_out)
+    )(order, tok, grad_queries, grad_pooled)
     vecs = after(vecs, lead_keep)
 
     pair_total, tap_grads, edges = pl.pallas_call(
@@ -1285,7 +1283,7 @@
         cost_estimate=cost(10),
         name="weight_grad",
     )(order, tok, tok_low, tok_high, pair_total, tap_grads, lead_keep, lead_give)
-    pieces = tuple((k * width, width) for k in range(5)) + ((5 * width, 128),)
+    pieces = tuple((k * width, width) for k in range(4)) + ((4 * width, 128),)
     lead_sum = Scatter(lead_keep, lead_give, order, 24 * 128, pieces)
     if direct():
         lead_sum.split()
@@ -1313,34 +1311,36 @@
         lead_sum.a_keep = after(lead_sum.a_keep, tokens_grad, lead_sum.b_arrived)
         lead_sum.fold()
         lead_sum.join()
-        own_bulk = after(own_bulk, lead_sum.turned[0])
+        own_bulk = after(own_bulk, lead_sum.turned[1])
         lead_sum.gather()
-        own_in, own_down, small_own = pl.pallas_call(
+        own_in, own_down, own_out, small_own = pl.pallas_call(
             bulk_final_kernel,
             out_shape=(
                 shape_of(part, hidden, dtype=F32),
                 shape_of(folds * part, width, dtype=F32),
+                shape_of(part, width, dtype=F32),
                 shape_of(SMALL_ROWS, width, dtype=F32),
             ),
             in_specs=[vmem_spec()] * 2,
-            out_specs=(vmem_spec(),) * 3,
+            out_specs=(vmem_spec(),) * 4,
             compiler_params=params(10),
             cost_estimate=cost(2),
             name="bulk_final",
         )(own_bulk, other(own_bulk))
         vec_own = [small_own[k, :part] for k in range(6)]
         bias_own = small_own[8, : folds * part]
-        own_query, own_keys, own_values, own_pooled, own_out, taps_own = lead_sum.final()
+        own_query, own_keys, own_values, own_pooled, taps_own = lead_sum.final()
     else:
         whole = grad_bulk.reshape(SLOTS, each, width)
         inner_part = whole[:, : folds * block].reshape(SLOTS, folds, block, width).transpose(0, 2, 1, 3)
         own_in = plain_total(inner_part.reshape(width, hidden))
         own_down = plain_total(whole[:, folds * block : 2 * folds * block].reshape(hidden, width))
-        small = whole[:, 2 * folds * block :]
+        small = whole[:, (2 * folds + 1) * block :]
         vec_own = [plain_total(small[:, k, :block].reshape(width)) for k in range(6)]
         bias_own = plain_total(small[:, 8, : folds * block].reshape(hidden))
-        parts = [(k * width, (k + 1) * width) for k in range(5)] + [(5 * width, None)]
-        own_query, own_keys, own_values, own_pooled, own_out, taps_own = plain_scatter(
+        own_out = plain_total(whole[:, 2 * folds * block : (2 * folds + 1) * block].reshape(width, width))
+        parts = [(k * width, (k + 1) * width) for k in range(4)] + [(4 * width, None)]
+        own_query, own_keys, own_values, own_pooled, taps_own = plain_scatter(
             (lead_keep, lead_give), parts
         )
     taps_own = taps_own.T[: 2 * KERNEL].reshape(KERNEL, 2, part)

time: 366 us -> 362 us (0.989)
  local copies, waits for them, and re-layouts: 25 us -> 18.1 us
  waiting for transfers between devices: 124 us -> 128 us
    unnamed x86 -> x72, local copies, waits for them, and re-layouts: 19.6 us -> 12.7 us
    ppermute x4, waiting for transfers between devices: 26 us -> 30.7 us  [other(): return lax.ppermute(block, 'rep', [(0, 1), (1, 0)])]
    ppermute x3, waiting for transfers between devices: 37.7 us -> 41.8 us  [flip(): return lax.ppermute(block, 'shard', [(i, i ^ 2) for i in range(SLOTS)])]
  transfers between devices with their start and end apart: 29 -> 29, of which waited for: 17 -> 16; matrix products, arithmetic and copies ran while one was open for 2% -> 2% of each run, Pallas kernels for 21% -> 21%
where the time goes in v5:
time: 362 us; the launch traced here: 361 us
  Pallas kernels  138 us (38%)
  waiting for transfers between devices  128 us (35%)
  starting transfers between devices  57 us (16%)
  local copies, waits for them, and re-layouts  18.1 us (5%)
  between operations  14.7 us (4%)
  other arithmetic  4.77 us (1%)
    pallas_call x1, Pallas kernels, shards(): pl.pallas_call(feed_kernel, out_shape=(shape_of(rows, width), shape_of(ro...  44.8 us
    ppermute x3, waiting for transfers between devices, flip(): return lax.ppermute(block, 'shard', [(i, i ^ 2) for i in range(SLOTS)])  41.8 us
    ppermute x4, waiting for transfers between devices, other(): return lax.ppermute(block, 'rep', [(0, 1), (1, 0)])  30.7 us
    ppermute x6, waiting for transfers between devices, turn(): lax.ppermute(block, 'shard', [(i, (i - 4 * step) % SLOTS) for i in range(...  21.9 us
    pallas_call x1, Pallas kernels, shards(): pl.pallas_call(functools.partial(project_kernel, lead_table), out_shape=(...  14.1 us
    pallas_call x1, Pallas kernels, shards(): pl.pallas_call(pooled_back_kernel, grid=(seqs,), out_shape=(shape_of(rows...  13.7 us
    ppermute x1, waiting for transfers between devices, shards(): back_near = lax.ppermute(pg_near, 'shard', back_route(device_count, False))  13.3 us
    pallas_call x1, Pallas kernels, shards(): pl.pallas_call(window_back_kernel, grid=(seqs,), out_shape=(shape_of(rows...  13.3 us
  transfers between devices with their start and end apart: 29, of which 16 were waited for; matrix products, arithmetic and copies ran while one was open for 2% of the time, Pallas kernels for 21%

profile of v5, /device:TPU:0, one launch (start us, length us, event | category | flops | bytes accessed | tf_op | source)
XLA Modules:
  0.0 360.8 jit_solution(11071067903739459714)
XLA Ops:
  9.2 3.0 pack.1
  12.2 3.1 collective-permute-start.2
  15.3 2.6 collective-permute-start.1
  20.1 1.6 collective-permute-done.2
  21.7 4.4 %collective-permute-done.1 = bf16[48,1280]{1,0:T(8,128)(2,1)S(1)} collective-permute-done((bf16[48,1280]{1,0:T(8,128)(2,1)}, bf16[48,1280]{1,0:T(8,128)(2,1)S(1)}, u32[]{:S(2)}, u32[]{:S(2)}) %collective-permute-start.1) | collective-permute-done | bytes 122912 | tf_op jit(solution)/shard_map/ppermute | solution.py:683
  27.2 1.6 collective-permute-start.3
  28.8 15.5 %collective-permute-done.3.refs_1_ = bf16[4,48,1280]{2,1,0:T(8,128)(2,1)S(1)} collective-permute-done((bf16[4,48,1280]{2,1,0:T(8,128)(2,1)S(1)}, bf16[4,48,1280]{2,1,0:T(8,128)(2,1)S(1)}, u32[]{:S(2)}, u32[]{:S(2)}) %collective-permute-start.3) | collective-permute-done | bytes 491552 | tf_op jit(solution)/shard_map/ppermute | solution.py:687
  44.3 1.5 collective-permute-start.6
  45.9 1.5 collective-permute-start.4
  48.7 1.7 collective-permute-start.7
  50.5 1.4 collective-permute-done.5
  51.9 16.0 %collective-permute-done.6.refs_0_ = bf16[8,48,1280]{2,1,0:T(8,128)(2,1)S(1)} collective-permute-done((bf16[8,48,1280]{2,1,0:T(8,128)(2,1)S(1)}, bf16[8,48,1280]{2,1,0:T(8,128)(2,1)S(1)}, u32[]{:S(2)}, u32[]{:S(2)}) %collective-permute-start.6) | collective-permute-done | bytes 983072 | tf_op jit(solution)/shard_map/ppermute | solution.py:691
  70.7 14.1 %project.1 = (bf16[768,768]{1,0:T(8,128)(2,1)}, bf16[1536,1536]{1,0:T(8,128)(2,1)}, bf16[192,1536]{1,0:T(8,128)(2,1)}, f32[24,768]{1,0:T(8,128)}) custom-call(s32[17]{0:T(128)} %pad_add_fusion.order, bf16[768,768]{1,0:T(8,128)(2,1)} %bitcast.48, bf16[384,768]{1,0:T(8,128)(2,1)} %bitcast.54, bf16[384,768]{1,0:T(8,128)(2,1)} %bitcast.57, ...), custom_call_target="tpu_custom_call" | custom-call | flops 825000000 | bytes 2625000 | tf_op jit(solution)/shard_map/project/pallas_call | solution.py:1073
  87.5 10.0 %collective-permute-start.12 = (bf16[192,1536]{1,0:T(8,128)(2,1)}, bf16[192,1536]{1,0:T(8,128)(2,1)S(1)}, u32[]{:S(2)}, u32[]{:S(2)}) collective-permute-start(bf16[192,1536]{1,0:T(8,128)(2,1)} %get-tuple-element.76.refs_0_), channel_id=1, source_target_pairs={{0,2},{2,4},{3,1},{4,6},{5,3},{6,8},{7,5},{8,10},{9,7},{10,12},{11... | collective-permute-start | bytes 1769480 | tf_op jit(solution)/shard_map/ppermute | solution.py:960
  97.7 2.3 copy-done
  101.3 6.9 %window.1 = (bf16[768,768]{1,0:T(8,128)(2,1)S(1)}, bf16[6,6,128,256]{3,2,1,0:T(8,128)(2,1)S(1)}) custom-call(bf16[768,768]{1,0:T(8,128)(2,1)S(1)} %copy-done.14, bf16[1536,1536]{1,0:T(8,128)(2,1)S(1)} %copy-done, f32[6,128,128]{2,1,0:T(8,128)S(1)} %get-tuple-element.152.bias), custom_call_target="tpu_custom_call" | custom-call | flops 550000000 | bytes 1750000 | tf_op jit(solution)/shard_map/window/pallas_call | solution.py:1108
  108.2 1.4 copy-done.19
  113.3 11.6 %all-gather.2.cloned.1.call-done.bulk = bf16[7680,768]{1,0:T(8,128)(2,1)} async-done(((bf16[480,768]{1,0:T(8,128)(2,1)}), bf16[7680,768]{1,0:T(8,128)(2,1)}) %all-gather.2.cloned.1.call-update) | async-done | bytes 11796496 | tf_op jit(solution)/shard_map/all_gather | solution.py:1030
  124.9 12.7 %pooled.3 = (bf16[768,768]{1,0:T(8,128)(2,1)}, bf16[768,768]{1,0:T(8,128)(2,1)}, bf16[6,6,128,256]{3,2,1,0:T(8,128)(2,1)}, bf16[768,768]{1,0:T(8,128)(2,1)}) custom-call(s32[5]{0:T(128)} %broadcast_select_fusion.places, bf16[768,768]{1,0:T(8,128)(2,1)} %copy-done.4, f32[6,128,128]{2,1,0:T(8,128)} %get-tuple-element.151.bias, ...), custom_call_target="tpu_custom_call" | custom-call | flops 770000000 | bytes 2450000 | tf_op jit(solution)/shard_map/pooled/pallas_call | solution.py:1122
  137.6 44.8 %feed.1 = (bf16[768,768]{1,0:T(8,128)(2,1)}, f32[768,768]{1,0:T(8,128)}, bf16[768,768]{1,0:T(8,128)(2,1)}, bf16[7168,768]{1,0:T(8,128)(2,1)}, f32[8,768]{1,0:T(8,128)}) custom-call(bf16[768,768]{1,0:T(8,128)(2,1)} %bitcast.49, bf16[768,768]{1,0:T(8,128)(2,1)} %get-tuple-element.77.mixed, bf16[768,768]{1,0:T(8,128)(2,1)} %bitcast.60, ...), custom_call_target="tpu_custom_call" | custom-call | flops 2475000064 | bytes 7875000 | tf_op jit(solution)/shard_map/feed/pallas_call | solution.py:1140
  182.5 13.7 %pooled_back.1 = (bf16[768,768]{1,0:T(8,128)(2,1)}, bf16[192,1536]{1,0:T(8,128)(2,1)}, bf16[2,192,1536]{2,1,0:T(8,128)(2,1)}, bf16[192,1536]{1,0:T(8,128)(2,1)}, bf16[192,1536]{1,0:T(8,128)(2,1)}) custom-call(s32[5]{0:T(128)} %broadcast_select_fusion.places, bf16[768,768]{1,0:T(8,128)(2,1)} %get-tuple-element.81.grad_mixed, ...), custom_call_target="tpu_custom_call" | custom-call | flops 825000000 | bytes 2625000 | tf_op jit(solution)/shard_map/pooled_back/pallas_call | solution.py:1178
  196.5 1.4 collective-permute-start.15
  197.9 1.5 collective-permute-done.13
  200.8 6.9 %collective-permute-start.14 = (bf16[192,1536]{1,0:T(8,128)(2,1)S(1)}, bf16[192,1536]{1,0:T(8,128)(2,1)S(1)}, u32[]{:S(2)}, u32[]{:S(2)}) collective-permute-start(bf16[192,1536]{1,0:T(8,128)(2,1)S(1)} %fusion.refs_1_), channel_id=1, source_target_pairs={{3,1},{0,2},{5,3},{2,4},{7,5},{4,6},{9,7},{6,8},{11,9},{8,10},{13,... | collective-permute-start | bytes 1769480 | tf_op jit(solution)/shard_map/ppermute | solution.py:1210
  211.0 13.3 %window_back.1 = (bf16[768,768]{1,0:T(8,128)(2,1)S(1)}, bf16[1536,1536]{1,0:T(8,128)(2,1)S(1)}, bf16[768,768]{1,0:T(8,128)(2,1)S(1)}) custom-call(bf16[768,768]{1,0:T(8,128)(2,1)S(1)} %copy-done.17, bf16[768,768]{1,0:T(8,128)(2,1)S(1)} %gate.15.grad_second, bf16[768,768]{1,0:T(8,128)(2,1)S(1)} %copy-done.5, bf16[768,768]{1,0:T(8,128)(2,1)S(1)} %copy-done.15, ...), custom_call_target="tpu_custom_call" | custom-call | flops 1210000000 | bytes 3850000 | tf_op jit(solution)/shard_map/window_back/pallas_call | solution.py:1214
  224.3 3.0 query_grad.1
  227.3 13.3 %collective-permute-done.14.near = bf16[192,1536]{1,0:T(8,128)(2,1)S(1)} collective-permute-done((bf16[192,1536]{1,0:T(8,128)(2,1)S(1)}, bf16[192,1536]{1,0:T(8,128)(2,1)S(1)}, u32[]{:S(2)}, u32[]{:S(2)}) %collective-permute-start.14) | collective-permute-done | bytes 589856 | tf_op jit(solution)/shard_map/ppermute | solution.py:1210
  240.7 7.4 %conv_back.1 = (bf16[1536,1536]{1,0:T(8,128)(2,1)S(1)}, f32[16,768]{1,0:T(8,128)S(1)}, bf16[768,768]{1,0:T(8,128)(2,1)S(1)}) custom-call(s32[17]{0:T(128)S(1)} %copy-done.26, bf16[192,1536]{1,0:T(8,128)(2,1)S(1)} %copy-done.23, bf16[192,1536]{1,0:T(8,128)(2,1)S(1)} %slice_bitcast_fusion.away, bf16[192,1536]{1,0:T(8,128)(2,1)S(1)} %collective-permute-done.14.near, ...), custom_call_target="tpu_custom_call" | custom-call | flops 660000000 | bytes 2100000 | tf_op jit(solution)/shard_map/conv_back/pallas_call | solution.py:1251
  248.1 6.7 %weight_grad.1 = (bf16[2,4,48,3200]{3,2,1,0:T(8,128)(2,1)S(1)}, bf16[2,4,48,3200]{3,2,1,0:T(8,128)(2,1)S(1)}) custom-call(s32[17]{0:T(128)S(1)} %copy-done.26, bf16[768,768]{1,0:T(8,128)(2,1)S(1)} %bitcast.51, bf16[384,768]{1,0:T(8,128)(2,1)S(1)} %bitcast.55, bf16[384,768]{1,0:T(8,128)(2,1)S(1)} %bitcast.58, ...), custom_call_target="tpu_custom_call", output_to_operand_aliasing={{0}: (6, {}), {1}: (7, {})} | custom-call | flops 550000000 | bytes 1750000 | tf_op jit(solution)/shard_map/weight_grad/pallas_call | solution.py:1270
  254.8 4.7 %collective-permute-done.16.arrived = bf16[2,4,48,3200]{3,2,1,0:T(8,128)(2,1)S(1)} collective-permute-done((bf16[2,4,48,3200]{3,2,1,0:T(8,128)(2,1)S(1)}, bf16[2,4,48,3200]{3,2,1,0:T(8,128)(2,1)S(1)}, u32[]{:S(2)}, u32[]{:S(2)}) %collective-permute-start.16) | collective-permute-done | bytes 2457632 | tf_op jit(solution)/shard_map/ppermute | solution.py:954
  261.0 1.4 collective-permute-start.18
  262.5 3.1 collective-permute-start.17
  265.5 2.5 collective-permute-start.19
  268.1 7.0 %token_grad.1.refs_1_ = f32[768,768]{1,0:T(8,128)} custom-call(s32[17]{0:T(128)S(1)} %copy-done.26, f32[768,768]{1,0:T(8,128)S(1)} %copy-done.18, bf16[768,768]{1,0:T(8,128)(2,1)S(1)} %get-tuple-element.89.grad_queries, bf16[1536,1536]{1,0:T(8,128)(2,1)S(1)} %get-tuple-element.95.grad_pairs, bf16[384,768]{1,0:T(8,128)(2,1)S(1)} %collective-permute-done.17.low, ...), custom_call_target="tpu_custom_call" | custom-call | flops 605000000 | bytes 1925000 | tf_op jit(solution)/shard_map/token_grad/pallas_call | solution.py:1294
  275.1 6.2 %collective-permute-done.19.refs_2_.b_arrived = bf16[4,48,128]{2,1,0:T(8,128)(2,1)S(1)} collective-permute-done((bf16[4,48,128]{2,1,0:T(8,128)(2,1)S(1)}, bf16[4,48,128]{2,1,0:T(8,128)(2,1)S(1)}, u32[]{:S(2)}, u32[]{:S(2)}) %collective-permute-start.19) | collective-permute-done | bytes 49184 | tf_op jit(solution)/shard_map/ppermute | solution.py:687
  281.3 1.7 copy-done.8
  283.0 6.0 %collective-permute-done.20.arrived = bf16[2,4,48,1536]{3,2,1,0:T(8,128)(2,1)S(1)} collective-permute-done((bf16[2,4,48,1536]{3,2,1,0:T(8,128)(2,1)S(1)}, bf16[2,4,48,1536]{3,2,1,0:T(8,128)(2,1)S(1)}, u32[]{:S(2)}, u32[]{:S(2)}) %collective-permute-start.20) | collective-permute-done | bytes 1179680 | tf_op jit(solution)/shard_map/ppermute | solution.py:691
  289.3 7.2 %collective-permute-start.21 = (bf16[4,48,1536]{2,1,0:T(8,128)(2,1)S(1)}, bf16[4,48,1536]{2,1,0:T(8,128)(2,1)S(1)}, u32[]{:S(2)}, u32[]{:S(2)}) collective-permute-start(bf16[4,48,1536]{2,1,0:T(8,128)(2,1)S(1)} %get-tuple-element.106), channel_id=1, source_target_pairs={{0,2},{1,3},{2,0},{3,1},{4,6},{5,7},{6,4},{7,5},{8,10},{9,11},{10,... | collective-permute-start | bytes 1769480 | tf_op jit(solution)/shard_map/ppermute | solution.py:687
  296.5 20.0 %collective-permute-done.21.x_arrived = bf16[4,48,1536]{2,1,0:T(8,128)(2,1)S(1)} collective-permute-done((bf16[4,48,1536]{2,1,0:T(8,128)(2,1)S(1)}, bf16[4,48,1536]{2,1,0:T(8,128)(2,1)S(1)}, u32[]{:S(2)}, u32[]{:S(2)}) %collective-permute-start.21) | collective-permute-done | bytes 589856 | tf_op jit(solution)/shard_map/ppermute | solution.py:687
  316.6 1.5 collective-permute-start.22
  318.1 9.8 %collective-permute-done.22.first.refs_1_ = bf16[48,1664]{1,0:T(8,128)(2,1)S(1)} collective-permute-done((bf16[48,1664]{1,0:T(8,128)(2,1)S(1)}, bf16[48,1664]{1,0:T(8,128)(2,1)S(1)}, u32[]{:S(2)}, u32[]{:S(2)}) %collective-permute-start.22) | collective-permute-done | bytes 159776 | tf_op jit(solution)/shard_map/ppermute | solution.py:683
  328.0 1.5 collective-permute-start.26
  329.5 1.9 collective-permute-start.23
  331.4 1.7 collective-permute-start.24
  333.1 6.0 %collective-permute-done.23.second = bf16[48,1664]{1,0:T(8,128)(2,1)S(1)} collective-permute-done((bf16[48,1664]{1,0:T(8,128)(2,1)S(1)}, bf16[48,1664]{1,0:T(8,128)(2,1)S(1)}, u32[]{:S(2)}, u32[]{:S(2)}) %collective-permute-start.23) | collective-permute-done | bytes 159776 | tf_op jit(solution)/shard_map/ppermute | solution.py:683
  339.8 8.7 %collective-permute-done.25.arrived = bf16[48,1664]{1,0:T(8,128)(2,1)S(1)} collective-permute-done((bf16[48,1664]{1,0:T(8,128)(2,1)S(1)}, bf16[48,1664]{1,0:T(8,128)(2,1)S(1)}, u32[]{:S(2)}, u32[]{:S(2)}) %collective-permute-start.25) | collective-permute-done | bytes 159776 | tf_op jit(solution)/shard_map/ppermute | solution.py:691
  348.5 1.4 final.1
  350.6 2.2 bulk_final.1
  (136 shorter events, 26.4 us)
Async XLA Ops:
  7.2 117.7 %all-gather.2.cloned.1.call-start = ((), (), s32[]{:S(2)}) async-start(), calls=%async_computation.1 | async-start | bytes 12533760 | tf_op jit(solution)/shard_map/all_gather | solution.py:1030
  12.1 315.8 %reduce-scatter.2.cloned.1.call-start = ((), (), s32[]{:S(2)}) async-start(), calls=%async_computation.2 | async-start | bytes 11698176 | tf_op jit(solution)/shard_map/reduce_scatter | solution.py:1175
  12.2 9.6 %collective-permute-start.2 = (bf16[48,1280]{1,0:T(8,128)(2,1)}, bf16[48,1280]{1,0:T(8,128)(2,1)S(1)}, u32[]{:S(2)}, u32[]{:S(2)}) collective-permute-start(bf16[48,1280]{1,0:T(8,128)(2,1)} %get-tuple-element.70), channel_id=1, source_target_pairs={{0,4},{1,5},{2,6},{3,7},{4,8},{5,9},{6,10},{7,11},{8,12},{9,13},{1... | collective-permute-start | bytes 368648 | tf_op jit(solution)/shard_map/ppermute | solution.py:683
  15.3 10.9 %collective-permute-start.1 = (bf16[48,1280]{1,0:T(8,128)(2,1)}, bf16[48,1280]{1,0:T(8,128)(2,1)S(1)}, u32[]{:S(2)}, u32[]{:S(2)}) collective-permute-start(bf16[48,1280]{1,0:T(8,128)(2,1)} %get-tuple-element.70), channel_id=1, source_target_pairs={{0,8},{1,9},{2,10},{3,11},{4,12},{5,13},{6,14},{7,15},{8,0},{9,1},... | collective-permute-start | bytes 368648 | tf_op jit(solution)/shard_map/ppermute | solution.py:683
  17.9 8.3 %collective-permute-start = (bf16[48,1280]{1,0:T(8,128)(2,1)}, bf16[48,1280]{1,0:T(8,128)(2,1)S(1)}, u32[]{:S(2)}, u32[]{:S(2)}) collective-permute-start(bf16[48,1280]{1,0:T(8,128)(2,1)} %get-tuple-element.70), channel_id=1, source_target_pairs={{0,12},{1,13},{2,14},{3,15},{4,0},{5,1},{6,2},{7,3},{8,4},{9,5},{1... | collective-permute-start | bytes 368648 | tf_op jit(solution)/shard_map/ppermute | solution.py:683
  27.2 18.7 %copy-start.25 = (bf16[6,64,768]{2,1,0:T(8,128)(2,1)S(1)}, bf16[6,64,768]{2,1,0:T(8,128)(2,1)}, u32[]{:S(2)}) copy-start(bf16[6,64,768]{2,1,0:T(8,128)(2,1)} %get-tuple-element.71.refs_0_) | copy-start | bytes 1769476
  27.2 17.1 %collective-permute-start.3 = (bf16[4,48,1280]{2,1,0:T(8,128)(2,1)S(1)}, bf16[4,48,1280]{2,1,0:T(8,128)(2,1)S(1)}, u32[]{:S(2)}, u32[]{:S(2)}) collective-permute-start(bf16[4,48,1280]{2,1,0:T(8,128)(2,1)S(1)} %pad_maximum_fusion), channel_id=1, source_target_pairs={{0,2},{1,3},{2,0},{3,1},{4,6},{5,7},{6,4},{7,5},{8,10},{9,11},{10,... | collective-permute-start | bytes 1474568 | tf_op jit(solution)/shard_map/ppermute | solution.py:687
  28.8 17.1 %copy-start.24 = (bf16[6,64,768]{2,1,0:T(8,128)(2,1)S(1)}, bf16[6,64,768]{2,1,0:T(8,128)(2,1)}, u32[]{:S(2)}) copy-start(bf16[6,64,768]{2,1,0:T(8,128)(2,1)} %get-tuple-element.69.refs_0_) | copy-start | bytes 1769476
  44.3 23.6 %collective-permute-start.6 = (bf16[8,48,1280]{2,1,0:T(8,128)(2,1)S(1)}, bf16[8,48,1280]{2,1,0:T(8,128)(2,1)S(1)}, u32[]{:S(2)}, u32[]{:S(2)}) collective-permute-start(bf16[8,48,1280]{2,1,0:T(8,128)(2,1)S(1)} %constant_dynamic-update-slice_fusion.refs_0_), channel_id=1, source_target_pairs={{0,16},{16,0},{1,17},{17,1},{2,18},{18,2},{3,19},{19,3},{4,20},{20... | collective-permute-start | bytes 2949128 | tf_op jit(solution)/shard_map/ppermute | solution.py:691
  45.9 4.6 %collective-permute-start.4 = (bf16[6,64,768]{2,1,0:T(8,128)(2,1)S(1)}, bf16[6,64,768]{2,1,0:T(8,128)(2,1)S(1)}, u32[]{:S(2)}, u32[]{:S(2)}) collective-permute-start(bf16[6,64,768]{2,1,0:T(8,128)(2,1)S(1)} %gate.11), channel_id=1, source_target_pairs={{0,1},{1,2},{2,3},{3,4},{4,5},{5,6},{6,7},{7,8},{8,9},{9,10},{10,1... | collective-permute-start | bytes 1769480 | tf_op jit(solution)/shard_map/ppermute | solution.py:948
  47.4 4.5 %collective-permute-start.5 = (bf16[6,64,768]{2,1,0:T(8,128)(2,1)S(1)}, bf16[6,64,768]{2,1,0:T(8,128)(2,1)S(1)}, u32[]{:S(2)}, u32[]{:S(2)}) collective-permute-start(bf16[6,64,768]{2,1,0:T(8,128)(2,1)S(1)} %gate.12), channel_id=1, source_target_pairs={{1,0},{2,1},{3,2},{4,3},{5,4},{6,5},{7,6},{8,7},{9,8},{10,9},{11,1... | collective-permute-start | bytes 1769480 | tf_op jit(solution)/shard_map/ppermute | solution.py:948
  48.7 20.6 %collective-permute-start.7 = (bf16[8,48,1280]{2,1,0:T(8,128)(2,1)S(1)}, bf16[8,48,1280]{2,1,0:T(8,128)(2,1)}, u32[]{:S(2)}, u32[]{:S(2)}) collective-permute-start(bf16[8,48,1280]{2,1,0:T(8,128)(2,1)S(1)} %constant_dynamic-update-slice_fusion.refs_0_), channel_id=1, source_target_pairs={{0,1},{1,0},{2,3},{3,2},{4,5},{5,4},{6,7},{7,6},{8,9},{9,8},{10,11... | collective-permute-start | bytes 2949128 | tf_op jit(solution)/shard_map/ppermute | solution.py:954
  50.5 17.4 %copy-start.9 = (bf16[6,64,768]{2,1,0:T(8,128)(2,1)}, bf16[6,64,768]{2,1,0:T(8,128)(2,1)S(1)}, u32[]{:S(2)}) copy-start(bf16[6,64,768]{2,1,0:T(8,128)(2,1)S(1)} %collective-permute-done.4) | copy-start | bytes 1769476
  51.9 16.1 %copy-start.11 = (bf16[6,64,768]{2,1,0:T(8,128)(2,1)}, bf16[6,64,768]{2,1,0:T(8,128)(2,1)S(1)}, u32[]{:S(2)}) copy-start(bf16[6,64,768]{2,1,0:T(8,128)(2,1)S(1)} %collective-permute-done.5) | copy-start | bytes 1769476
  68.0 2.8 collective-permute-start.8
  84.9 24.8 %collective-permute-start.10 = (bf16[192,1536]{1,0:T(8,128)(2,1)}, bf16[192,1536]{1,0:T(8,128)(2,1)S(1)}, u32[]{:S(2)}, u32[]{:S(2)}) collective-permute-start(bf16[192,1536]{1,0:T(8,128)(2,1)} %get-tuple-element.76.refs_0_), channel_id=1, source_target_pairs={{1,3},{2,0},{3,5},{4,2},{5,7},{6,4},{7,9},{8,6},{9,11},{10,8},{11,... | collective-permute-start | bytes 1769480 | tf_op jit(solution)/shard_map/ppermute | solution.py:960
  87.5 25.7 %collective-permute-start.12 = (bf16[192,1536]{1,0:T(8,128)(2,1)}, bf16[192,1536]{1,0:T(8,128)(2,1)S(1)}, u32[]{:S(2)}, u32[]{:S(2)}) collective-permute-start(bf16[192,1536]{1,0:T(8,128)(2,1)} %get-tuple-element.76.refs_0_), channel_id=1, source_target_pairs={{0,2},{2,4},{3,1},{4,6},{5,3},{6,8},{7,5},{8,10},{9,7},{10,12},{11... | collective-permute-start | bytes 1769480 | tf_op jit(solution)/shard_map/ppermute | solution.py:960
  97.6 15.7 %collective-permute-start.9 = (bf16[192,1536]{1,0:T(8,128)(2,1)}, bf16[192,1536]{1,0:T(8,128)(2,1)S(1)}, u32[]{:S(2)}, u32[]{:S(2)}) collective-permute-start(bf16[192,1536]{1,0:T(8,128)(2,1)} %get-tuple-element.76.refs_0_), channel_id=1, source_target_pairs={{0,1},{1,0},{2,3},{3,2},{4,5},{5,4},{6,7},{7,6},{8,9},{9,8},{10,11... | collective-permute-start | bytes 1769480 | tf_op jit(solution)/shard_map/ppermute | solution.py:954
  110.7 14.3 %copy-start.13 = (bf16[192,1536]{1,0:T(8,128)(2,1)}, bf16[192,1536]{1,0:T(8,128)(2,1)S(1)}, u32[]{:S(2)}) copy-start(bf16[192,1536]{1,0:T(8,128)(2,1)S(1)} %gate.14.refs_3_) | copy-start | bytes 1769476
  110.7 2.6 collective-permute-start.11
  113.2 11.7 %copy-start.27 = (bf16[192,1536]{1,0:T(8,128)(2,1)}, bf16[192,1536]{1,0:T(8,128)(2,1)S(1)}, u32[]{:S(2)}) copy-start(bf16[192,1536]{1,0:T(8,128)(2,1)S(1)} %collective-permute-done.12.refs_4_) | copy-start | bytes 1769476
  113.3 11.7 %copy-start.28 = (bf16[192,1536]{1,0:T(8,128)(2,1)}, bf16[192,1536]{1,0:T(8,128)(2,1)S(1)}, u32[]{:S(2)}) copy-start(bf16[192,1536]{1,0:T(8,128)(2,1)S(1)} %collective-permute-done.9.refs_1_) | copy-start | bytes 1769476
  182.5 25.3 %slice-start = ((s8[4718592]{0:T(1024)(128)(4,1)}), s8[524288]{0:T(1024)(128)(4,1)S(1)}, s32[]{:S(2)}) async-start(s8[4718592]{0:T(1024)(128)(4,1)} %bitcast.46), calls=%async_computation.3 | async-start | bytes 1048576
  182.5 25.3 %slice-start.1 = ((s8[4718592]{0:T(1024)(128)(4,1)}), s8[4194304]{0:T(1024)(128)(4,1)S(1)}, s32[]{:S(2)}) async-start(s8[4718592]{0:T(1024)(128)(4,1)} %bitcast.46), calls=%async_computation.4 | async-start | bytes 8388608
  182.5 25.3 %copy-start.20 = (bf16[6,6,128,256]{3,2,1,0:T(8,128)(2,1)S(1)}, bf16[6,6,128,256]{3,2,1,0:T(8,128)(2,1)}, u32[]{:S(2)}) copy-start(bf16[6,6,128,256]{3,2,1,0:T(8,128)(2,1)} %copy-done.19) | copy-start | bytes 7077892
  196.2 11.5 %copy-start.16 = (bf16[768,768]{1,0:T(8,128)(2,1)S(1)}, bf16[768,768]{1,0:T(8,128)(2,1)}, u32[]{:S(2)}) copy-start(bf16[768,768]{1,0:T(8,128)(2,1)} %get-tuple-element.84.refs_0_) | copy-start | bytes 3538948
  196.2 3.3 collective-permute-start.13
  196.5 30.8 %collective-permute-start.15 = (bf16[192,1536]{1,0:T(8,128)(2,1)}, bf16[192,1536]{1,0:T(8,128)(2,1)S(1)}, u32[]{:S(2)}, u32[]{:S(2)}) collective-permute-start(bf16[192,1536]{1,0:T(8,128)(2,1)} %get-tuple-element.91), channel_id=1, source_target_pairs={{2,0},{4,2},{1,3},{6,4},{3,5},{8,6},{5,7},{10,8},{7,9},{12,10},{9,... | collective-permute-start | bytes 1769480 | tf_op jit(solution)/shard_map/ppermute | solution.py:1211
  199.5 8.3 %copy-start.17 = (bf16[768,768]{1,0:T(8,128)(2,1)S(1)}, bf16[768,768]{1,0:T(8,128)(2,1)}, u32[]{:S(2)}) copy-start(bf16[768,768]{1,0:T(8,128)(2,1)} %get-tuple-element.81.grad_mixed) | copy-start | bytes 3538948
  200.8 39.9 %collective-permute-start.14 = (bf16[192,1536]{1,0:T(8,128)(2,1)S(1)}, bf16[192,1536]{1,0:T(8,128)(2,1)S(1)}, u32[]{:S(2)}, u32[]{:S(2)}) collective-permute-start(bf16[192,1536]{1,0:T(8,128)(2,1)S(1)} %fusion.refs_1_), channel_id=1, source_target_pairs={{3,1},{0,2},{5,3},{2,4},{7,5},{4,6},{9,7},{6,8},{11,9},{8,10},{13,... | collective-permute-start | bytes 1769480 | tf_op jit(solution)/shard_map/ppermute | solution.py:1210
  210.9 13.3 %copy-start.1 = (bf16[6,128,768]{2,1,0:T(8,128)(2,1)S(1)}, bf16[6,128,768]{2,1,0:T(8,128)(2,1)}, u32[]{:S(2)}) copy-start(bf16[6,128,768]{2,1,0:T(8,128)(2,1)} %tokens.1) | copy-start | bytes 3538948
  210.9 13.3 %copy-start.26 = (s32[17]{0:T(128)S(1)}, s32[17]{0:T(128)}, u32[]{:S(2)}) copy-start(s32[17]{0:T(128)} %pad_add_fusion.order) | copy-start | bytes 208
  227.2 13.4 %copy-start.7 = (bf16[8,48,1280]{2,1,0:T(8,128)(2,1)S(1)}, bf16[8,48,1280]{2,1,0:T(8,128)(2,1)}, u32[]{:S(2)}) copy-start(bf16[8,48,1280]{2,1,0:T(8,128)(2,1)} %copy-done.6) | copy-start | bytes 2949124
  227.3 13.4 %copy-start.23 = (bf16[192,1536]{1,0:T(8,128)(2,1)S(1)}, bf16[192,1536]{1,0:T(8,128)(2,1)}, u32[]{:S(2)}) copy-start(bf16[192,1536]{1,0:T(8,128)(2,1)} %get-tuple-element.90.own) | copy-start | bytes 1769476
  227.3 13.4 %copy-start.3 = (bf16[8,48,1280]{2,1,0:T(8,128)(2,1)S(1)}, bf16[8,48,1280]{2,1,0:T(8,128)(2,1)}, u32[]{:S(2)}) copy-start(bf16[8,48,1280]{2,1,0:T(8,128)(2,1)} %copy-done.2) | copy-start | bytes 2949124
  240.7 7.4 %copy-start.10 = (bf16[6,64,768]{2,1,0:T(8,128)(2,1)S(1)}, bf16[6,64,768]{2,1,0:T(8,128)(2,1)}, u32[]{:S(2)}) copy-start(bf16[6,64,768]{2,1,0:T(8,128)(2,1)} %copy-done.9) | copy-start | bytes 1769476
  240.7 7.4 %copy-start.12 = (bf16[6,64,768]{2,1,0:T(8,128)(2,1)S(1)}, bf16[6,64,768]{2,1,0:T(8,128)(2,1)}, u32[]{:S(2)}) copy-start(bf16[6,64,768]{2,1,0:T(8,128)(2,1)} %copy-done.11) | copy-start | bytes 1769476
  254.7 4.7 %collective-permute-start.16 = (bf16[2,4,48,3200]{3,2,1,0:T(8,128)(2,1)S(1)}, bf16[2,4,48,3200]{3,2,1,0:T(8,128)(2,1)S(1)}, u32[]{:S(2)}, u32[]{:S(2)}) collective-permute-start(bf16[2,4,48,3200]{3,2,1,0:T(8,128)(2,1)S(1)} %get-tuple-element.100), channel_id=1, source_target_pairs={{0,1},{1,0},{2,3},{3,2},{4,5},{5,4},{6,7},{7,6},{8,9},{9,8},{10,11... | collective-permute-start | bytes 7372808 | tf_op jit(solution)/shard_map/ppermute | solution.py:954
  260.8 28.1 %collective-permute-start.20 = (bf16[2,4,48,1536]{3,2,1,0:T(8,128)(2,1)S(1)}, bf16[2,4,48,1536]{3,2,1,0:T(8,128)(2,1)S(1)}, u32[]{:S(2)}, u32[]{:S(2)}) collective-permute-start(bf16[2,4,48,1536]{3,2,1,0:T(8,128)(2,1)S(1)} %get-tuple-element.104), channel_id=1, source_target_pairs={{0,16},{16,0},{1,17},{17,1},{2,18},{18,2},{3,19},{19,3},{4,20},{20... | collective-permute-start | bytes 3538952 | tf_op jit(solution)/shard_map/ppermute | solution.py:691
  261.0 7.0 %collective-permute-start.18 = (bf16[384,768]{1,0:T(8,128)(2,1)S(1)}, bf16[384,768]{1,0:T(8,128)(2,1)S(1)}, u32[]{:S(2)}, u32[]{:S(2)}) collective-permute-start(bf16[384,768]{1,0:T(8,128)(2,1)S(1)} %get-tuple-element.138), channel_id=1, source_target_pairs={{1,0},{2,1},{3,2},{4,3},{5,4},{6,5},{7,6},{8,7},{9,8},{10,9},{11,1... | collective-permute-start | bytes 1769480 | tf_op jit(solution)/shard_map/ppermute | solution.py:948
  262.5 5.6 %collective-permute-start.17 = (bf16[384,768]{1,0:T(8,128)(2,1)S(1)}, bf16[384,768]{1,0:T(8,128)(2,1)S(1)}, u32[]{:S(2)}, u32[]{:S(2)}) collective-permute-start(bf16[384,768]{1,0:T(8,128)(2,1)S(1)} %get-tuple-element.139), channel_id=1, source_target_pairs={{0,1},{1,2},{2,3},{3,4},{4,5},{5,6},{6,7},{7,8},{8,9},{9,10},{10,1... | collective-permute-start | bytes 1769480 | tf_op jit(solution)/shard_map/ppermute | solution.py:948
  265.5 15.7 %collective-permute-start.19 = (bf16[4,48,128]{2,1,0:T(8,128)(2,1)S(1)}, bf16[4,48,128]{2,1,0:T(8,128)(2,1)S(1)}, u32[]{:S(2)}, u32[]{:S(2)}) collective-permute-start(bf16[4,48,128]{2,1,0:T(8,128)(2,1)S(1)} %get-tuple-element.103), channel_id=1, source_target_pairs={{0,2},{1,3},{2,0},{3,1},{4,6},{5,7},{6,4},{7,5},{8,10},{9,11},{10,... | collective-permute-start | bytes 147464 | tf_op jit(solution)/shard_map/ppermute | solution.py:687
  289.3 27.2 %collective-permute-start.21 = (bf16[4,48,1536]{2,1,0:T(8,128)(2,1)S(1)}, bf16[4,48,1536]{2,1,0:T(8,128)(2,1)S(1)}, u32[]{:S(2)}, u32[]{:S(2)}) collective-permute-start(bf16[4,48,1536]{2,1,0:T(8,128)(2,1)S(1)} %get-tuple-element.106), channel_id=1, source_target_pairs={{0,2},{1,3},{2,0},{3,1},{4,6},{5,7},{6,4},{7,5},{8,10},{9,11},{10,... | collective-permute-start | bytes 1769480 | tf_op jit(solution)/shard_map/ppermute | solution.py:687
  316.6 11.3 %collective-permute-start.22 = (bf16[48,1664]{1,0:T(8,128)(2,1)S(1)}, bf16[48,1664]{1,0:T(8,128)(2,1)S(1)}, u32[]{:S(2)}, u32[]{:S(2)}) collective-permute-start(bf16[48,1664]{1,0:T(8,128)(2,1)S(1)} %get-tuple-element.108), channel_id=1, source_target_pairs={{0,4},{1,5},{2,6},{3,7},{4,8},{5,9},{6,10},{7,11},{8,12},{9,13},{1... | collective-permute-start | bytes 479240 | tf_op jit(solution)/shard_map/ppermute | solution.py:683
  328.0 22.7 %collective-permute-start.26 = (bf16[448,768]{1,0:T(8,128)(2,1)}, bf16[448,768]{1,0:T(8,128)(2,1)S(1)}, u32[]{:S(2)}, u32[]{:S(2)}) collective-permute-start(bf16[448,768]{1,0:T(8,128)(2,1)} %gate.19.own), channel_id=1, source_target_pairs={{0,16},{16,0},{1,17},{17,1},{2,18},{18,2},{3,19},{19,3},{4,20},{20... | collective-permute-start | bytes 2064392 | tf_op jit(solution)/shard_map/ppermute | solution.py:691
  329.5 9.6 %collective-permute-start.23 = (bf16[48,1664]{1,0:T(8,128)(2,1)S(1)}, bf16[48,1664]{1,0:T(8,128)(2,1)S(1)}, u32[]{:S(2)}, u32[]{:S(2)}) collective-permute-start(bf16[48,1664]{1,0:T(8,128)(2,1)S(1)} %get-tuple-element.109), channel_id=1, source_target_pairs={{0,8},{1,9},{2,10},{3,11},{4,12},{5,13},{6,14},{7,15},{8,0},{9,1},... | collective-permute-start | bytes 479240 | tf_op jit(solution)/shard_map/ppermute | solution.py:683
  331.4 7.7 %collective-permute-start.24 = (bf16[48,1664]{1,0:T(8,128)(2,1)S(1)}, bf16[48,1664]{1,0:T(8,128)(2,1)S(1)}, u32[]{:S(2)}, u32[]{:S(2)}) collective-permute-start(bf16[48,1664]{1,0:T(8,128)(2,1)S(1)} %get-tuple-element.110), channel_id=1, source_target_pairs={{0,12},{1,13},{2,14},{3,15},{4,0},{5,1},{6,2},{7,3},{8,4},{9,5},{1... | collective-permute-start | bytes 479240 | tf_op jit(solution)/shard_map/ppermute | solution.py:683
  339.2 9.3 %collective-permute-start.25 = (bf16[48,1664]{1,0:T(8,128)(2,1)S(1)}, bf16[48,1664]{1,0:T(8,128)(2,1)S(1)}, u32[]{:S(2)}, u32[]{:S(2)}) collective-permute-start(bf16[48,1664]{1,0:T(8,128)(2,1)S(1)} %gather_sum.1.own), channel_id=1, source_target_pairs={{0,16},{16,0},{1,17},{17,1},{2,18},{18,2},{3,19},{19,3},{4,20},{20... | collective-permute-start | bytes 479240 | tf_op jit(solution)/shard_map/ppermute | solution.py:691
  (15 other events, 33.5 us)
Sparse Core Ops, SparseCore 0:
  12.3 112.6 all-gather.1
  182.6 142.2 reduce-scatter.1
